TPU v7x, 32 devices: a whole 2x2x4 slice. The times are simulated.
32 devices in a mesh: dp: 4 (over y, x), expert: 8 (over z, core).
Axes of the slice: x: 2, y: 2, z: 4, core: 2. Of those that a mesh axis runs over, the one named last changes fastest.
Arguments:
- tokens: bfloat16 [4096, 768], P(('dp', 'expert')), may hold values from -6 to 6
- w_query: bfloat16 [768, 768], P('dp'), may hold values from -0.109375 to 0.109375
- w_key: bfloat16 [768, 768], P('dp'), may hold values from -0.109375 to 0.109375
- w_value: bfloat16 [768, 768], P('dp'), may hold values from -0.21875 to 0.21875
- w_attn_out: bfloat16 [768, 768], P('dp'), may hold values from -0.875 to 0.875
- w_router: bfloat16 [768, 8], P('dp'), may hold values from -0.109375 to 0.109375
- norm1_gain: bfloat16 [768], P('dp'), may hold values from 0.5 to 1.5
- norm2_gain: bfloat16 [768], P('dp'), may hold values from 0.5 to 1.5
- bias_table: bfloat16 [32, 12], P('dp'), may hold values from -4 to 4
- w_expert_in: bfloat16 [8, 768, 3072], P('expert', None, 'dp'), may hold values from -0.21875 to 0.21875
- w_expert_out: bfloat16 [8, 3072, 768], P('expert', 'dp'), may hold values from -1.25 to 1.25
- routes: int32 [4096, 1], P(('dp', 'expert')), may hold values from 0 to 7; in each aligned block of 128 rows (0 to 127, 128 to 255, ...) at most 20 rows name the same one
- segments: int32 [4096], P(('dp', 'expert')), may hold values from 0 to 31, as said below
- cotangent: bfloat16 [4096, 768], P(('dp', 'expert')), may hold values from -6 to 6
Outputs:
- layer_out: bfloat16 [4096, 768], P(('dp', 'expert'))
- d_tokens: float32 [4096, 768], P(('dp', 'expert'))
- grad_query: float32 [768, 768], P('dp')
- grad_key: float32 [768, 768], P('dp')
- grad_value: float32 [768, 768], P('dp')
- grad_attn_out: float32 [768, 768], P('dp')
- grad_router: float32 [768, 8], P('dp')
- grad_norm1_gain: float32 [768], P('dp')
- grad_norm2_gain: float32 [768], P('dp')
- grad_bias_table: float32 [32, 12], P('dp')
- grad_expert_in: float32 [8, 768, 3072], P('expert', None, 'dp')
- grad_expert_out: float32 [8, 3072, 768], P('expert', 'dp')
Inputs may be any that keep to these rules, and one draw needn't show every extreme that they name: `routes`: within the 128 rows of one device no expert is named more than 20 times, and in every draw some expert of some device is named exactly 20 times. `segments`: within one device the values never fall along the rows and the first row holds 0; the largest value is reached on some device in every draw.
All inputs are finite; a program needn't handle non-finite values.
Results may differ from a plain program's by a relative error of at most 0.022.
Values may be sent and summed in bfloat16 or wider, within the bound.
No kernel may reach another device: no remote copies, remote signals or barrier semaphores. Data moves between devices by JAX's collectives and lax.ppermute only.
A program may use at most 128 MiB of HBM per device.

v0:
```python
from functools import partial

import jax
import jax.numpy as jnp
from jax import lax
from jax.sharding import PartitionSpec as P

eps = 1e-06
bucket_edges = (12, 16, 23, 32, 46, 64, 91)


def in_blocks(shard, dim, length):
    before, after = (shard.shape[:dim], shard.shape[dim + 1 :])
    return jnp.moveaxis(shard.reshape(*before, length, -1, *after), dim, 0)


def sent_and_summed(shard, axis, dim):
    blocks = in_blocks(shard, dim, lax.axis_size(axis))
    arrived = lax.all_to_all(blocks, axis, split_axis=0, concat_axis=0, tiled=True)
    return arrived.astype(jnp.float32).sum(axis=0)


def bucket_ids(offsets):
    distance = -offsets
    upper_half = jnp.where(distance < 0, 16, 0).astype(jnp.int32)
    magnitude = jnp.abs(distance)
    far_bucket = jnp.full_like(magnitude, 8)
    for threshold in bucket_edges:
        far_bucket = far_bucket + (magnitude >= threshold).astype(jnp.int32)
    return upper_half + jnp.where(magnitude < 8, magnitude, far_bucket)


def relative_bias(table, length):
    offsets = jnp.arange(2 * length - 1, dtype=jnp.int32) - (length - 1)
    chosen = bucket_ids(offsets)
    onehot_rows = (chosen[:, None] == jnp.arange(table.shape[0], dtype=jnp.int32)[None, :]).astype(
        jnp.float32
    )
    per_offset = jnp.dot(
        onehot_rows, table, precision=lax.Precision.HIGHEST, preferred_element_type=jnp.float32
    )
    places = jnp.arange(length, dtype=jnp.int32)
    lookup = places[None, :] - places[:, None] + (length - 1)
    return jnp.transpose(per_offset[lookup], (2, 0, 1))


def matmul(left, right):
    return jnp.dot(left, right, preferred_element_type=jnp.float32)


def times_transposed(left, right):
    return lax.dot_general(
        left, right, (((1,), (1,)), ((), ())), preferred_element_type=jnp.float32
    )


def transposed_times(left, right):
    return lax.dot_general(
        left, right, (((0,), (0,)), ((), ())), preferred_element_type=jnp.float32
    )


def rms_scale(values):
    return lax.rsqrt(jnp.mean(values * values, axis=-1, keepdims=True) + eps)


def norm_back(d_normed, normed, scale):
    return scale * (d_normed - normed * jnp.mean(d_normed * normed, axis=-1, keepdims=True))


def on_device(
    tokens,
    w_query,
    w_key,
    w_value,
    w_attn_out,
    w_router,
    norm1_gain,
    norm2_gain,
    bias_table,
    w_expert_in,
    w_expert_out,
    routes,
    segments,
    cotangent,
):
    wq, wk, wv, wo, wr, gain1, gain2, table = (
        lax.all_gather(w_query, "dp", axis=0, tiled=True),
        lax.all_gather(w_key, "dp", axis=0, tiled=True),
        lax.all_gather(w_value, "dp", axis=0, tiled=True),
        lax.all_gather(w_attn_out, "dp", axis=0, tiled=True),
        lax.all_gather(w_router, "dp", axis=0, tiled=True),
        lax.all_gather(norm1_gain, "dp", axis=0, tiled=True),
        lax.all_gather(norm2_gain, "dp", axis=0, tiled=True),
        lax.all_gather(bias_table, "dp", axis=0, tiled=True),
    )
    tok_rows = tokens.shape[0]
    model_width = tokens.shape[1]
    head_count = table.shape[1]
    head_size = model_width // head_count
    expert_count = wr.shape[1]
    capacity = 5 * tok_rows // (4 * expert_count)
    gain1_f = gain1.astype(jnp.float32)
    gain2_f = gain2.astype(jnp.float32)
    token_f = tokens.astype(jnp.float32)
    scale1 = rms_scale(token_f)
    normed1 = token_f * scale1
    h_one = (normed1 * gain1_f).astype(jnp.bfloat16)
    query_rows = matmul(h_one, wq).astype(jnp.bfloat16).reshape(tok_rows, head_count, head_size)
    key_rows = matmul(h_one, wk).astype(jnp.bfloat16).reshape(tok_rows, head_count, head_size)
    value_rows = matmul(h_one, wv).astype(jnp.bfloat16).reshape(tok_rows, head_count, head_size)
    bias, bias_back = jax.vjp(partial(relative_bias, length=tok_rows), table.astype(jnp.float32))
    same_doc = segments[:, None] == segments[None, :]
    scores = (
        jnp.einsum("thd,shd->hts", query_rows, key_rows, preferred_element_type=jnp.float32) + bias
    )
    scores = jnp.where(same_doc[None], scores, -1000000000.0)
    probs = jax.nn.softmax(scores, axis=-1)
    attn_weights = probs.astype(jnp.bfloat16)
    context = jnp.einsum(
        "hts,shd->thd", attn_weights, value_rows, preferred_element_type=jnp.float32
    )
    context = context.astype(jnp.bfloat16).reshape(tok_rows, model_width)
    mixed1 = token_f + matmul(context, wo)
    scale2 = rms_scale(mixed1)
    normed2 = mixed1 * scale2
    h_two = (normed2 * gain2_f).astype(jnp.bfloat16)
    logits = matmul(h_two, wr)
    router_probs = jax.nn.softmax(logits, axis=-1)
    route_ids = routes[:, 0]
    onehot = route_ids[:, None] == jnp.arange(expert_count, dtype=jnp.int32)[None, :]
    hot_f = onehot.astype(jnp.float32)
    gate = jnp.sum(router_probs * hot_f, axis=1)
    ranks = jnp.cumsum(onehot.astype(jnp.int32), axis=0) - 1
    slot = jnp.sum(jnp.where(onehot, ranks, 0), axis=1)
    position = route_ids * capacity + slot
    placer = (
        jnp.arange(expert_count * capacity, dtype=jnp.int32)[:, None] == position[None, :]
    ).astype(jnp.bfloat16)
    send_rows = (
        matmul(placer, h_two).astype(jnp.bfloat16).reshape(expert_count, capacity, model_width)
    )
    arrived = lax.all_to_all(send_rows, "expert", split_axis=0, concat_axis=0, tiled=True)
    gelu_fn = partial(jax.nn.gelu, approximate=True)
    weight_in = w_expert_in[0]
    weight_out = w_expert_out[0]
    expert_rows = lax.all_gather(arrived, "dp", axis=0, tiled=True).reshape(-1, model_width)
    pre_act = matmul(expert_rows, weight_in)
    hidden_f, gelu_back = jax.vjp(gelu_fn, pre_act)
    hidden = hidden_f.astype(jnp.bfloat16)
    partial_out = matmul(hidden, weight_out).reshape(-1, capacity, model_width)
    produced = lax.psum_scatter(
        partial_out.astype(jnp.bfloat16), "dp", scatter_dimension=0, tiled=True
    )
    returned = lax.all_to_all(produced, "expert", split_axis=0, concat_axis=0, tiled=True).reshape(
        -1, model_width
    )
    expert_out = transposed_times(placer, returned)
    layer_out = (mixed1 + gate[:, None] * expert_out).astype(jnp.bfloat16)
    grad_f = cotangent.astype(jnp.float32)
    d_gate = jnp.sum(grad_f * expert_out, axis=1)
    d_result = (grad_f * gate[:, None]).astype(jnp.bfloat16)
    d_send = (
        matmul(placer, d_result).astype(jnp.bfloat16).reshape(expert_count, capacity, model_width)
    )
    d_arrived = lax.all_to_all(d_send, "expert", split_axis=0, concat_axis=0, tiled=True)
    d_rows_in = lax.all_gather(d_arrived, "dp", axis=0, tiled=True).reshape(-1, model_width)
    d_hidden = times_transposed(d_rows_in, weight_out)
    d_pre = gelu_back(d_hidden)[0].astype(jnp.bfloat16)
    grad_expert_out = transposed_times(hidden, d_rows_in)[None]
    grad_expert_in = transposed_times(expert_rows, d_pre)[None]
    partial_grads = times_transposed(d_pre, weight_in).reshape(-1, capacity, model_width)
    d_expert_rows = lax.psum_scatter(
        partial_grads.astype(jnp.bfloat16), "dp", scatter_dimension=0, tiled=True
    )
    d_back = lax.all_to_all(
        d_expert_rows, "expert", split_axis=0, concat_axis=0, tiled=True
    ).reshape(-1, model_width)
    d_h_expert = transposed_times(placer, d_back)
    d_logits = (router_probs * (hot_f - gate[:, None]) * d_gate[:, None]).astype(jnp.bfloat16)
    g_router = transposed_times(h_two, d_logits)
    d_h_two = times_transposed(d_logits, wr) + d_h_expert
    g_gain2 = jnp.sum(d_h_two * normed2, axis=0)
    d_mixed1 = grad_f + norm_back(d_h_two * gain2_f, normed2, scale2)
    d_attn = d_mixed1.astype(jnp.bfloat16)
    g_attn_out = transposed_times(context, d_attn)
    d_context = (
        times_transposed(d_attn, wo).astype(jnp.bfloat16).reshape(tok_rows, head_count, head_size)
    )
    d_weights = jnp.einsum(
        "thd,shd->hts", d_context, value_rows, preferred_element_type=jnp.float32
    )
    d_values = jnp.einsum(
        "hts,thd->shd", attn_weights, d_context, preferred_element_type=jnp.float32
    ).astype(jnp.bfloat16)
    d_scores = (probs * (d_weights - jnp.sum(probs * d_weights, axis=-1, keepdims=True))).astype(
        jnp.bfloat16
    )
    d_queries = jnp.einsum(
        "hts,shd->thd", d_scores, key_rows, preferred_element_type=jnp.float32
    ).astype(jnp.bfloat16)
    d_keys = jnp.einsum(
        "hts,thd->shd", d_scores, query_rows, preferred_element_type=jnp.float32
    ).astype(jnp.bfloat16)
    g_table = bias_back(d_scores.astype(jnp.float32))[0]
    d_queries = d_queries.reshape(tok_rows, model_width)
    d_keys = d_keys.reshape(tok_rows, model_width)
    d_values = d_values.reshape(tok_rows, model_width)
    g_query = transposed_times(h_one, d_queries)
    g_key = transposed_times(h_one, d_keys)
    g_value = transposed_times(h_one, d_values)
    d_h_one = (
        times_transposed(d_queries, wq)
        + times_transposed(d_keys, wk)
        + times_transposed(d_values, wv)
    )
    g_gain1 = jnp.sum(d_h_one * normed1, axis=0)
    d_tokens = d_mixed1 + norm_back(d_h_one * gain1_f, normed1, scale1)
    shares = (
        lax.psum_scatter(
            g_query.astype(jnp.bfloat16), "dp", scatter_dimension=0, tiled=True
        ).astype(jnp.float32),
        lax.psum_scatter(g_key.astype(jnp.bfloat16), "dp", scatter_dimension=0, tiled=True).astype(
            jnp.float32
        ),
        lax.psum_scatter(
            g_value.astype(jnp.bfloat16), "dp", scatter_dimension=0, tiled=True
        ).astype(jnp.float32),
        lax.psum_scatter(
            g_attn_out.astype(jnp.bfloat16), "dp", scatter_dimension=0, tiled=True
        ).astype(jnp.float32),
        lax.psum_scatter(
            g_router.astype(jnp.bfloat16), "dp", scatter_dimension=0, tiled=True
        ).astype(jnp.float32),
        lax.psum_scatter(
            g_gain1.astype(jnp.bfloat16), "dp", scatter_dimension=0, tiled=True
        ).astype(jnp.float32),
        lax.psum_scatter(
            g_gain2.astype(jnp.bfloat16), "dp", scatter_dimension=0, tiled=True
        ).astype(jnp.float32),
        lax.psum_scatter(
            g_table.astype(jnp.bfloat16), "dp", scatter_dimension=0, tiled=True
        ).astype(jnp.float32),
    )
    flat_parts = [item.reshape(-1) for item in shares]
    lengths = [item.shape[0] for item in flat_parts]
    joined = jnp.concatenate(flat_parts)
    group = lax.axis_size("expert")
    padding = -joined.shape[0] % group
    joined = jnp.pad(joined, (0, padding))
    summed_share = sent_and_summed(joined.astype(jnp.bfloat16), "expert", 0)
    whole = lax.all_gather(summed_share.astype(jnp.bfloat16), "expert", axis=0, tiled=True).astype(
        summed_share.dtype
    )
    totals = []
    offset = 0
    for item, count in zip(shares, lengths):
        totals.append(whole[offset : offset + count].reshape(item.shape))
        offset = offset + count
    return (
        layer_out,
        d_tokens,
        totals[0],
        totals[1],
        totals[2],
        totals[3],
        totals[4],
        totals[5],
        totals[6],
        totals[7],
        grad_expert_in,
        grad_expert_out,
    )


def solution(mesh):
    return jax.shard_map(
        on_device,
        mesh=mesh,
        in_specs=(
            P(("dp", "expert"), None),
            P("dp", None),
            P("dp", None),
            P("dp", None),
            P("dp", None),
            P("dp", None),
            P("dp"),
            P("dp"),
            P("dp", None),
            P("expert", None, "dp"),
            P("expert", "dp", None),
            P(("dp", "expert"), None),
            P(("dp", "expert")),
            P(("dp", "expert"), None),
        ),
        out_specs=(
            P(("dp", "expert"), None),
            P(("dp", "expert"), None),
            P("dp", None),
            P("dp", None),
            P("dp", None),
            P("dp", None),
            P("dp", None),
            P("dp"),
            P("dp"),
            P("dp", None),
            P("expert", None, "dp"),
            P("expert", "dp", None),
        ),
        check_vma=False,
    )
```

profile of v0, /device:TPU:0, one launch (start us, length us, event | category | flops | bytes accessed | tf_op | source)
XLA Modules:
  0.0 603.2 jit_solution(17981154554330774607)
XLA Ops:
  10.2 9.5 %all_gather.37 = bf16[32,12]{1,0:T(8,128)(2,1)S(1)} all-gather(bf16[8,12]{1,0:T(8,128)(2,1)S(1)} %copy-done.49), channel_id=1, replica_groups=mesh['dp'=4,'expert'=8] {'dp'}, dimensions={0}, use_global_device_ids=true | all-gather | bytes 960 | tf_op jit(solution)/shard_map/all_gather | solution.py:95
  22.6 8.9 %all-reduce.9 = (bf16[768]{0:T(1024)(128)(2,1)S(1)}, bf16[768]{0:T(1024)(128)(2,1)S(1)}) all-reduce(bf16[768]{0:T(1024)(128)(2,1)S(1)} %dynamic-update-slice, bf16[768]{0:T(1024)(128)(2,1)S(1)} %dynamic-update-slice.1), channel_id=1, replica_groups=mesh['dp'=4,'expert'=8] {'dp'}, use_global_device_ids=true, to_apply=%add | all-reduce | flops 1536 | bytes 6144
  31.5 54.4 %gather_fusion = f32[16384,12]{1,0:T(8,128)} fusion(f32[255,12]{1,0:T(8,128)S(1)} %fusion.44, s32[16384]{0:T(1024)S(1)} %broadcast_clamp_fusion), kind=kCustom, calls=%fused_computation | custom fusion | bytes 1638400 | tf_op jit(solution)/shard_map/jvp()/gather | solution.py:44
  86.0 6.9 %copy.93 = f32[128,128,12]{0,1,2:T(8,128)S(1)} copy(f32[128,128,12]{2,1,0:T(8,128)} %bitcast.126) | data formatting | bytes 1572864 | tf_op jit(solution)/shard_map/jvp()/gather | solution.py:44
  92.9 8.0 %all-gather = bf16[4,192,8]{1,2,0:T(8,128)(2,1)S(1)} all-gather(bf16[1,192,8]{1,2,0:T(8,128)(2,1)S(1)} %bitcast.152), channel_id=1, replica_groups=mesh['dp'=4,'expert'=8] {'dp'}, dimensions={0}, use_global_device_ids=true | all-gather | bytes 15360 | tf_op jit(solution)/shard_map/all_gather | solution.py:92
  101.7 1.6 convolution_convert_fusion.15
  106.0 1.7 convolution_convert_fusion.13
  109.8 19.4 %all-gather.12.cloned.1.call-done = bf16[768,768]{1,0:T(8,128)(2,1)} async-done(((bf16[192,768]{1,0:T(8,128)(2,1)}), bf16[768,768]{1,0:T(8,128)(2,1)}) %all-gather.12.cloned.1.call-update) | async-done | bytes 1179664 | tf_op jit(solution)/shard_map/all_gather | solution.py:91
  129.2 1.7 multiply_reduce_fusion.3
  132.4 1.7 reshape.271
  134.1 4.6 all-to-all-start
  141.5 1.9 convolution_convert_fusion.6
  143.4 1.7 reshape.274
  145.1 4.2 all-to-all-done
  149.3 4.1 all-to-all-start.2
  154.4 16.7 %all_gather.41 = bf16[32,20,768]{2,0,1:T(8,128)(2,1)S(1)} all-gather(bf16[8,20,768]{2,0,1:T(8,128)(2,1)S(1)} %copy.98), channel_id=1, replica_groups=mesh['dp'=4,'expert'=8] {'dp'}, dimensions={0}, use_global_device_ids=true | all-gather | bytes 1228800 | tf_op jit(solution)/shard_map/all_gather | solution.py:147
  172.7 2.1 reshape.272
  174.8 3.9 multiply_convert_fusion
  178.8 2.1 dot_general.117
  181.9 13.2 %all_gather.42 = bf16[32,20,768]{2,0,1:T(8,128)(2,1)S(1)} all-gather(bf16[8,20,768]{2,0,1:T(8,128)(2,1)S(1)} %copy.102), channel_id=1, replica_groups=mesh['dp'=4,'expert'=8] {'dp'}, dimensions={0}, use_global_device_ids=true | all-gather | bytes 1228800 | tf_op jit(solution)/shard_map/all_gather | solution.py:167
  196.6 2.1 reshape.275
  198.8 3.7 convolution_convert_fusion.5
  202.5 2.8 fusion.6
  205.3 2.1 dot_general.123
  207.4 3.2 convolution_convert_fusion.4
  211.3 67.3 %all-reduce.16.cloned.1.call-done = (bf16[32,20,768]{2,0,1:T(8,128)(2,1)}, bf16[32,20,768]{2,0,1:T(8,128)(2,1)}) async-done(((bf16[32,20,768]{2,0,1:T(8,128)(2,1)}, bf16[32,20,768]{2,0,1:T(8,128)(2,1)}), (bf16[32,20,768]{2,0,1:T(8,128)(2,1)}, bf16[32,20,768]{2,0,1:T(8,128)(2,1)})) %all-reduce.16.cloned.1.call-update) | async-done | bytes 1966096
  280.3 4.6 all-to-all-start.1
  286.8 8.6 %all-to-all-done.1 = bf16[8,20,768]{2,1,0:T(8,128)(2,1)S(1)} async-done(((bf16[8,20,768]{2,1,0:T(8,128)(2,1)}), bf16[8,20,768]{2,1,0:T(8,128)(2,1)S(1)}, u32[]{:S(2)}, u32[]{:S(2)}) %all-to-all-start.1) | async-done | bytes 245792 | tf_op jit(solution)/shard_map/all_to_all | solution.py:155
  295.4 4.1 all-to-all-start.3
  302.6 7.3 %all-to-all-done.3 = bf16[8,20,768]{2,1,0:T(8,128)(2,1)} async-done(((bf16[8,20,768]{2,1,0:T(8,128)(2,1)}), bf16[8,20,768]{2,1,0:T(8,128)(2,1)}, u32[]{:S(2)}, u32[]{:S(2)}) %all-to-all-start.3) | async-done | bytes 245792 | tf_op jit(solution)/shard_map/all_to_all | solution.py:176
  309.9 1.7 reshape.276
  311.6 1.9 multiply_reduce_fusion.1
  322.6 1.7 convolution_convert_fusion.1
  328.5 7.7 %copy.124 = f32[128,128,12]{2,1,0:T(8,128)} copy(f32[128,128,12]{0,1,2:T(8,128)S(1)} %fusion.39) | data formatting | bytes 1572864 | tf_op jit(solution)/shard_map/convert_element_type | solution.py:205
  336.2 87.6 %scatter_custom_fusion = f32[255,12]{1,0:T(8,128)S(1)} fusion(s32[16384]{0:T(1024)} %fusion.48, f32[16384,12]{1,0:T(8,128)} %bitcast.127, f32[]{:T(128)} %constant.26.clone.1), kind=kCustom, calls=%fused_computation.94 | custom fusion | flops 196608 | bytes 12752 | tf_op jit(solution)/shard_map/transpose(jvp())/scatter-add | solution.py:44
  424.8 1.9 convolution_add_fusion.1
  427.4 15.5 %all-reduce.8 = (bf16[768]{0:T(1024)(128)(2,1)S(1)}, bf16[768]{0:T(1024)(128)(2,1)S(1)}, bf16[32,12]{1,0:T(8,128)(2,1)S(1)}) all-reduce(bf16[768]{0:T(1024)(128)(2,1)S(1)} %get-tuple-element.50, bf16[768]{0:T(1024)(128)(2,1)S(1)} %copy-done.41, ...), channel_id=9, replica_groups=mesh['dp'=4,'expert'=8] {'dp'}, use_global_device_ids=true, to_apply=%region_21.22.clone | all-reduce | flops 1920 | bytes 7680
  447.8 19.7 %reduce-scatter.16.cloned.1.call-done = bf16[192,768]{1,0:T(8,128)(2,1)} async-done(((bf16[768,768]{1,0:T(8,128)(2,1)}), bf16[192,768]{1,0:T(8,128)(2,1)}) %reduce-scatter.16.cloned.1.call-update) | async-done | bytes 294928 | tf_op jit(solution)/shard_map/reduce_scatter | solution.py:229
  469.7 2.5 convert_element_type.269
  472.7 8.9 %reduce.2 = bf16[8,73980]{1,0:T(8,128)(2,1)S(1)} reduce(bf16[8,1,73980]{2,1,0:T(2,128)(2,1)} %convert_element_type.269, bf16[]{:T(256)} %broadcast.216), dimensions={1}, to_apply=%convert_element_type.269.reduce_sub_computation | reduce | bytes 2367362 | tf_op jit(solution)/shard_map/convert_element_type | solution.py:251
  481.5 1.8 reshape.341
  483.4 4.7 all-to-all-start.4
  489.7 3.7 convolution_bitcast_fusion.1
  493.4 24.2 %all-to-all-done.4 = bf16[8,2,36990]{2,1,0:T(2,128)(2,1)S(1)} async-done(((bf16[8,2,36990]{2,1,0:T(2,128)(2,1)}), bf16[8,2,36990]{2,1,0:T(2,128)(2,1)S(1)}, u32[]{:S(2)}, u32[]{:S(2)}) %all-to-all-start.4) | async-done | bytes 1183712 | tf_op jit(solution)/shard_map/all_to_all | solution.py:19
  517.6 5.9 reshape.342
  523.5 4.0 reduce_sum.132
  530.1 3.7 convolution_bitcast_fusion
  534.8 52.2 %all-reduce.14.cloned.1.call-done = bf16[591840]{0:T(1024)(128)(2,1)} async-done(((bf16[591840]{0:T(1024)(128)(2,1)}), bf16[591840]{0:T(1024)(128)(2,1)}) %all-reduce.14.cloned.1.call-update) | async-done | bytes 1183696
  (235 shorter events, 61.9 us)
Async XLA Ops:
  7.2 167.7 %copy-start = (bf16[1,768,768]{2,1,0:T(8,128)(2,1)S(1)}, bf16[1,768,768]{2,1,0:T(8,128)(2,1)}, u32[]{:S(2)}) copy-start(bf16[1,768,768]{2,1,0:T(8,128)(2,1)} %param.23) | copy-start | bytes 3538948
  7.2 13.7 %copy-start.51 = (u32[32]{0:T(128)S(1)}, u32[32]{0:T(128)}, u32[]{:S(2)}) copy-start(u32[32]{0:T(128)} %constant.73) | copy-start | bytes 388
  7.2 3.0 copy-start.49
  7.2 12.5 %copy-start.35 = (s32[128,1]{0,1:T(1,128)S(1)}, s32[128,1]{0,1:T(1,128)}, u32[]{:S(2)}) copy-start(s32[128,1]{0,1:T(1,128)} %param.25) | copy-start | bytes 1540
  7.2 14.9 %copy-start.53 = (bf16[192]{0:T(256)(128)(2,1)S(1)}, bf16[192]{0:T(256)(128)(2,1)}, u32[]{:S(2)}) copy-start(bf16[192]{0:T(256)(128)(2,1)} %param.20) | copy-start | bytes 1156
  7.3 15.1 %copy-start.54 = (bf16[192]{0:T(256)(128)(2,1)S(1)}, bf16[192]{0:T(256)(128)(2,1)}, u32[]{:S(2)}) copy-start(bf16[192]{0:T(256)(128)(2,1)} %param.21) | copy-start | bytes 1156
  7.3 94.4 %all-gather.6.cloned.1.call-start = ((), (), s32[]{:S(2)}) async-start(), calls=%async_computation.10 | async-start | bytes 1474560 | tf_op jit(solution)/shard_map/all_gather | solution.py:90
  8.0 96.2 %all-gather.8.cloned.1.call-start = ((), (), s32[]{:S(2)}) async-start(), calls=%async_computation.11 | async-start | bytes 1474560 | tf_op jit(solution)/shard_map/all_gather | solution.py:88
  8.7 97.2 %all-gather.10.cloned.1.call-start = ((), (), s32[]{:S(2)}) async-start(), calls=%async_computation.12 | async-start | bytes 1474560 | tf_op jit(solution)/shard_map/all_gather | solution.py:89
  9.5 119.7 %all-gather.12.cloned.1.call-start = ((), (), s32[]{:S(2)}) async-start(), calls=%async_computation.13 | async-start | bytes 1474560 | tf_op jit(solution)/shard_map/all_gather | solution.py:91
  10.1 75.9 %copy-start.46 = (s32[255]{0:T(256)}, s32[255]{0:T(256)S(1)}, u32[]{:S(2)}) copy-start(s32[255]{0:T(256)S(1)} %fusion.60) | copy-start | bytes 3064
  20.8 85.1 %copy-start.30 = (f32[128]{0:T(128)}, f32[128]{0:T(128)S(1)}, u32[]{:S(2)}) copy-start(f32[128]{0:T(128)S(1)} %add_rsqrt_fusion.1) | copy-start | bytes 1540
  86.0 6.9 %copy-start.48 = (bf16[192,8]{0,1:T(8,128)(2,1)S(1)}, bf16[192,8]{0,1:T(8,128)(2,1)}, u32[]{:S(2)}) copy-start(bf16[192,8]{0,1:T(8,128)(2,1)} %param.19) | copy-start | bytes 9220
  86.0 15.6 %copy-start.50 = (s32[128]{0:T(128)S(1)}, s32[128]{0:T(128)}, u32[]{:S(2)}) copy-start(s32[128]{0:T(128)} %param.26) | copy-start | bytes 1540
  92.9 38.1 %copy-start.26 = (f32[768]{0:T(1024)}, f32[768]{0:T(1024)S(1)}, u32[]{:S(2)}) copy-start(f32[768]{0:T(1024)S(1)} %convert_element_type.234) | copy-start | bytes 9220
  101.6 6.2 %copy-start.21 = (pred[128,128]{0,1:T(8,128)(4,1)}, pred[128,128]{0,1:T(8,128)(4,1)S(1)}, u32[]{:S(2)}) copy-start(pred[128,128]{0,1:T(8,128)(4,1)S(1)} %broadcast_compare_fusion) | copy-start | bytes 49156
  106.0 3.1 copy-start.10
  109.8 21.1 %copy-start.17 = (bf16[12,64,128]{2,1,0:T(8,128)(2,1)}, bf16[12,64,128]{2,1,0:T(8,128)(2,1)S(1)}, u32[]{:S(2)}) copy-start(bf16[12,64,128]{2,1,0:T(8,128)(2,1)S(1)} %convolution_convert_fusion.12) | copy-start | bytes 589828
  134.1 15.2 %all-to-all-start = ((bf16[8,20,768]{2,1,0:T(8,128)(2,1)}), bf16[8,20,768]{2,1,0:T(8,128)(2,1)}, u32[]{:S(2)}, u32[]{:S(2)}) async-start(bf16[8,20,768]{2,1,0:T(8,128)(2,1)} %reshape.271), calls=%async_computation | async-start | bytes 589824 | tf_op jit(solution)/shard_map/all_to_all | solution.py:143
  149.3 31.6 %all-to-all-start.2 = ((bf16[8,20,768]{2,1,0:T(8,128)(2,1)}), bf16[8,20,768]{2,1,0:T(8,128)(2,1)}, u32[]{:S(2)}, u32[]{:S(2)}) async-start(bf16[8,20,768]{2,1,0:T(8,128)(2,1)} %reshape.274), calls=%async_computation.2 | async-start | bytes 589824 | tf_op jit(solution)/shard_map/all_to_all | solution.py:166
  153.4 125.3 %all-reduce.16.cloned.1.call-start = ((), (), s32[]{:S(2)}) async-start(), calls=%async_computation.20 | async-start | bytes 3932160
  198.8 3.7 copy-start.15
  198.8 3.7 copy-start.52
  198.8 3.7 copy-start.56
  280.3 15.1 %all-to-all-start.1 = ((bf16[8,20,768]{2,1,0:T(8,128)(2,1)}), bf16[8,20,768]{2,1,0:T(8,128)(2,1)S(1)}, u32[]{:S(2)}, u32[]{:S(2)}) async-start(bf16[8,20,768]{2,1,0:T(8,128)(2,1)} %copy.101), calls=%async_computation.1 | async-start | bytes 589824 | tf_op jit(solution)/shard_map/all_to_all | solution.py:155
  284.9 15.3 %copy-start.9 = (bf16[128,768]{1,0:T(8,128)(2,1)S(1)}, bf16[128,768]{1,0:T(8,128)(2,1)}, u32[]{:S(2)}) copy-start(bf16[128,768]{1,0:T(8,128)(2,1)} %param.27) | copy-start | bytes 589828
  285.0 15.3 %copy-start.43 = (s32[128]{0:T(128)S(1)}, s32[128]{0:T(128)}, u32[]{:S(2)}) copy-start(s32[128]{0:T(128)} %multiply_add_fusion) | copy-start | bytes 1540
  286.0 15.6 %copy-start.34 = (f32[128]{0:T(128)S(1)}, f32[128]{0:T(128)}, u32[]{:S(2)}) copy-start(f32[128]{0:T(128)} %copy-done.33) | copy-start | bytes 1540
  286.0 15.6 %copy-start.36 = (s32[128,1]{0,1:T(1,128)S(1)}, s32[128,1]{0,1:T(1,128)}, u32[]{:S(2)}) copy-start(s32[128,1]{0,1:T(1,128)} %param.25) | copy-start | bytes 1540
  286.0 15.6 %copy-start.38 = (f32[128]{0:T(128)S(1)}, f32[128]{0:T(128)}, u32[]{:S(2)}) copy-start(f32[128]{0:T(128)} %copy-done.37) | copy-start | bytes 1540
  286.0 15.6 %copy-start.40 = (f32[128]{0:T(128)S(1)}, f32[128]{0:T(128)}, u32[]{:S(2)}) copy-start(f32[128]{0:T(128)} %copy-done.39) | copy-start | bytes 1540
  286.8 15.6 %copy-start.22 = (bf16[768,8]{0,1:T(8,128)(2,1)S(1)}, bf16[768,8]{0,1:T(8,128)(2,1)}, u32[]{:S(2)}) copy-start(bf16[768,8]{0,1:T(8,128)(2,1)} %reshape.319) | copy-start | bytes 36868
  295.4 14.5 %all-to-all-start.3 = ((bf16[8,20,768]{2,1,0:T(8,128)(2,1)}), bf16[8,20,768]{2,1,0:T(8,128)(2,1)}, u32[]{:S(2)}, u32[]{:S(2)}) async-start(bf16[8,20,768]{2,1,0:T(8,128)(2,1)} %copy.105), calls=%async_computation.3 | async-start | bytes 589824 | tf_op jit(solution)/shard_map/all_to_all | solution.py:176
  299.5 12.2 %copy-start.27 = (f32[768]{0:T(1024)S(1)}, f32[768]{0:T(1024)}, u32[]{:S(2)}) copy-start(f32[768]{0:T(1024)} %copy-done.26) | copy-start | bytes 9220
  299.5 12.1 %copy-start.45 = (f32[128]{0:T(128)S(1)}, f32[128]{0:T(128)}, u32[]{:S(2)}) copy-start(f32[128]{0:T(128)} %copy-done.44) | copy-start | bytes 1540
  299.5 143.6 %reduce-scatter.18.cloned.1.call-start = ((), (), s32[]{:S(2)}) async-start(), calls=%async_computation.19 | async-start | bytes 245760 | tf_op jit(solution)/shard_map/reduce_scatter | solution.py:232
  318.4 125.7 %reduce-scatter.10.cloned.1.call-start = ((), (), s32[]{:S(2)}) async-start(), calls=%async_computation.14 | async-start | bytes 1474560 | tf_op jit(solution)/shard_map/reduce_scatter | solution.py:220
  320.1 125.3 %reduce-scatter.12.cloned.1.call-start = ((), (), s32[]{:S(2)}) async-start(), calls=%async_computation.15 | async-start | bytes 1474560 | tf_op jit(solution)/shard_map/reduce_scatter | solution.py:223
  322.1 124.5 %reduce-scatter.14.cloned.1.call-start = ((), (), s32[]{:S(2)}) async-start(), calls=%async_computation.16 | async-start | bytes 1474560 | tf_op jit(solution)/shard_map/reduce_scatter | solution.py:226
  324.3 143.3 %reduce-scatter.16.cloned.1.call-start = ((), (), s32[]{:S(2)}) async-start(), calls=%async_computation.17 | async-start | bytes 1474560 | tf_op jit(solution)/shard_map/reduce_scatter | solution.py:229
  328.5 95.4 %copy-start.47 = (s32[255]{0:T(256)S(1)}, s32[255]{0:T(256)}, u32[]{:S(2)}) copy-start(s32[255]{0:T(256)} %copy-done.46) | copy-start | bytes 3064
  328.5 95.7 %copy-start.5 = (bf16[768,768]{1,0:T(8,128)(2,1)S(1)}, bf16[768,768]{1,0:T(8,128)(2,1)}, u32[]{:S(2)}) copy-start(bf16[768,768]{1,0:T(8,128)(2,1)} %all-gather.8.cloned.1.call-done) | copy-start | bytes 3538948
  483.4 5.0 copy-start.55
  483.4 6.3 %copy-start.16 = (bf16[640,768]{1,0:T(8,128)(2,1)S(1)}, bf16[640,768]{1,0:T(8,128)(2,1)}, u32[]{:S(2)}) copy-start(bf16[640,768]{1,0:T(8,128)(2,1)} %reshape.272) | copy-start | bytes 2949124
  483.4 34.2 %all-to-all-start.4 = ((bf16[8,2,36990]{2,1,0:T(2,128)(2,1)}), bf16[8,2,36990]{2,1,0:T(2,128)(2,1)S(1)}, u32[]{:S(2)}, u32[]{:S(2)}) async-start(bf16[8,2,36990]{2,1,0:T(2,128)(2,1)} %reshape.341), calls=%async_computation.8 | async-start | bytes 2367488 | tf_op jit(solution)/shard_map/all_to_all | solution.py:19
  488.1 98.9 %all-reduce.14.cloned.1.call-start = ((), (), s32[]{:S(2)}) async-start(), calls=%async_computation.18 | async-start | bytes 2367488
  530.1 3.7 copy-start.32
  590.2 6.1 %copy-start.1 = (bf16[1,768,768]{2,1,0:T(8,128)(2,1)S(1)}, bf16[1,768,768]{2,1,0:T(8,128)(2,1)}, u32[]{:S(2)}) copy-start(bf16[1,768,768]{2,1,0:T(8,128)(2,1)} %param.23) | copy-start | bytes 3538948
  (25 other events, 34.1 us)
Sparse Core Ops, SparseCore 0:
  9.9 30.4 all-gather.5
  42.3 27.7 all-gather.7
  71.9 27.7 all-gather.9
  101.4 27.7 all-gather.11
  210.8 67.7 all-reduce.15
  318.5 21.9 reduce-scatter.17
  344.0 28.5 reduce-scatter.9
  376.0 28.5 reduce-scatter.11
  407.5 28.6 reduce-scatter.13
  439.0 28.4 reduce-scatter.15
  530.2 56.6 all-reduce.13
where the time goes:
time: 612 us; the launch traced here: 603 us
  waiting for transfers between devices  206 us (34%)
  local copies, waits for them, and re-layouts  130 us (21%)
  other arithmetic  106 us (17%)
  blocking collectives  71.8 us (12%)
  matrix products  48.8 us (8%)
  starting transfers between devices  22.8 us (4%)
  between operations  17.8 us (3%)
    unnamed x13, waiting for transfers between devices  122 us
    scatter-add x1, other arithmetic, relative_bias(): return jnp.transpose(per_offset[lookup], (2, 0, 1))  87.6 us
    gather x2, local copies, waits for them, and re-layouts, relative_bias(): return jnp.transpose(per_offset[lookup], (2, 0, 1))  61.3 us
    unnamed x2, blocking collectives  24.5 us
    all_to_all x1, waiting for transfers between devices, sent_and_summed(): lax.all_to_all(blocks, axis, split_axis=0, concat_axis=0, tiled=True)  24.2 us
    unnamed x132, local copies, waits for them, and re-layouts  20 us
    reduce_scatter x1, waiting for transfers between devices, on_device(): lax.psum_scatter(g_attn_out.astype(jnp.bfloat16), 'dp', scatter_dimension...  19.7 us
    all_gather x1, waiting for transfers between devices, on_device(): lax.all_gather(w_attn_out, 'dp', axis=0, tiled=True)  19.4 us
  transfers between devices with their start and end apart: 16, of which 8 were waited for; matrix products, arithmetic and copies ran while one was open for 36% of the time, Pallas kernels for 0%

commit v1 on v0

v1 whole, which is shorter than its diff:
```python
from functools import partial

import jax
import jax.numpy as jnp
import numpy as np
from jax import lax
from jax.experimental import pallas as pl
from jax.experimental.pallas import tpu as pltpu
from jax.sharding import PartitionSpec as P

eps = 1e-06
bucket_edges = (12, 16, 23, 32, 46, 64, 91)
f32 = jnp.float32
bf16 = jnp.bfloat16
i32 = jnp.int32
gelu_a = float(np.sqrt(2.0 / np.pi))
gelu_b = 0.044715

owner_of = (1, 2, 0, 3)


def nn(left, right):
    return lax.dot_general(left, right, (((1,), (0,)), ((), ())), preferred_element_type=f32)


def nt(left, right):
    return lax.dot_general(left, right, (((1,), (1,)), ((), ())), preferred_element_type=f32)


def tn(left, right):
    return lax.dot_general(left, right, (((0,), (0,)), ((), ())), preferred_element_type=f32)


def iota(shape, dim):
    return lax.broadcasted_iota(i32, shape, dim)


def call(body, outs, idx, *args, scratch=()):
    return pl.pallas_call(
        body,
        out_shape=[jax.ShapeDtypeStruct(s, d) for s, d in outs],
        in_specs=[pl.BlockSpec(memory_space=pltpu.SMEM)]
        + [pl.BlockSpec(memory_space=pltpu.VMEM)] * len(args),
        out_specs=[pl.BlockSpec(memory_space=pltpu.VMEM)] * len(outs),
        scratch_shapes=list(scratch),
        compiler_params=pltpu.CompilerParams(vmem_limit_bytes=40 * 1024 * 1024),
    )(idx, *args)


def rms_scale(values):
    return lax.rsqrt(jnp.mean(values * values, axis=-1, keepdims=True) + eps)


def norm_back(d_normed, normed, scale):
    return scale * (d_normed - normed * jnp.mean(d_normed * normed, axis=-1, keepdims=True))


def bucket_onehot(rows, length, centred):
    col = iota((rows, 2 * length), 1)
    n = (length - 1) - col if centred else jnp.where(col < length, -col, 2 * length - col)
    mag = jnp.abs(n)
    far = jnp.full_like(mag, 8)
    for threshold in bucket_edges:
        far = far + (mag >= threshold).astype(i32)
    bucket = jnp.where(n < 0, 16, 0) + jnp.where(mag < 8, mag, far)
    return (bucket == iota((rows, 2 * length), 0)).astype(f32).astype(bf16)


def pack_body(experts, smalls, idx, wq, wk, wv, wo, wr, g1, g2, tab, out):
    rows, width = wq.shape
    core = idx[2]

    @pl.when(core == 0)
    def _():
        out[0:rows, :] = wq[...]
        out[rows : 2 * rows, :] = wv[...]

    @pl.when(core == 1)
    def _():
        out[0:rows, :] = wk[...]
        out[rows : 2 * rows, :] = wo[...]

    heads = tab.shape[1]
    pick = (iota((smalls, experts), 0) == iota((smalls, experts), 1)).astype(f32).astype(bf16)
    part = nt(pick, wr[...])
    line = iota((smalls, rows), 0)
    part = part + jnp.where(line == experts, g1[...].astype(f32), 0.0)
    part = part + jnp.where(line == experts + 1, g2[...].astype(f32), 0.0)
    spread = (iota((rows, width), 0) == iota((rows, width), 1)).astype(f32).astype(bf16)
    whole = nn(part.astype(bf16), spread)
    pick_t = (iota((smalls, heads), 0) == iota((smalls, heads), 1) + experts + 2).astype(f32)
    table_t = nt(pick_t.astype(bf16), tab[...])
    shard = tab.shape[0]
    spread_t = (iota((shard, width), 0) + rows == iota((shard, width), 1)).astype(f32)
    whole = whole + nn(table_t.astype(bf16), spread_t.astype(bf16))
    out[2 * rows : 2 * rows + smalls, :] = whole.astype(bf16)


def place_body(experts, idx, consts, routes2, cot, cot_t, place, rows_out):
    me = idx[1]
    slots = place.shape[0]
    both = routes2.shape[1]
    half = both // 2
    route = routes2[...]
    hot = (iota((experts, both), 0) == route).astype(f32)
    a, b = iota((both, both), 0), iota((both, both), 1)
    earlier = ((a < b) & ((a < half) == (b < half))).astype(f32).astype(bf16)
    ranks = nn(hot.astype(bf16), earlier)
    slot = jnp.sum(hot * ranks, axis=0, keepdims=True).astype(i32)
    which = consts[:, 0:1] ^ me
    turn = consts[:, 1:2]
    number = consts[:, 2:3]
    side = (iota((slots, both), 1) >= half).astype(i32)
    hit = (which == route) & (number == slot) & (turn == side)
    placer = hit.astype(f32).astype(bf16)
    place[...] = placer
    rows = nn(placer[:, 0:half], cot[...]) + nn(placer[:, half:both], cot_t[...])
    rows_out[...] = rows.astype(bf16)


def place_rows_body(idx, place, own, other, rows_out):
    half = own.shape[0]
    rows = nn(place[:, 0:half], own[...]) + nn(place[:, half : 2 * half], other[...])
    rows_out[...] = rows.astype(bf16)


def unplace_body(idx, place, rows, own, other):
    half = own.shape[0]
    arrived = rows[...]
    own[...] = tn(place[:, 0:half], arrived)
    other[...] = tn(place[:, half : 2 * half], arrived).astype(bf16)


def attend_body(
    experts, smalls, heads, idx,
    tokens, seg_c, seg_r, routes_c, wq, wk, wv, wo, own, hx, hy, da, db, tx, ty, ta, tb,
    w_all, small_all, q_o, k_o, v_o, probs_o, ctx_o, mixed_o, hcat_o, rp_o,
):
    mine, core = idx[0], idx[2]
    rows, width = wq.shape
    length = tokens.shape[0]
    size = width // heads
    home = pl.multiple_of(mine * rows, 64)
    for m, w in enumerate((wq, wk, wv, wo)):
        w_all[m, pl.ds(home, rows), :] = w[...]
    for k, piece, held in ((1, hx, core), (2, hy, core), (1, tx, 1 - core), (2, ty, 1 - core)):
        at = pl.multiple_of((mine ^ k) * rows, 64)
        w_all[held, pl.ds(at, rows), :] = piece[0:rows, :]
        w_all[2 + held, pl.ds(at, rows), :] = piece[rows : 2 * rows, :]
    cut = da.shape[0]
    at = pl.multiple_of((mine ^ 3) * rows, 64)
    for first, second, held in ((da, db, core), (ta, tb, 1 - core)):
        w_all[held, pl.ds(at, rows), :] = first[0:rows, :]
        w_all[2 + held, pl.ds(at, cut - rows), :] = first[rows:cut, :]
        w_all[2 + held, pl.ds(at + (cut - rows), 2 * rows - cut), :] = second[0 : 2 * rows - cut, :]
    small = jnp.zeros((smalls, width), f32)
    table_t = jnp.zeros((smalls, 128), f32)
    shard = 32 // 4
    for k, piece, start in ((0, own, 2 * rows), (1, hx, 2 * rows), (2, hy, 2 * rows), (3, db, 2 * rows - cut)):
        j = mine ^ k
        part = piece[start : start + smalls, 0:256]
        r, c = iota((256, width), 0), iota((256, width), 1)
        small = small + nn(part, ((r < rows) & (c == r + rows * j)).astype(f32).astype(bf16))
        r, c = iota((256, 128), 0), iota((256, 128), 1)
        keep = (r >= rows) & (r < rows + shard) & (c == r - rows + shard * j)
        table_t = table_t + nn(part, keep.astype(f32).astype(bf16))
    small_all[...] = small
    gain1 = small[experts : experts + 1, :]
    gain2 = small[experts + 1 : experts + 2, :]
    per_offset = nn(table_t.astype(bf16), bucket_onehot(128, length, False))

    x = tokens[...].astype(f32)
    h1 = (x * rms_scale(x) * gain1).astype(bf16)
    q_o[...] = nn(h1, w_all[0]).astype(bf16)
    k_o[...] = nn(h1, w_all[1]).astype(bf16)
    v_o[...] = nn(h1, w_all[2]).astype(bf16)
    same = seg_c[...] == seg_r[...]
    low = iota((length, 2 * size), 1) < size
    zero = jnp.zeros((length, 2 * size), bf16)
    for p in range(heads // 2):
        cols = slice(2 * size * p, 2 * size * (p + 1))
        q2, k2, v2 = q_o[:, cols], k_o[:, cols], v_o[:, cols]
        got = []
        for t in range(2):
            h = 2 * p + t
            qh = jnp.where(low, q2, zero) if t == 0 else jnp.where(low, zero, q2)
            line = per_offset[experts + 2 + h : experts + 3 + h, :]
            bias = pltpu.roll(
                jnp.broadcast_to(line, (length, 2 * length)), 0, 1, stride=1, stride_axis=0
            )[:, 0:length]
            s = jnp.where(same, nt(qh, k2) + bias, -1000000000.0)
            e = jnp.exp(s - jnp.max(s, axis=-1, keepdims=True))
            pr = e / jnp.sum(e, axis=-1, keepdims=True)
            probs_o[h] = pr
            got.append(nn(pr.astype(bf16), v2))
        ctx_o[:, cols] = jnp.where(low, got[0], got[1]).astype(bf16)
    mixed = x + nn(ctx_o[...], w_all[3])
    mixed_o[...] = mixed
    h2 = (mixed * rms_scale(mixed) * gain2).astype(bf16)
    logits = nt(h2, small[0:experts, :].astype(bf16))
    e = jnp.exp(logits - jnp.max(logits, axis=-1, keepdims=True))
    rp = e / jnp.sum(e, axis=-1, keepdims=True)
    rp_o[...] = rp
    gate = jnp.sum(jnp.where(routes_c[...] == iota((length, experts), 1), rp, 0.0), axis=-1, keepdims=True)
    hcat_o[:, 0:width] = h2
    high = gate.astype(bf16).astype(f32)
    lane = iota((length, 128), 1)
    tail = jnp.where(lane == 0, high, jnp.where(lane == 1, gate - high, 0.0))
    hcat_o[:, width : width + 128] = tail.astype(bf16)


def back_in_body(idx, w_out, *refs):
    for k in range(4):
        refs[4][k] = nt(refs[k][...], w_out[...])


def expert_body(idx, w_in, g_all, x0, x1, x2, x3, y0, y1, y2, y3, hid_o, dpre_o):
    width = w_in.shape[0]
    lane = iota((x0.shape[0], 128), 1)
    for k, (x, y) in enumerate(((x0, y0), (x1, y1), (x2, y2), (x3, y3))):
        pre = nn(x[:, 0:width], w_in[...])
        tail = x[:, width : width + 128].astype(f32)
        gate = jnp.sum(jnp.where(lane < 2, tail, 0.0), axis=-1, keepdims=True)
        sq = pre * pre
        t = jnp.tanh(gelu_a * (pre + gelu_b * sq * pre))
        hid = (0.5 * pre * (1.0 + t)).astype(bf16)
        slope = 0.5 * (1.0 + t) + 0.5 * pre * (1.0 - t * t) * (gelu_a * (1.0 + 3.0 * gelu_b * sq))
        g = g_all[k]
        dpre = (gate * g * slope).astype(bf16)
        hid_o[k] = hid
        dpre_o[k] = dpre
        d_gate = jnp.sum(hid.astype(f32) * g, axis=-1, keepdims=True)
        y[:, 0:width] = nt(dpre, w_in[...]).astype(bf16)
        y[:, width : width + 128] = jnp.where(lane == 0, d_gate, 0.0).astype(bf16)


def expert_out_body(idx, w_out, hid, y0, y1, y2, y3):
    for k, y in enumerate((y0, y1, y2, y3)):
        y[...] = nn(hid[k], w_out[...]).astype(bf16)


def expert_grad_body(idx, hid, dpre, x0, x1, x2, x3, g0, g1, g2, g3, gi, go):
    width = gi.shape[1]
    lane = iota((x0.shape[0], 128), 1)
    acc_i = jnp.zeros((width, dpre.shape[2]), f32)
    for k, x in enumerate((x0, x1, x2, x3)):
        acc_i = acc_i + tn(x[:, 0:width], dpre[k])
    gi[0] = acc_i
    acc_o = jnp.zeros((hid.shape[2], width), f32)
    for k, (x, g) in enumerate(((x0, g0), (x1, g1), (x2, g2), (x3, g3))):
        tail = x[:, width : width + 128].astype(f32)
        gate = jnp.sum(jnp.where(lane < 2, tail, 0.0), axis=-1, keepdims=True)
        acc_o = acc_o + tn(hid[k], (gate * g[...].astype(f32)).astype(bf16))
    go[0] = acc_o


def attend_back_body(
    experts, heads, chips, idx,
    own, other, mixed_r, cot, rp_r, routes_c, small_all, w_all, q, k, v, probs, ctx,
    dmixed_o, d_o, router_o, gain2_o, table_o, *rest,
):
    turned, diag = rest[:-1], rest[-1]
    length, width = mixed_r.shape
    size = width // heads
    back = own[...] + other[...].astype(f32)
    lane = iota((length, 128), 1)
    d_gate = jnp.sum(jnp.where(lane == 0, back[:, width : width + 128], 0.0), axis=-1, keepdims=True)
    hot = (routes_c[...] == iota((length, experts), 1)).astype(f32)
    rp = rp_r[...]
    gate = jnp.sum(rp * hot, axis=-1, keepdims=True)
    d_logits = (rp * (hot - gate) * d_gate).astype(bf16)
    gain2 = small_all[experts + 1 : experts + 2, :]
    wr_t = small_all[0:experts, :].astype(bf16)
    mixed = mixed_r[...]
    scale2 = rms_scale(mixed)
    normed2 = mixed * scale2
    h2 = (normed2 * gain2).astype(bf16)
    router_o[...] = tn(d_logits, h2)
    d_h2 = nn(d_logits, wr_t) + back[:, 0:width]
    gain2_o[...] = jnp.sum(d_h2 * normed2, axis=0, keepdims=True)
    d_mixed = cot[...].astype(f32) + norm_back(d_h2 * gain2, normed2, scale2)
    dmixed_o[...] = d_mixed
    d_attn = d_mixed.astype(bf16)
    d_o[3] = d_attn
    d_ctx = nt(d_attn, w_all[3]).astype(bf16)
    low = iota((length, 2 * size), 1) < size
    zero = jnp.zeros((length, 2 * size), bf16)
    blank = jnp.zeros((length, length), f32)
    upside = iota((length, length), 0) + iota((length, length), 1) == length - 1
    upside = upside.astype(f32).astype(bf16)
    for p in range(heads // 2):
        cols = slice(2 * size * p, 2 * size * (p + 1))
        q2, k2, v2, c2 = q[:, cols], k[:, cols], v[:, cols], d_ctx[:, cols]
        gq, gk, gv = [], [], []
        for t in range(2):
            h = 2 * p + t
            ch = jnp.where(low, c2, zero) if t == 0 else jnp.where(low, zero, c2)
            pr = probs[h]
            dw = nt(ch, v2)
            gv.append(tn(pr.astype(bf16), c2))
            ds = (pr * (dw - jnp.sum(pr * dw, axis=-1, keepdims=True))).astype(bf16)
            gq.append(nn(ds, k2))
            gk.append(tn(ds, q2))
            wide = jnp.concatenate([nn(upside, ds), blank], axis=1)
            wide = pltpu.roll(wide, 0, 1, stride=1, stride_axis=0)
            diag[h : h + 1, :] = jnp.sum(wide, axis=0, keepdims=True)
        d_o[0, :, cols] = jnp.where(low, gq[0], gq[1]).astype(bf16)
        d_o[1, :, cols] = jnp.where(low, gk[0], gk[1]).astype(bf16)
        d_o[2, :, cols] = jnp.where(low, gv[0], gv[1]).astype(bf16)
    sums = diag[0:heads, :]
    onehot = bucket_onehot(128, length, True)
    high = sums.astype(bf16)
    mid = (sums - high.astype(f32)).astype(bf16)
    table_o[...] = nt(high, onehot) + nt(mid, onehot)
    if chips == 4:
        z = idx[3]
        for zr in range(4):
            dest = z ^ zr
            for m in range(4):

                @pl.when(dest == owner_of[m])
                def _():
                    turned[zr][...] = d_o[m]


def token_grad_body(experts, smalls, idx, tokens, dmixed, d, w_all, small_all, router, gain2, table, dtok_o, small_o, table_o):
    x = tokens[...].astype(f32)
    scale1 = rms_scale(x)
    normed1 = x * scale1
    gain1 = small_all[experts : experts + 1, :]
    d_h1 = nt(d[0], w_all[0]) + nt(d[1], w_all[1]) + nt(d[2], w_all[2])
    g_gain1 = jnp.sum(d_h1 * normed1, axis=0, keepdims=True)
    dtok_o[...] = dmixed[...] + norm_back(d_h1 * gain1, normed1, scale1)
    width = x.shape[1]
    pick = (iota((smalls, experts), 0) == iota((smalls, experts), 1)).astype(f32).astype(bf16)
    line = iota((smalls, width), 0)
    out = nn(pick, router[...].astype(bf16))
    out = out + jnp.where(line == experts, g_gain1, 0.0) + jnp.where(line == experts + 1, gain2[...], 0.0)
    small_o[...] = out.astype(bf16)
    heads = table.shape[0]
    pick_t = (iota((smalls, heads), 0) == iota((smalls, heads), 1) + experts + 2).astype(f32)
    table_o[...] = nn(pick_t.astype(bf16), table[...].astype(bf16)).astype(bf16)


def mixer_grad_body(experts, idx, small_all, l0, l1, l2, l3, c0, c1, c2, c3, d0, d1, d2, d3, keep, send, acc, left):
    z, core = idx[3], idx[2]
    gain1 = small_all[experts : experts + 1, :]
    rows = l0.shape[0]

    @pl.when(z == owner_of[3])
    def _():
        for n, c in enumerate((c0, c1, c2, c3)):
            left[n * rows : (n + 1) * rows, :] = c[...]

    @pl.when(z != owner_of[3])
    def _():
        for n, item in enumerate((l0, l1, l2, l3)):
            x = item[...].astype(f32)
            left[n * rows : (n + 1) * rows, :] = (x * rms_scale(x) * gain1).astype(bf16)

    right = jnp.concatenate([d0[...], d1[...], d2[...], d3[...]], axis=0)
    acc[...] = tn(left[...], right)
    half = keep.shape[1]
    keep[...] = acc[:, pl.ds(pl.multiple_of(core * half, 128), half)]
    send[...] = acc[:, pl.ds(pl.multiple_of((1 - core) * half, 128), half)].astype(bf16)


def share_body(shard, idx, keep, got, small, table, s0, s1, s2, s3, total):
    mine = idx[0]
    total[...] = keep[...] + got[...].astype(f32)
    half = keep.shape[1]
    rows = total.shape[0] // 4
    width = small.shape[1]
    for k, out in enumerate((s0, s1, s2, s3)):
        j = mine ^ k
        out[0:rows, :] = total[pl.ds(pl.multiple_of(j * rows, 64), rows), :].astype(bf16)
        r, c = iota((width, half), 0), iota((width, half), 1)
        part = nn(small[...], ((c < rows) & (r == c + rows * j)).astype(f32).astype(bf16))
        r, c = iota((128, half), 0), iota((128, half), 1)
        keep_t = (c >= rows) & (c < rows + shard) & (r == c - rows + shard * j)
        part = part + nn(table[...], keep_t.astype(f32).astype(bf16))
        out[rows : rows + small.shape[0], :] = part.astype(bf16)


def sum_body(idx, a, b, c, d, out):
    out[...] = (
        a[...].astype(f32) + b[...].astype(f32) + c[...].astype(f32) + d[...].astype(f32)
    ).astype(bf16)


def finish_body(idx, a0, a1, a2, a3, b0, b1, b2, b3, gq, gk, gv, go, small):
    z, core = idx[3], idx[2]
    half = a0.shape[1]
    rows = gq.shape[0]
    at = pl.multiple_of(core * half, 128)
    off = pl.multiple_of((1 - core) * half, 128)
    for m, out in enumerate((gq, gk, gv, go)):
        for zr, (a, b) in enumerate(((a0, b0), (a1, b1), (a2, b2), (a3, b3))):

            @pl.when((z ^ zr) == owner_of[m])
            def _():
                out[:, pl.ds(at, half)] = a[0:rows, :].astype(f32)
                out[:, pl.ds(off, half)] = b[0:rows, :].astype(f32)

    total = jnp.zeros(small.shape, f32)
    for item in (a0, a1, a2, a3, b0, b1, b2, b3):
        total = total + item[rows : rows + small.shape[0], :].astype(f32)
    small[...] = total


def on_device(
    tokens, w_query, w_key, w_value, w_attn_out, w_router, norm1_gain, norm2_gain, bias_table,
    w_expert_in, w_expert_out, routes, segments, cotangent,
):
    experts = lax.axis_size("expert")
    chips = experts // 2
    length, width = tokens.shape
    heads = bias_table.shape[1]
    rows = w_query.shape[0]
    shard = bias_table.shape[0]
    cap = 5 * length // (4 * experts)
    smalls = -(-(experts + 2 + heads) // 16) * 16
    slots = experts * cap
    wide = width + 128

    def along(x, axis, mask):
        n = lax.axis_size(axis)
        return lax.ppermute(x, axis, [(s, s ^ mask) for s in range(n)])

    def twin(x):
        return along(x, "expert", 1)

    def chip_exchange(x):
        cut = 2 * cap
        parts = [x[0:cut]]
        for zr in range(1, chips):
            parts.append(along(x[cut * zr : cut * (zr + 1)], "expert", 2 * zr))
        return jnp.concatenate(parts, axis=0)

    mine, me = lax.axis_index("dp"), lax.axis_index("expert")
    idx = jnp.stack([mine, me, me % 2, me // 2]).astype(i32)
    weight_in, weight_out = w_expert_in[0], w_expert_out[0]

    parcel = call(
        partial(pack_body, experts, smalls), [((2 * rows + smalls, width), bf16)], idx,
        w_query, w_key, w_value, w_attn_out, w_router, norm1_gain[None], norm2_gain[None], bias_table,
    )[0]
    cut = (2 * rows + smalls) // 2
    hx = along(parcel, "dp", 1)
    hy = along(parcel, "dp", 2)
    da = along(hx[0:cut], "dp", 2)
    db = along(hy[cut:], "dp", 1)
    tx, ty, ta, tb = twin(hx), twin(hy), twin(da), twin(db)

    route_row = routes.reshape(1, length)
    routes2 = jnp.concatenate([route_row, twin(route_row.astype(f32)).astype(i32)], axis=1)
    r = np.arange(slots)
    consts = np.zeros((slots, 128), np.int32)
    consts[:, 0] = 2 * (r // (2 * cap))
    consts[:, 1] = (r // cap) % 2
    consts[:, 2] = r % cap
    place, g_rows = call(
        partial(place_body, experts), [((slots, 2 * length), bf16), ((slots, width), bf16)], idx,
        jnp.asarray(consts), routes2, cotangent, twin(cotangent),
    )
    g_here = chip_exchange(g_rows)
    g_set = [g_here] + [along(g_here, "dp", k) for k in (1, 2, 3)]
    g_back = call(back_in_body, [((4, slots, width), f32)], idx, weight_out, *g_set)[0]

    if chips == 4:
        tok_all = [tokens] + [along(tokens, "expert", 2 * zr) for zr in range(1, 4)]

    w_all, small_all, q, k, v, probs, ctx, mixed, hcat, rp = call(
        partial(attend_body, experts, smalls, heads),
        [
            ((4, width, width), bf16), ((smalls, width), f32),
            ((length, width), bf16), ((length, width), bf16), ((length, width), bf16),
            ((heads, length, length), f32), ((length, width), bf16), ((length, width), f32),
            ((length, wide), bf16), ((length, experts), f32),
        ],
        idx, tokens, segments.reshape(length, 1), segments.reshape(1, length), routes,
        w_query, w_key, w_value, w_attn_out, parcel, hx, hy, da, db, tx, ty, ta, tb,
    )

    x_rows = call(place_rows_body, [((slots, wide), bf16)], idx, place, hcat, twin(hcat))[0]
    x_here = chip_exchange(x_rows)
    x_set = [x_here] + [along(x_here, "dp", kk) for kk in (1, 2, 3)]
    *d_parts, hid, dpre = call(
        expert_body,
        [((slots, wide), bf16)] * 4 + [((4, slots, width), bf16)] * 2,
        idx, weight_in, g_back, *x_set,
    )
    d_got = [d_parts[0]] + [along(d_parts[kk], "dp", kk) for kk in (1, 2, 3)]
    d_here = call(sum_body, [((slots, wide), bf16)], idx, *d_got)[0]
    d_rows = chip_exchange(d_here)
    back_own, back_other = call(
        unplace_body, [((length, wide), f32), ((length, wide), bf16)], idx, place, d_rows
    )
    back_other = twin(back_other)

    outs = [
        ((length, width), f32), ((4, length, width), bf16), ((experts, width), f32),
        ((1, width), f32), ((heads, 128), f32),
    ]
    if chips == 4:
        outs = outs + [((length, width), bf16)] * 4
    d_mixed, d_all, g_router, g_gain2, g_table, *turned = call(
        partial(attend_back_body, experts, heads, chips), outs, idx,
        back_own, back_other, mixed, cotangent, rp, routes, small_all, w_all, q, k, v, probs, ctx,
        scratch=[pltpu.VMEM((16, 2 * length), f32)],
    )
    d_tokens, small_g, table_g = call(
        partial(token_grad_body, experts, smalls),
        [((length, width), f32), ((smalls, width), bf16), ((smalls, 128), bf16)], idx,
        tokens, d_mixed, d_all, w_all, small_all, g_router, g_gain2, g_table,
    )

    y_parts = call(expert_out_body, [((slots, width), bf16)] * 4, idx, weight_out, hid)
    y_got = [y_parts[0]] + [along(y_parts[kk], "dp", kk) for kk in (1, 2, 3)]
    y_here = call(sum_body, [((slots, width), bf16)], idx, *y_got)[0]
    y_rows = chip_exchange(y_here)
    y_own, y_other = call(
        unplace_body, [((length, width), f32), ((length, width), bf16)], idx, place, y_rows
    )
    y_other = twin(y_other)
    gate = jnp.sum(jnp.where(routes == jnp.arange(experts, dtype=i32)[None, :], rp, 0.0), axis=1, keepdims=True)
    layer_out = (mixed + gate * (y_own + y_other.astype(f32))).astype(bf16)

    grad_in, grad_out = call(
        expert_grad_body,
        [((1, width, weight_in.shape[1]), f32), ((1, weight_out.shape[0], width), f32)], idx,
        hid, dpre, *x_set, *g_set,
    )

    if chips == 4:
        ctx_all = [ctx] + [along(ctx, "expert", 2 * zr) for zr in range(1, 4)]
        d_in = [turned[0]] + [along(turned[zr], "expert", 2 * zr) for zr in range(1, 4)]
        keep, send = call(
            partial(mixer_grad_body, experts),
            [((width, width // 2), f32), ((width, width // 2), bf16)], idx,
            small_all, *tok_all, *ctx_all, *d_in,
            scratch=[pltpu.VMEM((width, width), f32), pltpu.VMEM((4 * length, width), bf16)],
        )
        parts = call(
            partial(share_body, shard), [((rows + smalls, width // 2), bf16)] * 4, idx,
            keep, twin(send), small_g, table_g, scratch=[pltpu.VMEM((width, width // 2), f32)],
        )
        got = [parts[0]] + [along(parts[kk], "dp", kk) for kk in (1, 2, 3)]
        total = call(sum_body, [((rows + smalls, width // 2), bf16)], idx, *got)[0]
        a_set = [total] + [along(total, "expert", 2 * zr) for zr in range(1, 4)]
        b_set = [twin(a) for a in a_set]
        g_q, g_k, g_v, g_o, small_t = call(
            finish_body, [((rows, width), f32)] * 4 + [((smalls, width // 2), f32)], idx, *a_set, *b_set
        )
        r_out = small_t[0:experts, 0:rows].T
        gain1_out = small_t[experts, 0:rows]
        gain2_out = small_t[experts + 1, 0:rows]
        table_out = small_t[experts + 2 : experts + 2 + heads, rows : rows + shard].T
    else:
        gain1 = small_all[experts : experts + 1]
        x = tokens.astype(f32)
        h1 = (x * rms_scale(x) * gain1).astype(bf16)
        both = jnp.concatenate(
            [tn(h1, d_all[0]), tn(h1, d_all[1]), tn(h1, d_all[2]), tn(ctx, d_all[3]), small_g.T.astype(f32)], axis=1
        )
        both = lax.psum_scatter(both, "dp", scatter_dimension=0, tiled=True)
        both = lax.psum(both, "expert")
        g_q, g_k, g_v, g_o = (both[:, m * width : (m + 1) * width] for m in range(4))
        rest = both[:, 4 * width :]
        r_out = rest[:, 0:experts]
        gain1_out, gain2_out = rest[:, experts], rest[:, experts + 1]
        tab = table_g.T[0 : 4 * shard, experts + 2 : experts + 2 + heads].astype(f32)
        table_out = lax.psum(lax.psum_scatter(tab, "dp", scatter_dimension=0, tiled=True), "expert")
    return (
        layer_out, d_tokens, g_q, g_k, g_v, g_o, r_out, gain1_out, gain2_out, table_out, grad_in, grad_out,
    )


def solution(mesh):
    return jax.shard_map(
        on_device,
        mesh=mesh,
        in_specs=(
            P(("dp", "expert"), None),
            P("dp", None),
            P("dp", None),
            P("dp", None),
            P("dp", None),
            P("dp", None),
            P("dp"),
            P("dp"),
            P("dp", None),
            P("expert", None, "dp"),
            P("expert", "dp", None),
            P(("dp", "expert"), None),
            P(("dp", "expert")),
            P(("dp", "expert"), None),
        ),
        out_specs=(
            P(("dp", "expert"), None),
            P(("dp", "expert"), None),
            P("dp", None),
            P("dp", None),
            P("dp", None),
            P("dp", None),
            P("dp", None),
            P("dp"),
            P("dp"),
            P("dp", None),
            P("expert", None, "dp"),
            P("expert", "dp", None),
        ),
        check_vma=False,
    )
```

time: 612 us -> 242 us (0.40); the launches traced: 603 us -> 241 us
  local copies, waits for them, and re-layouts: 130 us -> 14.5 us
  other arithmetic: 106 us -> 2.44 us
  waiting for transfers between devices: 206 us -> 107 us
  blocking collectives: 71.8 us -> 0 us
  starting transfers between devices: 22.8 us -> 76.3 us
  matrix products: 48.8 us -> 0 us
  Pallas kernels: 0 us -> 40.2 us
  between operations: 17.8 us -> 1.09 us
    unnamed x13 -> x0, waiting for transfers between devices: 122 us -> none
    ppermute x0 -> x57, waiting for transfers between devices: none -> 107 us  [along(): return lax.ppermute(x, axis, [(s, s ^ mask) for s in range(n)])]
    scatter-add x1 -> x0, other arithmetic: 87.6 us -> none  [relative_bias(): return jnp.transpose(per_offset[lookup], (2, 0, 1))]
    ppermute x0 -> x57, starting transfers between devices: none -> 76.3 us  [along(): return lax.ppermute(x, axis, [(s, s ^ mask) for s in range(n)])]
    gather x2 -> x0, local copies, waits for them, and re-layouts: 61.3 us -> none  [relative_bias(): return jnp.transpose(per_offset[lookup], (2, 0, 1))]
    dot_general x33 -> x0, matrix products: 48.8 us -> none  [the longest x9 17.9 us: matmul(): return jnp.dot(left, right, preferred_element_type=jnp.float32)]
    all_gather x4 -> x0, blocking collectives: 47.4 us -> none  [the longest x1 16.7 us: on_device(): lax.all_gather(arrived, 'dp', axis=0, tiled=True).reshape(-1, model_width)]
    all_to_all x5 -> x0, waiting for transfers between devices: 44.3 us -> none  [the longest x1 24.2 us: sent_and_summed(): lax.all_to_all(blocks, axis, split_axis=0, concat_axis=0, tiled=True)]
  transfers between devices with their start and end apart: 16 -> 57, of which waited for: 8 -> 23; matrix products, arithmetic and copies ran while one was open for 36% -> 2% of each run, Pallas kernels for 0% -> 9%
where the time goes in v1:
time: 242 us; the launch traced here: 241 us
  waiting for transfers between devices  107 us (44%)
  starting transfers between devices  76.3 us (32%)
  Pallas kernels  40.2 us (17%)
  local copies, waits for them, and re-layouts  14.5 us (6%)
  other arithmetic  2.44 us (1%)
    ppermute x57, waiting for transfers between devices, along(): return lax.ppermute(x, axis, [(s, s ^ mask) for s in range(n)])  107 us
    ppermute x57, starting transfers between devices, along(): return lax.ppermute(x, axis, [(s, s ^ mask) for s in range(n)])  76.3 us
    pallas_call x18, Pallas kernels, call(): pl.pallas_call(body, out_shape=[jax.ShapeDtypeStruct(s, d) for s, d in ou...  40.2 us
    unnamed x45, local copies, waits for them, and re-layouts  10.4 us
  transfers between devices with their start and end apart: 57, of which 23 were waited for; matrix products, arithmetic and copies ran while one was open for 2% of the time, Pallas kernels for 9%

profile of v1, /device:TPU:0, one launch (start us, length us, event | category | flops | bytes accessed | tf_op | source)
XLA Modules:
  0.0 241.2 jit_solution(12822830265073927780)
XLA Ops:
  8.4 3.0 %collective-permute-start = (bf16[416,768]{1,0:T(8,128)(2,1)S(1)}, bf16[416,768]{1,0:T(8,128)(2,1)S(1)}, u32[]{:S(2)}, u32[]{:S(2)}) collective-permute-start(bf16[416,768]{1,0:T(8,128)(2,1)S(1)} %shard_map.238.own), channel_id=1, source_target_pairs={{0,8},{8,0},{16,24},{24,16},{1,9},{9,1},{17,25},{25,17},{2,10},{10... | collective-permute-start | bytes 1916936 | tf_op jit(solution)/shard_map/ppermute | solution.py:428
  12.9 12.9 %collective-permute-done.hx = bf16[416,768]{1,0:T(8,128)(2,1)S(1)} collective-permute-done((bf16[416,768]{1,0:T(8,128)(2,1)S(1)}, bf16[416,768]{1,0:T(8,128)(2,1)S(1)}, u32[]{:S(2)}, u32[]{:S(2)}) %collective-permute-start) | collective-permute-done | bytes 639008 | tf_op jit(solution)/shard_map/ppermute | solution.py:428
  25.8 1.8 collective-permute-start.2
  27.7 1.6 collective-permute-start.3
  29.7 5.0 %collective-permute-done.2.da = bf16[208,768]{1,0:T(8,128)(2,1)} collective-permute-done((bf16[208,768]{1,0:T(8,128)(2,1)S(1)}, bf16[208,768]{1,0:T(8,128)(2,1)}, u32[]{:S(2)}, u32[]{:S(2)}) %collective-permute-start.2) | collective-permute-done | bytes 319520 | tf_op jit(solution)/shard_map/ppermute | solution.py:428
  46.2 7.2 %shard_map.239 = (bf16[4,768,768]{2,1,0:T(8,128)(2,1)S(1)}, f32[32,768]{1,0:T(8,128)S(1)}, bf16[128,768]{1,0:T(8,128)(2,1)S(1)}, bf16[128,768]{1,0:T(8,128)(2,1)...) custom-call(s32[4]{0:T(128)S(1)} %copy-done.14, ...), custom_call_target="tpu_custom_call" | custom-call | tf_op jit(solution)/shard_map/pallas_call | solution.py:39
  53.9 3.7 %collective-permute-start.12 = (bf16[40,768]{1,0:T(8,128)(2,1)S(1)}, bf16[40,768]{1,0:T(8,128)(2,1)S(1)}, u32[]{:S(2)}, u32[]{:S(2)}) collective-permute-start(bf16[40,768]{1,0:T(8,128)(2,1)S(1)} %get-tuple-element.139), channel_id=1, source_target_pairs={{0,6},{1,7},{2,4},{3,5},{4,2},{5,3},{6,0},{7,1},{8,14},{9,15},{10,... | collective-permute-start | bytes 184328 | tf_op jit(solution)/shard_map/ppermute | solution.py:428
  58.3 1.8 collective-permute-done.12
  60.1 3.0 %collective-permute-done.11 = bf16[40,768]{1,0:T(8,128)(2,1)S(1)} collective-permute-done((bf16[40,768]{1,0:T(8,128)(2,1)S(1)}, bf16[40,768]{1,0:T(8,128)(2,1)S(1)}, u32[]{:S(2)}, u32[]{:S(2)}) %collective-permute-start.11) | collective-permute-done | bytes 61472 | tf_op jit(solution)/shard_map/ppermute | solution.py:428
  63.2 1.5 collective-permute-start.13
  65.6 2.5 %collective-permute-start.19 = (bf16[40,896]{1,0:T(8,128)(2,1)S(1)}, bf16[40,896]{1,0:T(8,128)(2,1)S(1)}, u32[]{:S(2)}, u32[]{:S(2)}) collective-permute-start(bf16[40,896]{1,0:T(8,128)(2,1)S(1)} %get-tuple-element.131), channel_id=1, source_target_pairs={{0,6},{1,7},{2,4},{3,5},{4,2},{5,3},{6,0},{7,1},{8,14},{9,15},{10,... | collective-permute-start | bytes 215048 | tf_op jit(solution)/shard_map/ppermute | solution.py:428
  68.3 1.7 collective-permute-start.17
  70.0 2.4 %collective-permute-done.19 = bf16[40,896]{1,0:T(8,128)(2,1)S(1)} collective-permute-done((bf16[40,896]{1,0:T(8,128)(2,1)S(1)}, bf16[40,896]{1,0:T(8,128)(2,1)S(1)}, u32[]{:S(2)}, u32[]{:S(2)}) %collective-permute-start.19) | collective-permute-done | bytes 71712 | tf_op jit(solution)/shard_map/ppermute | solution.py:428
  72.5 2.6 %collective-permute-done.18 = bf16[40,896]{1,0:T(8,128)(2,1)S(1)} collective-permute-done((bf16[40,896]{1,0:T(8,128)(2,1)S(1)}, bf16[40,896]{1,0:T(8,128)(2,1)S(1)}, u32[]{:S(2)}, u32[]{:S(2)}) %collective-permute-start.18) | collective-permute-done | bytes 71712 | tf_op jit(solution)/shard_map/ppermute | solution.py:428
  76.8 1.8 collective-permute-start.22
  80.7 19.6 %collective-permute-done.14.refs_2_.g2 = bf16[160,768]{1,0:T(8,128)(2,1)S(1)} collective-permute-done((bf16[160,768]{1,0:T(8,128)(2,1)S(1)}, bf16[160,768]{1,0:T(8,128)(2,1)S(1)}, u32[]{:S(2)}, u32[]{:S(2)}) %collective-permute-start.14) | collective-permute-done | bytes 245792 | tf_op jit(solution)/shard_map/ppermute | solution.py:428
  100.2 2.2 shard_map.241.g_all
  102.5 3.8 %shard_map.243 = (bf16[160,896]{1,0:T(8,128)(2,1)S(1)}, bf16[160,896]{1,0:T(8,128)(2,1)S(1)}, bf16[160,896]{1,0:T(8,128)(2,1)S(1)}, bf16[160,896]{1,0:T(8,128)(2...) custom-call(s32[4]{0:T(128)S(1)} %copy-done.14, bf16[768,768]{1,0:T(8,128)(2,1)S(1)} %bitcast.19, ...), custom_call_target="tpu_custom_call" | custom-call | tf_op jit(solution)/shard_map/pallas_call | solution.py:39
  106.3 1.5 collective-permute-start.30
  109.9 6.3 %collective-permute-done.30.b = bf16[160,896]{1,0:T(8,128)(2,1)S(1)} collective-permute-done((bf16[160,896]{1,0:T(8,128)(2,1)S(1)}, bf16[160,896]{1,0:T(8,128)(2,1)S(1)}, u32[]{:S(2)}, u32[]{:S(2)}) %collective-permute-start.30) | collective-permute-done | bytes 286752 | tf_op jit(solution)/shard_map/ppermute | solution.py:428
  116.1 4.5 %collective-permute-done.31.c = bf16[160,896]{1,0:T(8,128)(2,1)S(1)} collective-permute-done((bf16[160,896]{1,0:T(8,128)(2,1)S(1)}, bf16[160,896]{1,0:T(8,128)(2,1)S(1)}, u32[]{:S(2)}, u32[]{:S(2)}) %collective-permute-start.31) | collective-permute-done | bytes 286752 | tf_op jit(solution)/shard_map/ppermute | solution.py:428
  121.4 2.0 collective-permute-start.35
  123.4 2.4 %collective-permute-start.33 = (bf16[40,896]{1,0:T(8,128)(2,1)S(1)}, bf16[40,896]{1,0:T(8,128)(2,1)S(1)}, u32[]{:S(2)}, u32[]{:S(2)}) collective-permute-start(bf16[40,896]{1,0:T(8,128)(2,1)S(1)} %get-tuple-element.129), channel_id=1, source_target_pairs={{0,2},{1,3},{2,0},{3,1},{4,6},{5,7},{6,4},{7,5},{8,10},{9,11},{10,... | collective-permute-start | bytes 215048 | tf_op jit(solution)/shard_map/ppermute | solution.py:428
  125.8 1.8 collective-permute-done.35
  132.7 1.9 collective-permute-start.39
  134.7 2.4 collective-permute-start.41
  137.1 5.3 %shard_map.249 = (f32[128,768]{1,0:T(8,128)S(1)}, bf16[4,128,768]{2,1,0:T(8,128)(2,1)S(1)}, f32[8,768]{1,0:T(8,128)S(1)}, f32[1,768]{1,0:T(1,128)S(1)}, f32[12,1...) custom-call(s32[4]{0:T(128)S(1)} %copy-done.14, ...), custom_call_target="tpu_custom_call" | custom-call | tf_op jit(solution)/shard_map/pallas_call | solution.py:39
  142.3 1.9 collective-permute-start.42
  144.3 4.1 %collective-permute-done.38.l2 = bf16[128,768]{1,0:T(8,128)(2,1)S(1)} collective-permute-done((bf16[128,768]{1,0:T(8,128)(2,1)S(1)}, bf16[128,768]{1,0:T(8,128)(2,1)S(1)}, u32[]{:S(2)}, u32[]{:S(2)}) %collective-permute-start.38) | collective-permute-done | bytes 196640 | tf_op jit(solution)/shard_map/ppermute | solution.py:428
  148.4 13.7 %collective-permute-start.44 = (bf16[128,768]{1,0:T(8,128)(2,1)S(1)}, bf16[128,768]{1,0:T(8,128)(2,1)S(1)}, u32[]{:S(2)}, u32[]{:S(2)}) collective-permute-start(bf16[128,768]{1,0:T(8,128)(2,1)S(1)} %get-tuple-element.96), channel_id=1, source_target_pairs={{0,4},{1,5},{2,6},{3,7},{4,0},{5,1},{6,2},{7,3},{8,12},{9,13},{10,... | collective-permute-start | bytes 589832 | tf_op jit(solution)/shard_map/ppermute | solution.py:428
  162.0 1.9 collective-permute-start.45
  163.9 9.7 %collective-permute-done.41.c2 = bf16[128,768]{1,0:T(8,128)(2,1)S(1)} collective-permute-done((bf16[128,768]{1,0:T(8,128)(2,1)S(1)}, bf16[128,768]{1,0:T(8,128)(2,1)S(1)}, u32[]{:S(2)}, u32[]{:S(2)}) %collective-permute-start.41) | collective-permute-done | bytes 196640 | tf_op jit(solution)/shard_map/ppermute | solution.py:428
  173.6 8.4 %collective-permute-done.44.d2 = bf16[128,768]{1,0:T(8,128)(2,1)S(1)} collective-permute-done((bf16[128,768]{1,0:T(8,128)(2,1)S(1)}, bf16[128,768]{1,0:T(8,128)(2,1)S(1)}, u32[]{:S(2)}, u32[]{:S(2)}) %collective-permute-start.44) | collective-permute-done | bytes 196640 | tf_op jit(solution)/shard_map/ppermute | solution.py:428
  182.1 1.8 shard_map.251
  187.3 1.8 collective-permute-start.25
  189.0 5.3 %collective-permute-done.23.b = bf16[160,768]{1,0:T(8,128)(2,1)S(1)} collective-permute-done((bf16[160,768]{1,0:T(8,128)(2,1)S(1)}, bf16[160,768]{1,0:T(8,128)(2,1)S(1)}, u32[]{:S(2)}, u32[]{:S(2)}) %collective-permute-start.23) | collective-permute-done | bytes 245792 | tf_op jit(solution)/shard_map/ppermute | solution.py:428
  194.3 5.1 %collective-permute-done.24.c = bf16[160,768]{1,0:T(8,128)(2,1)S(1)} collective-permute-done((bf16[160,768]{1,0:T(8,128)(2,1)S(1)}, bf16[160,768]{1,0:T(8,128)(2,1)S(1)}, u32[]{:S(2)}, u32[]{:S(2)}) %collective-permute-start.24) | collective-permute-done | bytes 245792 | tf_op jit(solution)/shard_map/ppermute | solution.py:428
  200.1 1.7 collective-permute-start.28
  201.8 3.8 %collective-permute-start.27 = (bf16[40,768]{1,0:T(8,128)(2,1)S(1)}, bf16[40,768]{1,0:T(8,128)(2,1)S(1)}, u32[]{:S(2)}, u32[]{:S(2)}) collective-permute-start(bf16[40,768]{1,0:T(8,128)(2,1)S(1)} %get-tuple-element.136), channel_id=1, source_target_pairs={{0,4},{1,5},{2,6},{3,7},{4,0},{5,1},{6,2},{7,3},{8,12},{9,13},{10,... | collective-permute-start | bytes 184328 | tf_op jit(solution)/shard_map/ppermute | solution.py:428
  205.6 2.7 %shard_map.250 = (f32[128,768]{1,0:T(8,128)}, bf16[32,768]{1,0:T(8,128)(2,1)S(1)}, bf16[32,128]{1,0:T(8,128)(2,1)S(1)}) custom-call(s32[4]{0:T(128)S(1)} %copy-done.14, bf16[128,768]{1,0:T(8,128)(2,1)S(1)} %copy-done.1, f32[128,768]{1,0:T(8,128)S(1)} %get-tuple-element.88.dmixed, bf16[4,128,768]{2,1,0:T(8,128)(2,1)S(1)} %get-tuple-element.89.d, ...), custom_call_target="tpu_custom_call" | custom-call | tf_op jit(solution)/shard_map/pallas_call | solution.py:39
  209.6 1.5 collective-permute-start.47
  214.1 2.8 %collective-permute-done.47.b = bf16[224,384]{1,0:T(8,128)(2,1)S(1)} collective-permute-done((bf16[224,384]{1,0:T(8,128)(2,1)S(1)}, bf16[224,384]{1,0:T(8,128)(2,1)S(1)}, u32[]{:S(2)}, u32[]{:S(2)}) %collective-permute-start.47) | collective-permute-done | bytes 172064 | tf_op jit(solution)/shard_map/ppermute | solution.py:428
  216.9 2.9 %collective-permute-done.48.c = bf16[224,384]{1,0:T(8,128)(2,1)S(1)} collective-permute-done((bf16[224,384]{1,0:T(8,128)(2,1)S(1)}, bf16[224,384]{1,0:T(8,128)(2,1)S(1)}, u32[]{:S(2)}, u32[]{:S(2)}) %collective-permute-start.48) | collective-permute-done | bytes 172064 | tf_op jit(solution)/shard_map/ppermute | solution.py:428
  220.4 1.8 collective-permute-start.50
  223.0 1.9 collective-permute-start.52
  225.0 5.5 %shard_map.255 = (f32[1,768,768]{2,1,0:T(8,128)}, f32[1,768,768]{2,1,0:T(8,128)}) custom-call(s32[4]{0:T(128)S(1)} %copy-done.14, bf16[4,160,768]{2,1,0:T(8,128)(2,1)S(1)} %get-tuple-element.68.hid, bf16[4,160,768]{2,1,0:T(8,128)(2,1)S(1)} %get-tuple-element.111.dpre, bf16[160,896]{1,0:T(8,128)(2,1)S(1)} %pad_maximum_fusion.x0, ...), custom_call_target="tpu_custom_call" | custom-call | tf_op jit(solution)/shard_map/pallas_call | solution.py:39
  231.1 4.4 %collective-permute-done.51.a2 = bf16[224,384]{1,0:T(8,128)(2,1)S(1)} collective-permute-done((bf16[224,384]{1,0:T(8,128)(2,1)S(1)}, bf16[224,384]{1,0:T(8,128)(2,1)S(1)}, u32[]{:S(2)}, u32[]{:S(2)}) %collective-permute-start.51) | collective-permute-done | bytes 172064 | tf_op jit(solution)/shard_map/ppermute | solution.py:428
  237.2 2.2 shard_map.254
  (151 shorter events, 49.0 us)
Async XLA Ops:
  8.4 17.4 %collective-permute-start = (bf16[416,768]{1,0:T(8,128)(2,1)S(1)}, bf16[416,768]{1,0:T(8,128)(2,1)S(1)}, u32[]{:S(2)}, u32[]{:S(2)}) collective-permute-start(bf16[416,768]{1,0:T(8,128)(2,1)S(1)} %shard_map.238.own), channel_id=1, source_target_pairs={{0,8},{8,0},{16,24},{24,16},{1,9},{9,1},{17,25},{25,17},{2,10},{10... | collective-permute-start | bytes 1916936 | tf_op jit(solution)/shard_map/ppermute | solution.py:428
  11.4 16.2 %collective-permute-start.1 = (bf16[416,768]{1,0:T(8,128)(2,1)S(1)}, bf16[416,768]{1,0:T(8,128)(2,1)S(1)}, u32[]{:S(2)}, u32[]{:S(2)}) collective-permute-start(bf16[416,768]{1,0:T(8,128)(2,1)S(1)} %shard_map.238.own), channel_id=1, source_target_pairs={{0,16},{8,24},{16,0},{24,8},{1,17},{9,25},{17,1},{25,9},{2,18},{10... | collective-permute-start | bytes 1916936 | tf_op jit(solution)/shard_map/ppermute | solution.py:428
  25.8 8.9 %collective-permute-start.2 = (bf16[208,768]{1,0:T(8,128)(2,1)S(1)}, bf16[208,768]{1,0:T(8,128)(2,1)}, u32[]{:S(2)}, u32[]{:S(2)}) collective-permute-start(bf16[208,768]{1,0:T(8,128)(2,1)S(1)} %slice.88), channel_id=1, source_target_pairs={{0,16},{8,24},{16,0},{24,8},{1,17},{9,25},{17,1},{25,9},{2,18},{10... | collective-permute-start | bytes 958472 | tf_op jit(solution)/shard_map/ppermute | solution.py:428
  27.7 8.3 %collective-permute-start.3 = (bf16[208,768]{1,0:T(8,128)(2,1)S(1)}, bf16[208,768]{1,0:T(8,128)(2,1)}, u32[]{:S(2)}, u32[]{:S(2)}) collective-permute-start(bf16[208,768]{1,0:T(8,128)(2,1)S(1)} %slice.89), channel_id=1, source_target_pairs={{0,8},{8,0},{16,24},{24,16},{1,9},{9,1},{17,25},{25,17},{2,10},{10... | collective-permute-start | bytes 958472 | tf_op jit(solution)/shard_map/ppermute | solution.py:428
  29.2 15.4 %collective-permute-start.4 = (bf16[416,768]{1,0:T(8,128)(2,1)S(1)}, bf16[416,768]{1,0:T(8,128)(2,1)}, u32[]{:S(2)}, u32[]{:S(2)}) collective-permute-start(bf16[416,768]{1,0:T(8,128)(2,1)S(1)} %collective-permute-done.hx), channel_id=1, source_target_pairs={{0,1},{1,0},{2,3},{3,2},{4,5},{5,4},{6,7},{7,6},{8,9},{9,8},{10,11... | collective-permute-start | bytes 1916936 | tf_op jit(solution)/shard_map/ppermute | solution.py:428
  29.2 15.4 %collective-permute-start.5 = (bf16[416,768]{1,0:T(8,128)(2,1)S(1)}, bf16[416,768]{1,0:T(8,128)(2,1)}, u32[]{:S(2)}, u32[]{:S(2)}) collective-permute-start(bf16[416,768]{1,0:T(8,128)(2,1)S(1)} %collective-permute-done.1.hy), channel_id=1, source_target_pairs={{0,1},{1,0},{2,3},{3,2},{4,5},{5,4},{6,7},{7,6},{8,9},{9,8},{10,11... | collective-permute-start | bytes 1916936 | tf_op jit(solution)/shard_map/ppermute | solution.py:428
  34.7 10.0 %collective-permute-start.6 = (bf16[208,768]{1,0:T(8,128)(2,1)}, bf16[208,768]{1,0:T(8,128)(2,1)}, u32[]{:S(2)}, u32[]{:S(2)}) collective-permute-start(bf16[208,768]{1,0:T(8,128)(2,1)} %collective-permute-done.2.da), channel_id=1, source_target_pairs={{0,1},{1,0},{2,3},{3,2},{4,5},{5,4},{6,7},{7,6},{8,9},{9,8},{10,11... | collective-permute-start | bytes 958472 | tf_op jit(solution)/shard_map/ppermute | solution.py:428
  36.0 8.7 %collective-permute-start.7 = (bf16[208,768]{1,0:T(8,128)(2,1)}, bf16[208,768]{1,0:T(8,128)(2,1)}, u32[]{:S(2)}, u32[]{:S(2)}) collective-permute-start(bf16[208,768]{1,0:T(8,128)(2,1)} %collective-permute-done.3.db), channel_id=1, source_target_pairs={{0,1},{1,0},{2,3},{3,2},{4,5},{5,4},{6,7},{7,6},{8,9},{9,8},{10,11... | collective-permute-start | bytes 958472 | tf_op jit(solution)/shard_map/ppermute | solution.py:428
  53.5 11.3 %collective-permute-start.16 = (bf16[128,896]{1,0:T(8,128)(2,1)S(1)}, bf16[128,896]{1,0:T(8,128)(2,1)S(1)}, u32[]{:S(2)}, u32[]{:S(2)}) collective-permute-start(bf16[128,896]{1,0:T(8,128)(2,1)S(1)} %get-tuple-element.67.own), channel_id=1, source_target_pairs={{0,1},{1,0},{2,3},{3,2},{4,5},{5,4},{6,7},{7,6},{8,9},{9,8},{10,11... | collective-permute-start | bytes 688136 | tf_op jit(solution)/shard_map/ppermute | solution.py:428
  53.9 6.2 %collective-permute-start.12 = (bf16[40,768]{1,0:T(8,128)(2,1)S(1)}, bf16[40,768]{1,0:T(8,128)(2,1)S(1)}, u32[]{:S(2)}, u32[]{:S(2)}) collective-permute-start(bf16[40,768]{1,0:T(8,128)(2,1)S(1)} %get-tuple-element.139), channel_id=1, source_target_pairs={{0,6},{1,7},{2,4},{3,5},{4,2},{5,3},{6,0},{7,1},{8,14},{9,15},{10,... | collective-permute-start | bytes 184328 | tf_op jit(solution)/shard_map/ppermute | solution.py:428
  63.2 16.1 %collective-permute-start.13 = (bf16[160,768]{1,0:T(8,128)(2,1)S(1)}, bf16[160,768]{1,0:T(8,128)(2,1)S(1)}, u32[]{:S(2)}, u32[]{:S(2)}) collective-permute-start(bf16[160,768]{1,0:T(8,128)(2,1)S(1)} %pad_maximum_fusion.2.refs_0_.g0), channel_id=1, source_target_pairs={{0,8},{8,0},{16,24},{24,16},{1,9},{9,1},{17,25},{25,17},{2,10},{10... | collective-permute-start | bytes 737288 | tf_op jit(solution)/shard_map/ppermute | solution.py:428
  65.6 6.9 %collective-permute-start.19 = (bf16[40,896]{1,0:T(8,128)(2,1)S(1)}, bf16[40,896]{1,0:T(8,128)(2,1)S(1)}, u32[]{:S(2)}, u32[]{:S(2)}) collective-permute-start(bf16[40,896]{1,0:T(8,128)(2,1)S(1)} %get-tuple-element.131), channel_id=1, source_target_pairs={{0,6},{1,7},{2,4},{3,5},{4,2},{5,3},{6,0},{7,1},{8,14},{9,15},{10,... | collective-permute-start | bytes 215048 | tf_op jit(solution)/shard_map/ppermute | solution.py:428
  68.1 6.9 %collective-permute-start.18 = (bf16[40,896]{1,0:T(8,128)(2,1)S(1)}, bf16[40,896]{1,0:T(8,128)(2,1)S(1)}, u32[]{:S(2)}, u32[]{:S(2)}) collective-permute-start(bf16[40,896]{1,0:T(8,128)(2,1)S(1)} %get-tuple-element.132), channel_id=1, source_target_pairs={{0,4},{1,5},{2,6},{3,7},{4,0},{5,1},{6,2},{7,3},{8,12},{9,13},{10,... | collective-permute-start | bytes 215048 | tf_op jit(solution)/shard_map/ppermute | solution.py:428
  68.3 6.7 %collective-permute-start.17 = (bf16[40,896]{1,0:T(8,128)(2,1)S(1)}, bf16[40,896]{1,0:T(8,128)(2,1)S(1)}, u32[]{:S(2)}, u32[]{:S(2)}) collective-permute-start(bf16[40,896]{1,0:T(8,128)(2,1)S(1)} %get-tuple-element.133), channel_id=1, source_target_pairs={{0,2},{1,3},{2,0},{3,1},{4,6},{5,7},{6,4},{7,5},{8,10},{9,11},{10,... | collective-permute-start | bytes 215048 | tf_op jit(solution)/shard_map/ppermute | solution.py:428
  75.1 27.4 %collective-permute-start.20 = (bf16[160,896]{1,0:T(8,128)(2,1)S(1)}, bf16[160,896]{1,0:T(8,128)(2,1)S(1)}, u32[]{:S(2)}, u32[]{:S(2)}) collective-permute-start(bf16[160,896]{1,0:T(8,128)(2,1)S(1)} %pad_maximum_fusion.x0), channel_id=1, source_target_pairs={{0,8},{8,0},{16,24},{24,16},{1,9},{9,1},{17,25},{25,17},{2,10},{10... | collective-permute-start | bytes 860168 | tf_op jit(solution)/shard_map/ppermute | solution.py:428
  75.7 26.8 %collective-permute-start.21 = (bf16[160,896]{1,0:T(8,128)(2,1)S(1)}, bf16[160,896]{1,0:T(8,128)(2,1)S(1)}, u32[]{:S(2)}, u32[]{:S(2)}) collective-permute-start(bf16[160,896]{1,0:T(8,128)(2,1)S(1)} %pad_maximum_fusion.x0), channel_id=1, source_target_pairs={{0,16},{8,24},{16,0},{24,8},{1,17},{9,25},{17,1},{25,9},{2,18},{10... | collective-permute-start | bytes 860168 | tf_op jit(solution)/shard_map/ppermute | solution.py:428
  76.8 25.7 %collective-permute-start.22 = (bf16[160,896]{1,0:T(8,128)(2,1)S(1)}, bf16[160,896]{1,0:T(8,128)(2,1)S(1)}, u32[]{:S(2)}, u32[]{:S(2)}) collective-permute-start(bf16[160,896]{1,0:T(8,128)(2,1)S(1)} %pad_maximum_fusion.x0), channel_id=1, source_target_pairs={{0,24},{8,16},{16,8},{24,0},{1,25},{9,17},{17,9},{25,1},{2,26},{10... | collective-permute-start | bytes 860168 | tf_op jit(solution)/shard_map/ppermute | solution.py:428
  78.6 21.6 %collective-permute-start.14 = (bf16[160,768]{1,0:T(8,128)(2,1)S(1)}, bf16[160,768]{1,0:T(8,128)(2,1)S(1)}, u32[]{:S(2)}, u32[]{:S(2)}) collective-permute-start(bf16[160,768]{1,0:T(8,128)(2,1)S(1)} %pad_maximum_fusion.2.refs_0_.g0), channel_id=1, source_target_pairs={{0,16},{8,24},{16,0},{24,8},{1,17},{9,25},{17,1},{25,9},{2,18},{10... | collective-permute-start | bytes 737288 | tf_op jit(solution)/shard_map/ppermute | solution.py:428
  79.3 20.9 %collective-permute-start.15 = (bf16[160,768]{1,0:T(8,128)(2,1)S(1)}, bf16[160,768]{1,0:T(8,128)(2,1)S(1)}, u32[]{:S(2)}, u32[]{:S(2)}) collective-permute-start(bf16[160,768]{1,0:T(8,128)(2,1)S(1)} %pad_maximum_fusion.2.refs_0_.g0), channel_id=1, source_target_pairs={{0,24},{8,16},{16,8},{24,0},{1,25},{9,17},{17,9},{25,1},{2,26},{10... | collective-permute-start | bytes 737288 | tf_op jit(solution)/shard_map/ppermute | solution.py:428
  106.3 9.8 %collective-permute-start.30 = (bf16[160,896]{1,0:T(8,128)(2,1)S(1)}, bf16[160,896]{1,0:T(8,128)(2,1)S(1)}, u32[]{:S(2)}, u32[]{:S(2)}) collective-permute-start(bf16[160,896]{1,0:T(8,128)(2,1)S(1)} %get-tuple-element.76), channel_id=1, source_target_pairs={{0,8},{8,0},{16,24},{24,16},{1,9},{9,1},{17,25},{25,17},{2,10},{10... | collective-permute-start | bytes 860168 | tf_op jit(solution)/shard_map/ppermute | solution.py:428
  107.8 12.8 %collective-permute-start.31 = (bf16[160,896]{1,0:T(8,128)(2,1)S(1)}, bf16[160,896]{1,0:T(8,128)(2,1)S(1)}, u32[]{:S(2)}, u32[]{:S(2)}) collective-permute-start(bf16[160,896]{1,0:T(8,128)(2,1)S(1)} %get-tuple-element.77), channel_id=1, source_target_pairs={{0,16},{8,24},{16,0},{24,8},{1,17},{9,25},{17,1},{25,9},{2,18},{10... | collective-permute-start | bytes 860168 | tf_op jit(solution)/shard_map/ppermute | solution.py:428
  108.5 12.2 %collective-permute-start.32 = (bf16[160,896]{1,0:T(8,128)(2,1)S(1)}, bf16[160,896]{1,0:T(8,128)(2,1)S(1)}, u32[]{:S(2)}, u32[]{:S(2)}) collective-permute-start(bf16[160,896]{1,0:T(8,128)(2,1)S(1)} %get-tuple-element.78), channel_id=1, source_target_pairs={{0,24},{8,16},{16,8},{24,0},{1,25},{9,17},{17,9},{25,1},{2,26},{10... | collective-permute-start | bytes 860168 | tf_op jit(solution)/shard_map/ppermute | solution.py:428
  121.4 6.2 %collective-permute-start.35 = (bf16[40,896]{1,0:T(8,128)(2,1)S(1)}, bf16[40,896]{1,0:T(8,128)(2,1)S(1)}, u32[]{:S(2)}, u32[]{:S(2)}) collective-permute-start(bf16[40,896]{1,0:T(8,128)(2,1)S(1)} %get-tuple-element.127), channel_id=1, source_target_pairs={{0,6},{1,7},{2,4},{3,5},{4,2},{5,3},{6,0},{7,1},{8,14},{9,15},{10,... | collective-permute-start | bytes 215048 | tf_op jit(solution)/shard_map/ppermute | solution.py:428
  130.1 12.2 %collective-permute-start.37 = (bf16[128,768]{1,0:T(8,128)(2,1)S(1)}, bf16[128,768]{1,0:T(8,128)(2,1)S(1)}, u32[]{:S(2)}, u32[]{:S(2)}) collective-permute-start(bf16[128,768]{1,0:T(8,128)(2,1)S(1)} %copy-done.1), channel_id=1, source_target_pairs={{0,2},{1,3},{2,0},{3,1},{4,6},{5,7},{6,4},{7,5},{8,10},{9,11},{10,... | collective-permute-start | bytes 589832 | tf_op jit(solution)/shard_map/ppermute | solution.py:428
  131.2 17.2 %collective-permute-start.38 = (bf16[128,768]{1,0:T(8,128)(2,1)S(1)}, bf16[128,768]{1,0:T(8,128)(2,1)S(1)}, u32[]{:S(2)}, u32[]{:S(2)}) collective-permute-start(bf16[128,768]{1,0:T(8,128)(2,1)S(1)} %copy-done.1), channel_id=1, source_target_pairs={{0,4},{1,5},{2,6},{3,7},{4,0},{5,1},{6,2},{7,3},{8,12},{9,13},{10,... | collective-permute-start | bytes 589832 | tf_op jit(solution)/shard_map/ppermute | solution.py:428
  132.7 15.7 %collective-permute-start.39 = (bf16[128,768]{1,0:T(8,128)(2,1)S(1)}, bf16[128,768]{1,0:T(8,128)(2,1)S(1)}, u32[]{:S(2)}, u32[]{:S(2)}) collective-permute-start(bf16[128,768]{1,0:T(8,128)(2,1)S(1)} %copy-done.1), channel_id=1, source_target_pairs={{0,6},{1,7},{2,4},{3,5},{4,2},{5,3},{6,0},{7,1},{8,14},{9,15},{10,... | collective-permute-start | bytes 589832 | tf_op jit(solution)/shard_map/ppermute | solution.py:428
  134.5 27.5 %collective-permute-start.40 = (bf16[128,768]{1,0:T(8,128)(2,1)S(1)}, bf16[128,768]{1,0:T(8,128)(2,1)S(1)}, u32[]{:S(2)}, u32[]{:S(2)}) collective-permute-start(bf16[128,768]{1,0:T(8,128)(2,1)S(1)} %get-tuple-element.87.ctx.c0), channel_id=1, source_target_pairs={{0,2},{1,3},{2,0},{3,1},{4,6},{5,7},{6,4},{7,5},{8,10},{9,11},{10,... | collective-permute-start | bytes 589832 | tf_op jit(solution)/shard_map/ppermute | solution.py:428
  134.7 38.9 %collective-permute-start.41 = (bf16[128,768]{1,0:T(8,128)(2,1)S(1)}, bf16[128,768]{1,0:T(8,128)(2,1)S(1)}, u32[]{:S(2)}, u32[]{:S(2)}) collective-permute-start(bf16[128,768]{1,0:T(8,128)(2,1)S(1)} %get-tuple-element.87.ctx.c0), channel_id=1, source_target_pairs={{0,4},{1,5},{2,6},{3,7},{4,0},{5,1},{6,2},{7,3},{8,12},{9,13},{10,... | collective-permute-start | bytes 589832 | tf_op jit(solution)/shard_map/ppermute | solution.py:428
  142.3 31.3 %collective-permute-start.42 = (bf16[128,768]{1,0:T(8,128)(2,1)S(1)}, bf16[128,768]{1,0:T(8,128)(2,1)S(1)}, u32[]{:S(2)}, u32[]{:S(2)}) collective-permute-start(bf16[128,768]{1,0:T(8,128)(2,1)S(1)} %get-tuple-element.87.ctx.c0), channel_id=1, source_target_pairs={{0,6},{1,7},{2,4},{3,5},{4,2},{5,3},{6,0},{7,1},{8,14},{9,15},{10,... | collective-permute-start | bytes 589832 | tf_op jit(solution)/shard_map/ppermute | solution.py:428
  148.4 25.3 %collective-permute-start.43 = (bf16[128,768]{1,0:T(8,128)(2,1)S(1)}, bf16[128,768]{1,0:T(8,128)(2,1)S(1)}, u32[]{:S(2)}, u32[]{:S(2)}) collective-permute-start(bf16[128,768]{1,0:T(8,128)(2,1)S(1)} %get-tuple-element.95), channel_id=1, source_target_pairs={{0,2},{1,3},{2,0},{3,1},{4,6},{5,7},{6,4},{7,5},{8,10},{9,11},{10,... | collective-permute-start | bytes 589832 | tf_op jit(solution)/shard_map/ppermute | solution.py:428
  148.4 33.7 %collective-permute-start.44 = (bf16[128,768]{1,0:T(8,128)(2,1)S(1)}, bf16[128,768]{1,0:T(8,128)(2,1)S(1)}, u32[]{:S(2)}, u32[]{:S(2)}) collective-permute-start(bf16[128,768]{1,0:T(8,128)(2,1)S(1)} %get-tuple-element.96), channel_id=1, source_target_pairs={{0,4},{1,5},{2,6},{3,7},{4,0},{5,1},{6,2},{7,3},{8,12},{9,13},{10,... | collective-permute-start | bytes 589832 | tf_op jit(solution)/shard_map/ppermute | solution.py:428
  162.0 20.0 %collective-permute-start.45 = (bf16[128,768]{1,0:T(8,128)(2,1)S(1)}, bf16[128,768]{1,0:T(8,128)(2,1)S(1)}, u32[]{:S(2)}, u32[]{:S(2)}) collective-permute-start(bf16[128,768]{1,0:T(8,128)(2,1)S(1)} %get-tuple-element.97), channel_id=1, source_target_pairs={{0,6},{1,7},{2,4},{3,5},{4,2},{5,3},{6,0},{7,1},{8,14},{9,15},{10,... | collective-permute-start | bytes 589832 | tf_op jit(solution)/shard_map/ppermute | solution.py:428
  183.9 24.5 %collective-permute-start.46 = (bf16[768,384]{1,0:T(8,128)(2,1)S(1)}, bf16[768,384]{1,0:T(8,128)(2,1)S(1)}, u32[]{:S(2)}, u32[]{:S(2)}) collective-permute-start(bf16[768,384]{1,0:T(8,128)(2,1)S(1)} %get-tuple-element.99), channel_id=1, source_target_pairs={{0,1},{1,0},{2,3},{3,2},{4,5},{5,4},{6,7},{7,6},{8,9},{9,8},{10,11... | collective-permute-start | bytes 1769480 | tf_op jit(solution)/shard_map/ppermute | solution.py:428
  185.5 8.8 %collective-permute-start.23 = (bf16[160,768]{1,0:T(8,128)(2,1)S(1)}, bf16[160,768]{1,0:T(8,128)(2,1)S(1)}, u32[]{:S(2)}, u32[]{:S(2)}) collective-permute-start(bf16[160,768]{1,0:T(8,128)(2,1)S(1)} %get-tuple-element.70), channel_id=1, source_target_pairs={{0,8},{8,0},{16,24},{24,16},{1,9},{9,1},{17,25},{25,17},{2,10},{10... | collective-permute-start | bytes 737288 | tf_op jit(solution)/shard_map/ppermute | solution.py:428
  186.1 13.3 %collective-permute-start.24 = (bf16[160,768]{1,0:T(8,128)(2,1)S(1)}, bf16[160,768]{1,0:T(8,128)(2,1)S(1)}, u32[]{:S(2)}, u32[]{:S(2)}) collective-permute-start(bf16[160,768]{1,0:T(8,128)(2,1)S(1)} %get-tuple-element.71), channel_id=1, source_target_pairs={{0,16},{8,24},{16,0},{24,8},{1,17},{9,25},{17,1},{25,9},{2,18},{10... | collective-permute-start | bytes 737288 | tf_op jit(solution)/shard_map/ppermute | solution.py:428
  187.3 12.2 %collective-permute-start.25 = (bf16[160,768]{1,0:T(8,128)(2,1)S(1)}, bf16[160,768]{1,0:T(8,128)(2,1)S(1)}, u32[]{:S(2)}, u32[]{:S(2)}) collective-permute-start(bf16[160,768]{1,0:T(8,128)(2,1)S(1)} %get-tuple-element.72), channel_id=1, source_target_pairs={{0,24},{8,16},{16,8},{24,0},{1,25},{9,17},{17,9},{25,1},{2,26},{10... | collective-permute-start | bytes 737288 | tf_op jit(solution)/shard_map/ppermute | solution.py:428
  200.1 11.6 %collective-permute-start.28 = (bf16[40,768]{1,0:T(8,128)(2,1)S(1)}, bf16[40,768]{1,0:T(8,128)(2,1)S(1)}, u32[]{:S(2)}, u32[]{:S(2)}) collective-permute-start(bf16[40,768]{1,0:T(8,128)(2,1)S(1)} %get-tuple-element.135), channel_id=1, source_target_pairs={{0,6},{1,7},{2,4},{3,5},{4,2},{5,3},{6,0},{7,1},{8,14},{9,15},{10,... | collective-permute-start | bytes 184328 | tf_op jit(solution)/shard_map/ppermute | solution.py:428
  201.8 11.3 %collective-permute-start.27 = (bf16[40,768]{1,0:T(8,128)(2,1)S(1)}, bf16[40,768]{1,0:T(8,128)(2,1)S(1)}, u32[]{:S(2)}, u32[]{:S(2)}) collective-permute-start(bf16[40,768]{1,0:T(8,128)(2,1)S(1)} %get-tuple-element.136), channel_id=1, source_target_pairs={{0,4},{1,5},{2,6},{3,7},{4,0},{5,1},{6,2},{7,3},{8,12},{9,13},{10,... | collective-permute-start | bytes 184328 | tf_op jit(solution)/shard_map/ppermute | solution.py:428
  205.6 7.5 %collective-permute-start.26 = (bf16[40,768]{1,0:T(8,128)(2,1)S(1)}, bf16[40,768]{1,0:T(8,128)(2,1)S(1)}, u32[]{:S(2)}, u32[]{:S(2)}) collective-permute-start(bf16[40,768]{1,0:T(8,128)(2,1)S(1)} %get-tuple-element.137), channel_id=1, source_target_pairs={{0,2},{1,3},{2,0},{3,1},{4,6},{5,7},{6,4},{7,5},{8,10},{9,11},{10,... | collective-permute-start | bytes 184328 | tf_op jit(solution)/shard_map/ppermute | solution.py:428
  209.6 7.3 %collective-permute-start.47 = (bf16[224,384]{1,0:T(8,128)(2,1)S(1)}, bf16[224,384]{1,0:T(8,128)(2,1)S(1)}, u32[]{:S(2)}, u32[]{:S(2)}) collective-permute-start(bf16[224,384]{1,0:T(8,128)(2,1)S(1)} %get-tuple-element.103), channel_id=1, source_target_pairs={{0,8},{8,0},{16,24},{24,16},{1,9},{9,1},{17,25},{25,17},{2,10},{10... | collective-permute-start | bytes 516104 | tf_op jit(solution)/shard_map/ppermute | solution.py:428
  211.1 8.7 %collective-permute-start.48 = (bf16[224,384]{1,0:T(8,128)(2,1)S(1)}, bf16[224,384]{1,0:T(8,128)(2,1)S(1)}, u32[]{:S(2)}, u32[]{:S(2)}) collective-permute-start(bf16[224,384]{1,0:T(8,128)(2,1)S(1)} %get-tuple-element.104), channel_id=1, source_target_pairs={{0,16},{8,24},{16,0},{24,8},{1,17},{9,25},{17,1},{25,9},{2,18},{10... | collective-permute-start | bytes 516104 | tf_op jit(solution)/shard_map/ppermute | solution.py:428
  211.7 8.0 %collective-permute-start.49 = (bf16[224,384]{1,0:T(8,128)(2,1)S(1)}, bf16[224,384]{1,0:T(8,128)(2,1)S(1)}, u32[]{:S(2)}, u32[]{:S(2)}) collective-permute-start(bf16[224,384]{1,0:T(8,128)(2,1)S(1)} %get-tuple-element.105), channel_id=1, source_target_pairs={{0,24},{8,16},{16,8},{24,0},{1,25},{9,17},{17,9},{25,1},{2,26},{10... | collective-permute-start | bytes 516104 | tf_op jit(solution)/shard_map/ppermute | solution.py:428
  214.0 22.0 %collective-permute-start.29 = (bf16[128,768]{1,0:T(8,128)(2,1)S(1)}, bf16[128,768]{1,0:T(8,128)(2,1)S(1)}, u32[]{:S(2)}, u32[]{:S(2)}) collective-permute-start(bf16[128,768]{1,0:T(8,128)(2,1)S(1)} %get-tuple-element.74), channel_id=1, source_target_pairs={{0,1},{1,0},{2,3},{3,2},{4,5},{5,4},{6,7},{7,6},{8,9},{9,8},{10,11... | collective-permute-start | bytes 589832 | tf_op jit(solution)/shard_map/ppermute | solution.py:428
  220.4 10.2 %collective-permute-start.50 = (bf16[224,384]{1,0:T(8,128)(2,1)S(1)}, bf16[224,384]{1,0:T(8,128)(2,1)S(1)}, u32[]{:S(2)}, u32[]{:S(2)}) collective-permute-start(bf16[224,384]{1,0:T(8,128)(2,1)S(1)} %shard_map.253.a0), channel_id=1, source_target_pairs={{0,2},{1,3},{2,0},{3,1},{4,6},{5,7},{6,4},{7,5},{8,10},{9,11},{10,... | collective-permute-start | bytes 516104 | tf_op jit(solution)/shard_map/ppermute | solution.py:428
  222.2 13.3 %collective-permute-start.51 = (bf16[224,384]{1,0:T(8,128)(2,1)S(1)}, bf16[224,384]{1,0:T(8,128)(2,1)S(1)}, u32[]{:S(2)}, u32[]{:S(2)}) collective-permute-start(bf16[224,384]{1,0:T(8,128)(2,1)S(1)} %shard_map.253.a0), channel_id=1, source_target_pairs={{0,4},{1,5},{2,6},{3,7},{4,0},{5,1},{6,2},{7,3},{8,12},{9,13},{10,... | collective-permute-start | bytes 516104 | tf_op jit(solution)/shard_map/ppermute | solution.py:428
  223.0 12.5 %collective-permute-start.52 = (bf16[224,384]{1,0:T(8,128)(2,1)S(1)}, bf16[224,384]{1,0:T(8,128)(2,1)S(1)}, u32[]{:S(2)}, u32[]{:S(2)}) collective-permute-start(bf16[224,384]{1,0:T(8,128)(2,1)S(1)} %shard_map.253.a0), channel_id=1, source_target_pairs={{0,6},{1,7},{2,4},{3,5},{4,2},{5,3},{6,0},{7,1},{8,14},{9,15},{10,... | collective-permute-start | bytes 516104 | tf_op jit(solution)/shard_map/ppermute | solution.py:428
  230.6 6.3 %collective-permute-start.53 = (bf16[224,384]{1,0:T(8,128)(2,1)S(1)}, bf16[224,384]{1,0:T(8,128)(2,1)S(1)}, u32[]{:S(2)}, u32[]{:S(2)}) collective-permute-start(bf16[224,384]{1,0:T(8,128)(2,1)S(1)} %shard_map.253.a0), channel_id=1, source_target_pairs={{0,1},{1,0},{2,3},{3,2},{4,5},{5,4},{6,7},{7,6},{8,9},{9,8},{10,11... | collective-permute-start | bytes 516104 | tf_op jit(solution)/shard_map/ppermute | solution.py:428
  230.6 6.2 %collective-permute-start.54 = (bf16[224,384]{1,0:T(8,128)(2,1)S(1)}, bf16[224,384]{1,0:T(8,128)(2,1)S(1)}, u32[]{:S(2)}, u32[]{:S(2)}) collective-permute-start(bf16[224,384]{1,0:T(8,128)(2,1)S(1)} %collective-permute-done.50.a1), channel_id=1, source_target_pairs={{0,1},{1,0},{2,3},{3,2},{4,5},{5,4},{6,7},{7,6},{8,9},{9,8},{10,11... | collective-permute-start | bytes 516104 | tf_op jit(solution)/shard_map/ppermute | solution.py:428
  (30 other events, 391.3 us)

commit v2 on v1

--- a/solution.py
+++ b/solution.py
@@ -35,9 +35,15 @@
     return lax.broadcasted_iota(i32, shape, dim)
 
 
-def call(body, outs, idx, *args, scratch=()):
+def after(value, *earlier):
+    return lax.optimization_barrier((value, *earlier))[0]
+
+
+def call(name, micros, body, outs, idx, *args, scratch=()):
     return pl.pallas_call(
         body,
+        name=name,
+        cost_estimate=pl.CostEstimate(flops=int(micros * 1.1e9), bytes_accessed=int(micros * 1e6), transcendentals=0),
         out_shape=[jax.ShapeDtypeStruct(s, d) for s, d in outs],
         in_specs=[pl.BlockSpec(memory_space=pltpu.SMEM)]
         + [pl.BlockSpec(memory_space=pltpu.VMEM)] * len(args),
@@ -66,34 +72,22 @@
     return (bucket == iota((rows, 2 * length), 0)).astype(f32).astype(bf16)
 
 
-def pack_body(experts, smalls, idx, wq, wk, wv, wo, wr, g1, g2, tab, out):
-    rows, width = wq.shape
-    core = idx[2]
-
-    @pl.when(core == 0)
-    def _():
-        out[0:rows, :] = wq[...]
-        out[rows : 2 * rows, :] = wv[...]
-
-    @pl.when(core == 1)
-    def _():
-        out[0:rows, :] = wk[...]
-        out[rows : 2 * rows, :] = wo[...]
-
-    heads = tab.shape[1]
+def pack_body(experts, smalls, idx, wr_t, g1, g2, tab, out):
+    rows = wr_t.shape[1]
+    heads, shard = tab.shape[1], tab.shape[0]
     pick = (iota((smalls, experts), 0) == iota((smalls, experts), 1)).astype(f32).astype(bf16)
-    part = nt(pick, wr[...])
+    part = nn(pick, wr_t[...])
     line = iota((smalls, rows), 0)
     part = part + jnp.where(line == experts, g1[...].astype(f32), 0.0)
     part = part + jnp.where(line == experts + 1, g2[...].astype(f32), 0.0)
+    width = out.shape[1]
     spread = (iota((rows, width), 0) == iota((rows, width), 1)).astype(f32).astype(bf16)
     whole = nn(part.astype(bf16), spread)
     pick_t = (iota((smalls, heads), 0) == iota((smalls, heads), 1) + experts + 2).astype(f32)
     table_t = nt(pick_t.astype(bf16), tab[...])
-    shard = tab.shape[0]
     spread_t = (iota((shard, width), 0) + rows == iota((shard, width), 1)).astype(f32)
     whole = whole + nn(table_t.astype(bf16), spread_t.astype(bf16))
-    out[2 * rows : 2 * rows + smalls, :] = whole.astype(bf16)
+    out[...] = whole.astype(bf16)
 
 
 def place_body(experts, idx, consts, routes2, cot, cot_t, place, rows_out):
@@ -133,8 +127,8 @@
 
 def attend_body(
     experts, smalls, heads, idx,
-    tokens, seg_c, seg_r, routes_c, wq, wk, wv, wo, own, hx, hy, da, db, tx, ty, ta, tb,
-    w_all, small_all, q_o, k_o, v_o, probs_o, ctx_o, mixed_o, hcat_o, rp_o,
+    tokens, seg_c, seg_r, routes_c, wq, wk, wv, wo, s0, s1, hx, hy, da, db, tx, ty, ta, tb,
+    w_all, small_all, q_o, k_o, v_o, probs_o, ctx_o, mixed_o, hcat_o, rp_o, *left,
 ):
     mine, core = idx[0], idx[2]
     rows, width = wq.shape
@@ -147,16 +141,14 @@
         at = pl.multiple_of((mine ^ k) * rows, 64)
         w_all[held, pl.ds(at, rows), :] = piece[0:rows, :]
         w_all[2 + held, pl.ds(at, rows), :] = piece[rows : 2 * rows, :]
-    cut = da.shape[0]
     at = pl.multiple_of((mine ^ 3) * rows, 64)
     for first, second, held in ((da, db, core), (ta, tb, 1 - core)):
         w_all[held, pl.ds(at, rows), :] = first[0:rows, :]
-        w_all[2 + held, pl.ds(at, cut - rows), :] = first[rows:cut, :]
-        w_all[2 + held, pl.ds(at + (cut - rows), 2 * rows - cut), :] = second[0 : 2 * rows - cut, :]
+        w_all[2 + held, pl.ds(at, rows), :] = second[...]
     small = jnp.zeros((smalls, width), f32)
     table_t = jnp.zeros((smalls, 128), f32)
     shard = 32 // 4
-    for k, piece, start in ((0, own, 2 * rows), (1, hx, 2 * rows), (2, hy, 2 * rows), (3, db, 2 * rows - cut)):
+    for k, piece, start in ((0, s0, 0), (1, s1, 0), (2, da, rows), (3, da, rows + smalls)):
         j = mine ^ k
         part = piece[start : start + smalls, 0:256]
         r, c = iota((256, width), 0), iota((256, width), 1)
@@ -207,6 +199,15 @@
     lane = iota((length, 128), 1)
     tail = jnp.where(lane == 0, high, jnp.where(lane == 1, gate - high, 0.0))
     hcat_o[:, width : width + 128] = tail.astype(bf16)
+    for zr, item in enumerate(left):
+
+        @pl.when((idx[3] ^ zr) == owner_of[3])
+        def _():
+            item[...] = ctx_o[...]
+
+        @pl.when((idx[3] ^ zr) != owner_of[3])
+        def _():
+            item[...] = tokens[...]
 
 
 def back_in_body(idx, w_out, *refs):
@@ -342,14 +343,14 @@
     table_o[...] = nn(pick_t.astype(bf16), table[...].astype(bf16)).astype(bf16)
 
 
-def mixer_grad_body(experts, idx, small_all, l0, l1, l2, l3, c0, c1, c2, c3, d0, d1, d2, d3, keep, send, acc, left):
+def mixer_grad_body(experts, idx, small_all, l0, l1, l2, l3, d0, d1, d2, d3, keep, send, acc, left):
     z, core = idx[3], idx[2]
     gain1 = small_all[experts : experts + 1, :]
     rows = l0.shape[0]
 
     @pl.when(z == owner_of[3])
     def _():
-        for n, c in enumerate((c0, c1, c2, c3)):
+        for n, c in enumerate((l0, l1, l2, l3)):
             left[n * rows : (n + 1) * rows, :] = c[...]
 
     @pl.when(z != owner_of[3])
@@ -441,18 +442,22 @@
     idx = jnp.stack([mine, me, me % 2, me // 2]).astype(i32)
     weight_in, weight_out = w_expert_in[0], w_expert_out[0]
 
-    parcel = call(
-        partial(pack_body, experts, smalls), [((2 * rows + smalls, width), bf16)], idx,
-        w_query, w_key, w_value, w_attn_out, w_router, norm1_gain[None], norm2_gain[None], bias_table,
-    )[0]
-    cut = (2 * rows + smalls) // 2
+    first = me % 2 == 0
+    parcel = jnp.concatenate(
+        [jnp.where(first, w_query, w_key), jnp.where(first, w_value, w_attn_out)], axis=0
+    )
     hx = along(parcel, "dp", 1)
     hy = along(parcel, "dp", 2)
-    da = along(hx[0:cut], "dp", 2)
-    db = along(hy[cut:], "dp", 1)
-    tx, ty, ta, tb = twin(hx), twin(hy), twin(da), twin(db)
-
-    route_row = routes.reshape(1, length)
+
+    wr_t, gain_a, gain_b, tab, cot, route_c, seg = lax.optimization_barrier(
+        (w_router.T, norm1_gain, norm2_gain, bias_table, cotangent, routes, segments, parcel)
+    )[:-1]
+    small_own = call(
+        "pack", 1, partial(pack_body, experts, smalls), [((smalls, width), bf16)], idx,
+        wr_t, gain_a[None], gain_b[None], tab,
+    )[0]
+    small_x = along(small_own, "dp", 1)
+    route_row = route_c.reshape(1, length)
     routes2 = jnp.concatenate([route_row, twin(route_row.astype(f32)).astype(i32)], axis=1)
     r = np.arange(slots)
     consts = np.zeros((slots, 128), np.int32)
@@ -460,41 +465,62 @@
     consts[:, 1] = (r // cap) % 2
     consts[:, 2] = r % cap
     place, g_rows = call(
-        partial(place_body, experts), [((slots, 2 * length), bf16), ((slots, width), bf16)], idx,
-        jnp.asarray(consts), routes2, cotangent, twin(cotangent),
-    )
+        "place_cot", 1.5, partial(place_body, experts),
+        [((slots, 2 * length), bf16), ((slots, width), bf16)], idx,
+        jnp.asarray(consts), routes2, cot, twin(cot),
+    )
+    seg_c, seg_r = seg.reshape(length, 1), seg.reshape(1, length)
     g_here = chip_exchange(g_rows)
+    hx, hy, place, g_here, seg_c, seg_r, route_c, small_own, small_x = lax.optimization_barrier(
+        (hx, hy, place, g_here, seg_c, seg_r, route_c, small_own, small_x)
+    )
+    da = along(jnp.concatenate([hx[0:rows], small_own, small_x], axis=0), "dp", 2)
+    db = along(hy[rows:], "dp", 1)
+    tx, ty = twin(hx), twin(hy)
+    ta, tb = twin(da), twin(db)
+    g_here = after(g_here, da, db)
     g_set = [g_here] + [along(g_here, "dp", k) for k in (1, 2, 3)]
-    g_back = call(back_in_body, [((4, slots, width), f32)], idx, weight_out, *g_set)[0]
-
-    if chips == 4:
-        tok_all = [tokens] + [along(tokens, "expert", 2 * zr) for zr in range(1, 4)]
-
-    w_all, small_all, q, k, v, probs, ctx, mixed, hcat, rp = call(
-        partial(attend_body, experts, smalls, heads),
+    g_back = call("g_back", 2, back_in_body, [((4, slots, width), f32)], idx, weight_out, *g_set)[0]
+
+    w_all, small_all, q, k, v, probs, ctx, mixed, hcat, rp, *left = call(
+        "attend", 7, partial(attend_body, experts, smalls, heads),
         [
             ((4, width, width), bf16), ((smalls, width), f32),
             ((length, width), bf16), ((length, width), bf16), ((length, width), bf16),
             ((heads, length, length), f32), ((length, width), bf16), ((length, width), f32),
             ((length, wide), bf16), ((length, experts), f32),
-        ],
-        idx, tokens, segments.reshape(length, 1), segments.reshape(1, length), routes,
-        w_query, w_key, w_value, w_attn_out, parcel, hx, hy, da, db, tx, ty, ta, tb,
-    )
-
-    x_rows = call(place_rows_body, [((slots, wide), bf16)], idx, place, hcat, twin(hcat))[0]
+        ]
+        + ([((length, width), bf16)] * 4 if chips == 4 else []),
+        idx, tokens, seg_c, seg_r, route_c,
+        w_query, w_key, w_value, w_attn_out, small_own, small_x, hx, hy, da, db, tx, ty, ta, tb,
+    )
+
+    x_rows = call("place_x", 1, place_rows_body, [((slots, wide), bf16)], idx, place, hcat, twin(hcat))[0]
     x_here = chip_exchange(x_rows)
+    x_here = after(x_here, *g_set)
     x_set = [x_here] + [along(x_here, "dp", kk) for kk in (1, 2, 3)]
+    if chips == 4:
+        left = [left[0]] + [along(after(left[zr], x_here), "expert", 2 * zr) for zr in range(1, 4)]
+        x_set[3] = after(x_set[3], left[1])
     *d_parts, hid, dpre = call(
-        expert_body,
+        "expert", 4, expert_body,
         [((slots, wide), bf16)] * 4 + [((4, slots, width), bf16)] * 2,
         idx, weight_in, g_back, *x_set,
     )
     d_got = [d_parts[0]] + [along(d_parts[kk], "dp", kk) for kk in (1, 2, 3)]
-    d_here = call(sum_body, [((slots, wide), bf16)], idx, *d_got)[0]
+    y_parts = call("expert_out", 1, expert_out_body, [((slots, width), bf16)] * 4, idx, weight_out, hid)
+    grad_in, grad_out = call(
+        "expert_grad", 5.5, expert_grad_body,
+        [((1, width, weight_in.shape[1]), f32), ((1, weight_out.shape[0], width), f32)], idx,
+        hid, dpre, *x_set, *g_set,
+    )
+    d_here = call("sum_d", 0.7, sum_body, [((slots, wide), bf16)], idx, *d_got)[0]
+    y_parts = list(lax.optimization_barrier((*y_parts, d_here))[:-1])
+    y_got = [y_parts[0]] + [along(y_parts[kk], "dp", kk) for kk in (1, 2, 3)]
     d_rows = chip_exchange(d_here)
+    place_d = after(place, *left) if chips == 4 else place
     back_own, back_other = call(
-        unplace_body, [((length, wide), f32), ((length, wide), bf16)], idx, place, d_rows
+        "unplace_d", 1, unplace_body, [((length, wide), f32), ((length, wide), bf16)], idx, place_d, d_rows
     )
     back_other = twin(back_other)
 
@@ -505,52 +531,49 @@
     if chips == 4:
         outs = outs + [((length, width), bf16)] * 4
     d_mixed, d_all, g_router, g_gain2, g_table, *turned = call(
-        partial(attend_back_body, experts, heads, chips), outs, idx,
-        back_own, back_other, mixed, cotangent, rp, routes, small_all, w_all, q, k, v, probs, ctx,
+        "attend_back", 5.5, partial(attend_back_body, experts, heads, chips), outs, idx,
+        back_own, back_other, mixed, cotangent, rp, route_c, small_all, w_all, q, k, v, probs, ctx,
         scratch=[pltpu.VMEM((16, 2 * length), f32)],
     )
+    d_in = [d_all]
+    if chips == 4:
+        d_in = [turned[0]] + [along(turned[zr], "expert", 2 * zr) for zr in range(1, 4)]
     d_tokens, small_g, table_g = call(
-        partial(token_grad_body, experts, smalls),
+        "token_grad", 3, partial(token_grad_body, experts, smalls),
         [((length, width), f32), ((smalls, width), bf16), ((smalls, 128), bf16)], idx,
         tokens, d_mixed, d_all, w_all, small_all, g_router, g_gain2, g_table,
     )
 
-    y_parts = call(expert_out_body, [((slots, width), bf16)] * 4, idx, weight_out, hid)
-    y_got = [y_parts[0]] + [along(y_parts[kk], "dp", kk) for kk in (1, 2, 3)]
-    y_here = call(sum_body, [((slots, width), bf16)], idx, *y_got)[0]
-    y_rows = chip_exchange(y_here)
-    y_own, y_other = call(
-        unplace_body, [((length, width), f32), ((length, width), bf16)], idx, place, y_rows
-    )
-    y_other = twin(y_other)
-    gate = jnp.sum(jnp.where(routes == jnp.arange(experts, dtype=i32)[None, :], rp, 0.0), axis=1, keepdims=True)
-    layer_out = (mixed + gate * (y_own + y_other.astype(f32))).astype(bf16)
-
-    grad_in, grad_out = call(
-        expert_grad_body,
-        [((1, width, weight_in.shape[1]), f32), ((1, weight_out.shape[0], width), f32)], idx,
-        hid, dpre, *x_set, *g_set,
-    )
-
+    y_got[0] = after(y_got[0], d_mixed)
+    y_here = call("sum_y", 0.7, sum_body, [((slots, width), bf16)], idx, *y_got)[0]
     if chips == 4:
-        ctx_all = [ctx] + [along(ctx, "expert", 2 * zr) for zr in range(1, 4)]
-        d_in = [turned[0]] + [along(turned[zr], "expert", 2 * zr) for zr in range(1, 4)]
+        small_s, d_in[1] = lax.optimization_barrier((small_all, d_in[1], small_g, y_here))[0:2]
         keep, send = call(
-            partial(mixer_grad_body, experts),
+            "mixer_grad", 2, partial(mixer_grad_body, experts),
             [((width, width // 2), f32), ((width, width // 2), bf16)], idx,
-            small_all, *tok_all, *ctx_all, *d_in,
+            small_s, *left, *d_in,
             scratch=[pltpu.VMEM((width, width), f32), pltpu.VMEM((4 * length, width), bf16)],
         )
         parts = call(
-            partial(share_body, shard), [((rows + smalls, width // 2), bf16)] * 4, idx,
+            "share", 1.2, partial(share_body, shard), [((rows + smalls, width // 2), bf16)] * 4, idx,
             keep, twin(send), small_g, table_g, scratch=[pltpu.VMEM((width, width // 2), f32)],
         )
         got = [parts[0]] + [along(parts[kk], "dp", kk) for kk in (1, 2, 3)]
-        total = call(sum_body, [((rows + smalls, width // 2), bf16)], idx, *got)[0]
+        total = call("sum_share", 0.7, sum_body, [((rows + smalls, width // 2), bf16)], idx, *got)[0]
+        y_here = after(y_here, total)
+    y_rows = chip_exchange(y_here)
+    y_own, y_other = call(
+        "unplace_y", 1, unplace_body, [((length, width), f32), ((length, width), bf16)], idx, place, y_rows
+    )
+    y_other = twin(y_other)
+    gate = jnp.sum(jnp.where(route_c == jnp.arange(experts, dtype=i32)[None, :], rp, 0.0), axis=1, keepdims=True)
+    layer_out = (mixed + gate * (y_own + y_other.astype(f32))).astype(bf16)
+
+    if chips == 4:
         a_set = [total] + [along(total, "expert", 2 * zr) for zr in range(1, 4)]
         b_set = [twin(a) for a in a_set]
         g_q, g_k, g_v, g_o, small_t = call(
-            finish_body, [((rows, width), f32)] * 4 + [((smalls, width // 2), f32)], idx, *a_set, *b_set
+            "finish", 2, finish_body, [((rows, width), f32)] * 4 + [((smalls, width // 2), f32)], idx, *a_set, *b_set
         )
         r_out = small_t[0:experts, 0:rows].T
         gain1_out = small_t[experts, 0:rows]
@@ -569,8 +592,8 @@
         rest = both[:, 4 * width :]
         r_out = rest[:, 0:experts]
         gain1_out, gain2_out = rest[:, experts], rest[:, experts + 1]
-        tab = table_g.T[0 : 4 * shard, experts + 2 : experts + 2 + heads].astype(f32)
-        table_out = lax.psum(lax.psum_scatter(tab, "dp", scatter_dimension=0, tiled=True), "expert")
+        tab_g = table_g.T[0 : 4 * shard, experts + 2 : experts + 2 + heads].astype(f32)
+        table_out = lax.psum(lax.psum_scatter(tab_g, "dp", scatter_dimension=0, tiled=True), "expert")
     return (
         layer_out, d_tokens, g_q, g_k, g_v, g_o, r_out, gain1_out, gain2_out, table_out, grad_in, grad_out,
     )

time: 242 us -> 184 us (0.76)
  waiting for transfers between devices: 107 us -> 80 us
  starting transfers between devices: 76.3 us -> 57.5 us
  local copies, waits for them, and re-layouts: 14.5 us -> 3.27 us
    ppermute x57 -> x55, waiting for transfers between devices: 107 us -> 80 us  [along(): return lax.ppermute(x, axis, [(s, s ^ mask) for s in range(n)])]
    ppermute x57 -> x55, starting transfers between devices: 76.3 us -> 57.5 us  [along(): return lax.ppermute(x, axis, [(s, s ^ mask) for s in range(n)])]
    unnamed x45 -> x35, local copies, waits for them, and re-layouts: 10.4 us -> 1.67 us
  transfers between devices with their start and end apart: 57 -> 55, of which waited for: 23 -> 28; matrix products, arithmetic and copies ran while one was open for 2% -> 1% of each run, Pallas kernels for 9% -> 11%
where the time goes in v2:
time: 184 us
  waiting for transfers between devices  80 us (43%)
  starting transfers between devices  57.5 us (31%)
  Pallas kernels  39.9 us (22%)
  local copies, waits for them, and re-layouts  3.27 us (2%)
  other arithmetic  2.43 us (1%)
    ppermute x55, waiting for transfers between devices, along(): return lax.ppermute(x, axis, [(s, s ^ mask) for s in range(n)])  80 us
    ppermute x55, starting transfers between devices, along(): return lax.ppermute(x, axis, [(s, s ^ mask) for s in range(n)])  57.5 us
    pallas_call x18, Pallas kernels, call(): pl.pallas_call(body, name=name, cost_estimate=pl.CostEstimate(flops=int(m...  39.9 us
  transfers between devices with their start and end apart: 55, of which 28 were waited for; matrix products, arithmetic and copies ran while one was open for 1% of the time, Pallas kernels for 11%

profile of v2, /device:TPU:0, one launch (start us, length us, event | category | flops | bytes accessed | tf_op | source)
XLA Modules:
  0.0 184.2 jit_solution(16703128705564713378)
XLA Ops:
  2.0 3.0 %collective-permute-start.1 = (bf16[384,768]{1,0:T(8,128)(2,1)S(1)}, bf16[384,768]{1,0:T(8,128)(2,1)S(1)}, u32[]{:S(2)}, u32[]{:S(2)}) collective-permute-start(bf16[384,768]{1,0:T(8,128)(2,1)S(1)} %pad_maximum_fusion), channel_id=1, source_target_pairs={{0,16},{8,24},{16,0},{24,8},{1,17},{9,25},{17,1},{25,9},{2,18},{10... | collective-permute-start | bytes 1769480 | tf_op jit(solution)/shard_map/ppermute | solution.py:429
  5.0 1.5 collective-permute-start
  9.1 3.7 %collective-permute-start.6 = (bf16[40,768]{1,0:T(8,128)(2,1)S(1)}, bf16[40,768]{1,0:T(8,128)(2,1)S(1)}, u32[]{:S(2)}, u32[]{:S(2)}) collective-permute-start(bf16[40,768]{1,0:T(8,128)(2,1)S(1)} %get-tuple-element.209), channel_id=1, source_target_pairs={{0,6},{1,7},{2,4},{3,5},{4,2},{5,3},{6,0},{7,1},{8,14},{9,15},{10,... | collective-permute-start | bytes 184328 | tf_op jit(solution)/shard_map/ppermute | solution.py:429
  16.0 2.4 %collective-permute-done.5 = bf16[40,768]{1,0:T(8,128)(2,1)S(1)} collective-permute-done((bf16[40,768]{1,0:T(8,128)(2,1)S(1)}, bf16[40,768]{1,0:T(8,128)(2,1)S(1)}, u32[]{:S(2)}, u32[]{:S(2)}) %collective-permute-start.5) | collective-permute-done | bytes 61472 | tf_op jit(solution)/shard_map/ppermute | solution.py:429
  18.5 2.4 %collective-permute-done.7.s1 = bf16[32,768]{1,0:T(8,128)(2,1)S(1)} collective-permute-done((bf16[32,768]{1,0:T(8,128)(2,1)S(1)}, bf16[32,768]{1,0:T(8,128)(2,1)S(1)}, u32[]{:S(2)}, u32[]{:S(2)}) %collective-permute-start.7) | collective-permute-done | bytes 49184 | tf_op jit(solution)/shard_map/ppermute | solution.py:429
  21.4 1.7 collective-permute-start.9
  23.6 7.2 %collective-permute-done.8.da = bf16[256,768]{1,0:T(8,128)(2,1)} collective-permute-done((bf16[256,768]{1,0:T(8,128)(2,1)S(1)}, bf16[256,768]{1,0:T(8,128)(2,1)}, u32[]{:S(2)}, u32[]{:S(2)}) %collective-permute-start.8) | collective-permute-done | bytes 393248 | tf_op jit(solution)/shard_map/ppermute | solution.py:429
  31.5 1.7 collective-permute-done.13.tb
  34.3 7.3 %attend.1 = (bf16[4,768,768]{2,1,0:T(8,128)(2,1)S(1)}, f32[32,768]{1,0:T(8,128)S(1)}, bf16[128,768]{1,0:T(8,128)(2,1)S(1)}, bf16[128,768]{1,0:T(8,128)(2,1)S(1)}...) custom-call(s32[4]{0:T(128)S(1)} %pad_add_fusion.1.idx, ...), custom_call_target="tpu_custom_call" | custom-call | flops 7699999744 | bytes 7000000 | tf_op jit(solution)/shard_map/attend/pallas_call | solution.py:43
  44.0 3.7 %collective-permute-start.20 = (bf16[40,896]{1,0:T(8,128)(2,1)S(1)}, bf16[40,896]{1,0:T(8,128)(2,1)S(1)}, u32[]{:S(2)}, u32[]{:S(2)}) collective-permute-start(bf16[40,896]{1,0:T(8,128)(2,1)S(1)} %get-tuple-element.201), channel_id=1, source_target_pairs={{0,6},{1,7},{2,4},{3,5},{4,2},{5,3},{6,0},{7,1},{8,14},{9,15},{10,... | collective-permute-start | bytes 215048 | tf_op jit(solution)/shard_map/ppermute | solution.py:429
  47.7 1.4 collective-permute-start.16
  49.1 1.5 collective-permute-start.15
  52.0 4.6 %collective-permute-done.19 = bf16[40,896]{1,0:T(8,128)(2,1)S(1)} collective-permute-done((bf16[40,896]{1,0:T(8,128)(2,1)S(1)}, bf16[40,896]{1,0:T(8,128)(2,1)S(1)}, u32[]{:S(2)}, u32[]{:S(2)}) %collective-permute-start.19) | collective-permute-done | bytes 71712 | tf_op jit(solution)/shard_map/ppermute | solution.py:429
  57.5 4.1 %collective-permute-done.15.refs_2_.g2 = bf16[160,768]{1,0:T(8,128)(2,1)S(1)} collective-permute-done((bf16[160,768]{1,0:T(8,128)(2,1)S(1)}, bf16[160,768]{1,0:T(8,128)(2,1)S(1)}, u32[]{:S(2)}, u32[]{:S(2)}) %collective-permute-start.15) | collective-permute-done | bytes 245792 | tf_op jit(solution)/shard_map/ppermute | solution.py:429
  61.6 1.5 collective-permute-start.23
  65.1 2.2 %g_back.1.g_all = f32[4,160,768]{2,1,0:T(8,128)S(1)} custom-call(s32[4]{0:T(128)S(1)} %pad_add_fusion.1.idx, bf16[768,768]{1,0:T(8,128)(2,1)S(1)} %bitcast.21, bf16[160,768]{1,0:T(8,128)(2,1)S(1)} %pad_maximum_fusion.4.refs_0_.g0, bf16[160,768]{1,0:T(8,128)(2,1)S(1)} %collective-permute-done.14.refs_1_.g1, ...), custom_call_target="tpu_custom_call" | custom-call | flops 2200000000 | bytes 2000000 | tf_op jit(solution)/shard_map/g_back/pallas_call | solution.py:43
  67.3 3.8 %collective-permute-done.24.l1 = bf16[128,768]{1,0:T(8,128)(2,1)S(1)} collective-permute-done((bf16[128,768]{1,0:T(8,128)(2,1)S(1)}, bf16[128,768]{1,0:T(8,128)(2,1)S(1)}, u32[]{:S(2)}, u32[]{:S(2)}) %collective-permute-start.24) | collective-permute-done | bytes 196640 | tf_op jit(solution)/shard_map/ppermute | solution.py:429
  72.2 5.2 %collective-permute-done.22.x2 = bf16[160,896]{1,0:T(8,128)(2,1)S(1)} collective-permute-done((bf16[160,896]{1,0:T(8,128)(2,1)S(1)}, bf16[160,896]{1,0:T(8,128)(2,1)S(1)}, u32[]{:S(2)}, u32[]{:S(2)}) %collective-permute-start.22) | collective-permute-done | bytes 286752 | tf_op jit(solution)/shard_map/ppermute | solution.py:429
  77.4 3.7 %expert.1 = (bf16[160,896]{1,0:T(8,128)(2,1)S(1)}, bf16[160,896]{1,0:T(8,128)(2,1)S(1)}, bf16[160,896]{1,0:T(8,128)(2,1)S(1)}, bf16[160,896]{1,0:T(8,128)(2,1)S(...) custom-call(s32[4]{0:T(128)S(1)} %pad_add_fusion.1.idx, bf16[768,768]{1,0:T(8,128)(2,1)S(1)} %bitcast.20, ...), custom_call_target="tpu_custom_call" | custom-call | flops 4400000000 | bytes 4000000 | tf_op jit(solution)/shard_map/expert/pallas_call | solution.py:43
  81.8 1.4 collective-permute-start.26
  83.2 1.5 collective-permute-start.27
  84.7 1.9 %collective-permute-start.29 = (bf16[128,768]{1,0:T(8,128)(2,1)S(1)}, bf16[128,768]{1,0:T(8,128)(2,1)S(1)}, u32[]{:S(2)}, u32[]{:S(2)}) collective-permute-start(bf16[128,768]{1,0:T(8,128)(2,1)S(1)} %get-tuple-element.138), channel_id=1, source_target_pairs={{0,6},{1,7},{2,4},{3,5},{4,2},{5,3},{6,0},{7,1},{8,14},{9,15},{10,... | collective-permute-start | bytes 589832 | tf_op jit(solution)/shard_map/ppermute | solution.py:429
  86.6 4.3 %collective-permute-done.25.b = bf16[160,896]{1,0:T(8,128)(2,1)S(1)} collective-permute-done((bf16[160,896]{1,0:T(8,128)(2,1)S(1)}, bf16[160,896]{1,0:T(8,128)(2,1)S(1)}, u32[]{:S(2)}, u32[]{:S(2)}) %collective-permute-start.25) | collective-permute-done | bytes 286752 | tf_op jit(solution)/shard_map/ppermute | solution.py:429
  90.9 5.3 %collective-permute-done.26.c = bf16[160,896]{1,0:T(8,128)(2,1)S(1)} collective-permute-done((bf16[160,896]{1,0:T(8,128)(2,1)S(1)}, bf16[160,896]{1,0:T(8,128)(2,1)S(1)}, u32[]{:S(2)}, u32[]{:S(2)}) %collective-permute-start.26) | collective-permute-done | bytes 286752 | tf_op jit(solution)/shard_map/ppermute | solution.py:429
  98.0 3.4 %collective-permute-start.30 = (bf16[40,896]{1,0:T(8,128)(2,1)S(1)}, bf16[40,896]{1,0:T(8,128)(2,1)S(1)}, u32[]{:S(2)}, u32[]{:S(2)}) collective-permute-start(bf16[40,896]{1,0:T(8,128)(2,1)S(1)} %get-tuple-element.199), channel_id=1, source_target_pairs={{0,2},{1,3},{2,0},{3,1},{4,6},{5,7},{6,4},{7,5},{8,10},{9,11},{10,... | collective-permute-start | bytes 215048 | tf_op jit(solution)/shard_map/ppermute | solution.py:429
  101.4 2.2 %collective-permute-done.32 = bf16[40,896]{1,0:T(8,128)(2,1)S(1)} collective-permute-done((bf16[40,896]{1,0:T(8,128)(2,1)S(1)}, bf16[40,896]{1,0:T(8,128)(2,1)S(1)}, u32[]{:S(2)}, u32[]{:S(2)}) %collective-permute-start.32) | collective-permute-done | bytes 71712 | tf_op jit(solution)/shard_map/ppermute | solution.py:429
  103.5 5.8 %collective-permute-done.31 = bf16[40,896]{1,0:T(8,128)(2,1)S(1)} collective-permute-done((bf16[40,896]{1,0:T(8,128)(2,1)S(1)}, bf16[40,896]{1,0:T(8,128)(2,1)S(1)}, u32[]{:S(2)}, u32[]{:S(2)}) %collective-permute-start.31) | collective-permute-done | bytes 71712 | tf_op jit(solution)/shard_map/ppermute | solution.py:429
  110.3 1.5 expert_out.1
  112.3 1.6 collective-permute-start.35
  113.9 1.5 collective-permute-start.36
  115.4 5.2 %attend_back.1 = (f32[128,768]{1,0:T(8,128)S(1)}, bf16[4,128,768]{2,1,0:T(8,128)(2,1)S(1)}, f32[8,768]{1,0:T(8,128)S(1)}, f32[1,768]{1,0:T(1,128)S(1)}, f32[12,1...) custom-call(s32[4]{0:T(128)S(1)} %pad_add_fusion.1.idx, ...), custom_call_target="tpu_custom_call" | custom-call | flops 6049999872 | bytes 5500000 | tf_op jit(solution)/shard_map/attend_back/pallas_call | solution.py:43
  120.7 1.9 %collective-permute-start.38 = (bf16[128,768]{1,0:T(8,128)(2,1)S(1)}, bf16[128,768]{1,0:T(8,128)(2,1)S(1)}, u32[]{:S(2)}, u32[]{:S(2)}) collective-permute-start(bf16[128,768]{1,0:T(8,128)(2,1)S(1)} %get-tuple-element.163), channel_id=1, source_target_pairs={{0,4},{1,5},{2,6},{3,7},{4,0},{5,1},{6,2},{7,3},{8,12},{9,13},{10,... | collective-permute-start | bytes 589832 | tf_op jit(solution)/shard_map/ppermute | solution.py:429
  122.6 2.5 %collective-permute-start.39 = (bf16[128,768]{1,0:T(8,128)(2,1)S(1)}, bf16[128,768]{1,0:T(8,128)(2,1)S(1)}, u32[]{:S(2)}, u32[]{:S(2)}) collective-permute-start(bf16[128,768]{1,0:T(8,128)(2,1)S(1)} %get-tuple-element.164), channel_id=1, source_target_pairs={{0,6},{1,7},{2,4},{3,5},{4,2},{5,3},{6,0},{7,1},{8,14},{9,15},{10,... | collective-permute-start | bytes 589832 | tf_op jit(solution)/shard_map/ppermute | solution.py:429
  126.3 2.7 %token_grad.1 = (f32[128,768]{1,0:T(8,128)}, bf16[32,768]{1,0:T(8,128)(2,1)S(1)}, bf16[32,128]{1,0:T(8,128)(2,1)S(1)}) custom-call(s32[4]{0:T(128)S(1)} %pad_add_fusion.1.idx, bf16[128,768]{1,0:T(8,128)(2,1)S(1)} %copy-done.10, f32[128,768]{1,0:T(8,128)S(1)} %get-tuple-element.149.dmixed, bf16[4,128,768]{2,1,0:T(8,128)(2,1)S(1)} %get-tuple-element.155.d, ...), custom_call_target="tpu_custom_call" | custom-call | flops 3300000000 | bytes 3000000 | tf_op jit(solution)/shard_map/token_grad/pallas_call | solution.py:43
  130.0 7.9 %collective-permute-done.38.d2 = bf16[128,768]{1,0:T(8,128)(2,1)S(1)} collective-permute-done((bf16[128,768]{1,0:T(8,128)(2,1)S(1)}, bf16[128,768]{1,0:T(8,128)(2,1)S(1)}, u32[]{:S(2)}, u32[]{:S(2)}) %collective-permute-start.38) | collective-permute-done | bytes 196640 | tf_op jit(solution)/shard_map/ppermute | solution.py:429
  137.9 2.0 %mixer_grad.1 = (f32[768,384]{1,0:T(8,128)S(1)}, bf16[768,384]{1,0:T(8,128)(2,1)S(1)}) custom-call(s32[4]{0:T(128)S(1)} %pad_add_fusion.1.idx, f32[32,768]{1,0:T(8,128)S(1)} %get-tuple-element.160.small_all, bf16[128,768]{1,0:T(8,128)(2,1)S(1)} %get-tuple-element.134.l0, bf16[128,768]{1,0:T(8,128)(2,1)S(1)} %collective-permute-done.24.l1, ...), custom_call_target="tpu_custom_call" | custom-call | flops 2200000000 | bytes 2000000 | tf_op jit(solution)/shard_map/mixer_grad/pallas_call | solution.py:43
  140.0 2.0 %collective-permute-done.40.got = bf16[768,384]{1,0:T(8,128)(2,1)S(1)} collective-permute-done((bf16[768,384]{1,0:T(8,128)(2,1)S(1)}, bf16[768,384]{1,0:T(8,128)(2,1)S(1)}, u32[]{:S(2)}, u32[]{:S(2)}) %collective-permute-start.40) | collective-permute-done | bytes 589856 | tf_op jit(solution)/shard_map/ppermute | solution.py:429
  143.6 1.6 collective-permute-start.42
  145.3 1.5 collective-permute-start.43
  146.8 3.7 %collective-permute-done.41.b = bf16[224,384]{1,0:T(8,128)(2,1)S(1)} collective-permute-done((bf16[224,384]{1,0:T(8,128)(2,1)S(1)}, bf16[224,384]{1,0:T(8,128)(2,1)S(1)}, u32[]{:S(2)}, u32[]{:S(2)}) %collective-permute-start.41) | collective-permute-done | bytes 172064 | tf_op jit(solution)/shard_map/ppermute | solution.py:429
  150.5 3.0 %collective-permute-done.42.c = bf16[224,384]{1,0:T(8,128)(2,1)S(1)} collective-permute-done((bf16[224,384]{1,0:T(8,128)(2,1)S(1)}, bf16[224,384]{1,0:T(8,128)(2,1)S(1)}, u32[]{:S(2)}, u32[]{:S(2)}) %collective-permute-start.42) | collective-permute-done | bytes 172064 | tf_op jit(solution)/shard_map/ppermute | solution.py:429
  155.3 3.8 %collective-permute-start.45 = (bf16[40,768]{1,0:T(8,128)(2,1)S(1)}, bf16[40,768]{1,0:T(8,128)(2,1)S(1)}, u32[]{:S(2)}, u32[]{:S(2)}) collective-permute-start(bf16[40,768]{1,0:T(8,128)(2,1)S(1)} %get-tuple-element.206), channel_id=1, source_target_pairs={{0,4},{1,5},{2,6},{3,7},{4,0},{5,1},{6,2},{7,3},{8,12},{9,13},{10,... | collective-permute-start | bytes 184328 | tf_op jit(solution)/shard_map/ppermute | solution.py:429
  159.3 1.5 collective-permute-start.50
  160.8 2.0 %collective-permute-start.49 = (bf16[224,384]{1,0:T(8,128)(2,1)S(1)}, bf16[224,384]{1,0:T(8,128)(2,1)S(1)}, u32[]{:S(2)}, u32[]{:S(2)}) collective-permute-start(bf16[224,384]{1,0:T(8,128)(2,1)S(1)} %sum_share.1.a0), channel_id=1, source_target_pairs={{0,4},{1,5},{2,6},{3,7},{4,0},{5,1},{6,2},{7,3},{8,12},{9,13},{10,... | collective-permute-start | bytes 516104 | tf_op jit(solution)/shard_map/ppermute | solution.py:429
  162.8 1.4 collective-permute-start.48
  164.2 7.0 %collective-permute-done.45 = bf16[40,768]{1,0:T(8,128)(2,1)S(1)} collective-permute-done((bf16[40,768]{1,0:T(8,128)(2,1)S(1)}, bf16[40,768]{1,0:T(8,128)(2,1)S(1)}, u32[]{:S(2)}, u32[]{:S(2)}) %collective-permute-start.45) | collective-permute-done | bytes 61472 | tf_op jit(solution)/shard_map/ppermute | solution.py:429
  172.2 5.5 %expert_grad.1 = (f32[1,768,768]{2,1,0:T(8,128)}, f32[1,768,768]{2,1,0:T(8,128)}) custom-call(s32[4]{0:T(128)S(1)} %pad_add_fusion.1.idx, bf16[4,160,768]{2,1,0:T(8,128)(2,1)S(1)} %get-tuple-element.124.hid, bf16[4,160,768]{2,1,0:T(8,128)(2,1)S(1)} %get-tuple-element.181.dpre, bf16[160,896]{1,0:T(8,128)(2,1)S(1)} %pad_maximum_fusion.2.x0, ...), custom_call_target="tpu_custom_call" | custom-call | flops 6049999872 | bytes 5500000 | tf_op jit(solution)/shard_map/expert_grad/pallas_call | solution.py:43
  180.1 2.2 %finish.1 = (f32[192,768]{1,0:T(8,128)}, f32[192,768]{1,0:T(8,128)}, f32[192,768]{1,0:T(8,128)}, f32[192,768]{1,0:T(8,128)}, f32[32,384]{1,0:T(8,128)S(1)}) custom-call(s32[4]{0:T(128)S(1)} %pad_add_fusion.1.idx, bf16[224,384]{1,0:T(8,128)(2,1)S(1)} %sum_share.1.a0, bf16[224,384]{1,0:T(8,128)(2,1)S(1)} %collective-permute-done.48.a1, ...), custom_call_target="tpu_custom_call" | custom-call | flops 2200000000 | bytes 2000000 | tf_op jit(solution)/shard_map/finish/pallas_call | solution.py:43
  (141 shorter events, 32.7 us)
Async XLA Ops:
  2.0 18.9 %collective-permute-start.1 = (bf16[384,768]{1,0:T(8,128)(2,1)S(1)}, bf16[384,768]{1,0:T(8,128)(2,1)S(1)}, u32[]{:S(2)}, u32[]{:S(2)}) collective-permute-start(bf16[384,768]{1,0:T(8,128)(2,1)S(1)} %pad_maximum_fusion), channel_id=1, source_target_pairs={{0,16},{8,24},{16,0},{24,8},{1,17},{9,25},{17,1},{25,9},{2,18},{10... | collective-permute-start | bytes 1769480 | tf_op jit(solution)/shard_map/ppermute | solution.py:429
  5.0 15.9 %collective-permute-start = (bf16[384,768]{1,0:T(8,128)(2,1)S(1)}, bf16[384,768]{1,0:T(8,128)(2,1)S(1)}, u32[]{:S(2)}, u32[]{:S(2)}) collective-permute-start(bf16[384,768]{1,0:T(8,128)(2,1)S(1)} %pad_maximum_fusion), channel_id=1, source_target_pairs={{0,8},{8,0},{16,24},{24,16},{1,9},{9,1},{17,25},{25,17},{2,10},{10... | collective-permute-start | bytes 1769480 | tf_op jit(solution)/shard_map/ppermute | solution.py:429
  9.1 6.4 %collective-permute-start.6 = (bf16[40,768]{1,0:T(8,128)(2,1)S(1)}, bf16[40,768]{1,0:T(8,128)(2,1)S(1)}, u32[]{:S(2)}, u32[]{:S(2)}) collective-permute-start(bf16[40,768]{1,0:T(8,128)(2,1)S(1)} %get-tuple-element.209), channel_id=1, source_target_pairs={{0,6},{1,7},{2,4},{3,5},{4,2},{5,3},{6,0},{7,1},{8,14},{9,15},{10,... | collective-permute-start | bytes 184328 | tf_op jit(solution)/shard_map/ppermute | solution.py:429
  12.8 5.6 %collective-permute-start.5 = (bf16[40,768]{1,0:T(8,128)(2,1)S(1)}, bf16[40,768]{1,0:T(8,128)(2,1)S(1)}, u32[]{:S(2)}, u32[]{:S(2)}) collective-permute-start(bf16[40,768]{1,0:T(8,128)(2,1)S(1)} %get-tuple-element.210), channel_id=1, source_target_pairs={{0,4},{1,5},{2,6},{3,7},{4,0},{5,1},{6,2},{7,3},{8,12},{9,13},{10,... | collective-permute-start | bytes 184328 | tf_op jit(solution)/shard_map/ppermute | solution.py:429
  12.8 5.6 %collective-permute-start.4 = (bf16[40,768]{1,0:T(8,128)(2,1)S(1)}, bf16[40,768]{1,0:T(8,128)(2,1)S(1)}, u32[]{:S(2)}, u32[]{:S(2)}) collective-permute-start(bf16[40,768]{1,0:T(8,128)(2,1)S(1)} %get-tuple-element.211), channel_id=1, source_target_pairs={{0,2},{1,3},{2,0},{3,1},{4,6},{5,7},{6,4},{7,5},{8,10},{9,11},{10,... | collective-permute-start | bytes 184328 | tf_op jit(solution)/shard_map/ppermute | solution.py:429
  15.5 5.4 %collective-permute-start.7 = (bf16[32,768]{1,0:T(8,128)(2,1)S(1)}, bf16[32,768]{1,0:T(8,128)(2,1)S(1)}, u32[]{:S(2)}, u32[]{:S(2)}) collective-permute-start(bf16[32,768]{1,0:T(8,128)(2,1)S(1)} %pack.1.s0), channel_id=1, source_target_pairs={{0,8},{8,0},{16,24},{24,16},{1,9},{9,1},{17,25},{25,17},{2,10},{10... | collective-permute-start | bytes 147464 | tf_op jit(solution)/shard_map/ppermute | solution.py:429
  20.9 9.8 %collective-permute-start.8 = (bf16[256,768]{1,0:T(8,128)(2,1)S(1)}, bf16[256,768]{1,0:T(8,128)(2,1)}, u32[]{:S(2)}, u32[]{:S(2)}) collective-permute-start(bf16[256,768]{1,0:T(8,128)(2,1)S(1)} %pad_maximum_fusion.1), channel_id=1, source_target_pairs={{0,16},{8,24},{16,0},{24,8},{1,17},{9,25},{17,1},{25,9},{2,18},{10... | collective-permute-start | bytes 1179656 | tf_op jit(solution)/shard_map/ppermute | solution.py:429
  21.4 9.4 %collective-permute-start.9 = (bf16[192,768]{1,0:T(8,128)(2,1)S(1)}, bf16[192,768]{1,0:T(8,128)(2,1)}, u32[]{:S(2)}, u32[]{:S(2)}) collective-permute-start(bf16[192,768]{1,0:T(8,128)(2,1)S(1)} %slice.71), channel_id=1, source_target_pairs={{0,8},{8,0},{16,24},{24,16},{1,9},{9,1},{17,25},{25,17},{2,10},{10... | collective-permute-start | bytes 884744 | tf_op jit(solution)/shard_map/ppermute | solution.py:429
  23.1 10.2 %collective-permute-start.10 = (bf16[384,768]{1,0:T(8,128)(2,1)S(1)}, bf16[384,768]{1,0:T(8,128)(2,1)S(1)}, u32[]{:S(2)}, u32[]{:S(2)}) collective-permute-start(bf16[384,768]{1,0:T(8,128)(2,1)S(1)} %collective-permute-done.hx), channel_id=1, source_target_pairs={{0,1},{1,0},{2,3},{3,2},{4,5},{5,4},{6,7},{7,6},{8,9},{9,8},{10,11... | collective-permute-start | bytes 1769480 | tf_op jit(solution)/shard_map/ppermute | solution.py:429
  23.1 10.2 %collective-permute-start.11 = (bf16[384,768]{1,0:T(8,128)(2,1)S(1)}, bf16[384,768]{1,0:T(8,128)(2,1)}, u32[]{:S(2)}, u32[]{:S(2)}) collective-permute-start(bf16[384,768]{1,0:T(8,128)(2,1)S(1)} %collective-permute-done.1.hy), channel_id=1, source_target_pairs={{0,1},{1,0},{2,3},{3,2},{4,5},{5,4},{6,7},{7,6},{8,9},{9,8},{10,11... | collective-permute-start | bytes 1769480 | tf_op jit(solution)/shard_map/ppermute | solution.py:429
  30.8 2.5 %collective-permute-start.12 = (bf16[256,768]{1,0:T(8,128)(2,1)}, bf16[256,768]{1,0:T(8,128)(2,1)}, u32[]{:S(2)}, u32[]{:S(2)}) collective-permute-start(bf16[256,768]{1,0:T(8,128)(2,1)} %collective-permute-done.8.da), channel_id=1, source_target_pairs={{0,1},{1,0},{2,3},{3,2},{4,5},{5,4},{6,7},{7,6},{8,9},{9,8},{10,11... | collective-permute-start | bytes 1179656 | tf_op jit(solution)/shard_map/ppermute | solution.py:429
  30.8 2.5 %collective-permute-start.13 = (bf16[192,768]{1,0:T(8,128)(2,1)}, bf16[192,768]{1,0:T(8,128)(2,1)}, u32[]{:S(2)}, u32[]{:S(2)}) collective-permute-start(bf16[192,768]{1,0:T(8,128)(2,1)} %collective-permute-done.9.db), channel_id=1, source_target_pairs={{0,1},{1,0},{2,3},{3,2},{4,5},{5,4},{6,7},{7,6},{8,9},{9,8},{10,11... | collective-permute-start | bytes 884744 | tf_op jit(solution)/shard_map/ppermute | solution.py:429
  44.0 7.2 %collective-permute-start.20 = (bf16[40,896]{1,0:T(8,128)(2,1)S(1)}, bf16[40,896]{1,0:T(8,128)(2,1)S(1)}, u32[]{:S(2)}, u32[]{:S(2)}) collective-permute-start(bf16[40,896]{1,0:T(8,128)(2,1)S(1)} %get-tuple-element.201), channel_id=1, source_target_pairs={{0,6},{1,7},{2,4},{3,5},{4,2},{5,3},{6,0},{7,1},{8,14},{9,15},{10,... | collective-permute-start | bytes 215048 | tf_op jit(solution)/shard_map/ppermute | solution.py:429
  47.7 9.8 %collective-permute-start.16 = (bf16[160,768]{1,0:T(8,128)(2,1)S(1)}, bf16[160,768]{1,0:T(8,128)(2,1)S(1)}, u32[]{:S(2)}, u32[]{:S(2)}) collective-permute-start(bf16[160,768]{1,0:T(8,128)(2,1)S(1)} %pad_maximum_fusion.4.refs_0_.g0), channel_id=1, source_target_pairs={{0,24},{8,16},{16,8},{24,0},{1,25},{9,17},{17,9},{25,1},{2,26},{10... | collective-permute-start | bytes 737288 | tf_op jit(solution)/shard_map/ppermute | solution.py:429
  49.1 12.4 %collective-permute-start.15 = (bf16[160,768]{1,0:T(8,128)(2,1)S(1)}, bf16[160,768]{1,0:T(8,128)(2,1)S(1)}, u32[]{:S(2)}, u32[]{:S(2)}) collective-permute-start(bf16[160,768]{1,0:T(8,128)(2,1)S(1)} %pad_maximum_fusion.4.refs_0_.g0), channel_id=1, source_target_pairs={{0,16},{8,24},{16,0},{24,8},{1,17},{9,25},{17,1},{25,9},{2,18},{10... | collective-permute-start | bytes 737288 | tf_op jit(solution)/shard_map/ppermute | solution.py:429
  50.6 10.9 %collective-permute-start.14 = (bf16[160,768]{1,0:T(8,128)(2,1)S(1)}, bf16[160,768]{1,0:T(8,128)(2,1)S(1)}, u32[]{:S(2)}, u32[]{:S(2)}) collective-permute-start(bf16[160,768]{1,0:T(8,128)(2,1)S(1)} %pad_maximum_fusion.4.refs_0_.g0), channel_id=1, source_target_pairs={{0,8},{8,0},{16,24},{24,16},{1,9},{9,1},{17,25},{25,17},{2,10},{10... | collective-permute-start | bytes 737288 | tf_op jit(solution)/shard_map/ppermute | solution.py:429
  51.2 5.4 %collective-permute-start.19 = (bf16[40,896]{1,0:T(8,128)(2,1)S(1)}, bf16[40,896]{1,0:T(8,128)(2,1)S(1)}, u32[]{:S(2)}, u32[]{:S(2)}) collective-permute-start(bf16[40,896]{1,0:T(8,128)(2,1)S(1)} %get-tuple-element.202), channel_id=1, source_target_pairs={{0,4},{1,5},{2,6},{3,7},{4,0},{5,1},{6,2},{7,3},{8,12},{9,13},{10,... | collective-permute-start | bytes 215048 | tf_op jit(solution)/shard_map/ppermute | solution.py:429
  51.2 5.4 %collective-permute-start.18 = (bf16[40,896]{1,0:T(8,128)(2,1)S(1)}, bf16[40,896]{1,0:T(8,128)(2,1)S(1)}, u32[]{:S(2)}, u32[]{:S(2)}) collective-permute-start(bf16[40,896]{1,0:T(8,128)(2,1)S(1)} %get-tuple-element.203), channel_id=1, source_target_pairs={{0,2},{1,3},{2,0},{3,1},{4,6},{5,7},{6,4},{7,5},{8,10},{9,11},{10,... | collective-permute-start | bytes 215048 | tf_op jit(solution)/shard_map/ppermute | solution.py:429
  61.6 10.6 %collective-permute-start.23 = (bf16[160,896]{1,0:T(8,128)(2,1)S(1)}, bf16[160,896]{1,0:T(8,128)(2,1)S(1)}, u32[]{:S(2)}, u32[]{:S(2)}) collective-permute-start(bf16[160,896]{1,0:T(8,128)(2,1)S(1)} %pad_maximum_fusion.2.x0), channel_id=1, source_target_pairs={{0,24},{8,16},{16,8},{24,0},{1,25},{9,17},{17,9},{25,1},{2,26},{10... | collective-permute-start | bytes 860168 | tf_op jit(solution)/shard_map/ppermute | solution.py:429
  63.1 14.3 %collective-permute-start.22 = (bf16[160,896]{1,0:T(8,128)(2,1)S(1)}, bf16[160,896]{1,0:T(8,128)(2,1)S(1)}, u32[]{:S(2)}, u32[]{:S(2)}) collective-permute-start(bf16[160,896]{1,0:T(8,128)(2,1)S(1)} %pad_maximum_fusion.2.x0), channel_id=1, source_target_pairs={{0,16},{8,24},{16,0},{24,8},{1,17},{9,25},{17,1},{25,9},{2,18},{10... | collective-permute-start | bytes 860168 | tf_op jit(solution)/shard_map/ppermute | solution.py:429
  63.8 13.5 %collective-permute-start.21 = (bf16[160,896]{1,0:T(8,128)(2,1)S(1)}, bf16[160,896]{1,0:T(8,128)(2,1)S(1)}, u32[]{:S(2)}, u32[]{:S(2)}) collective-permute-start(bf16[160,896]{1,0:T(8,128)(2,1)S(1)} %pad_maximum_fusion.2.x0), channel_id=1, source_target_pairs={{0,8},{8,0},{16,24},{24,16},{1,9},{9,1},{17,25},{25,17},{2,10},{10... | collective-permute-start | bytes 860168 | tf_op jit(solution)/shard_map/ppermute | solution.py:429
  65.1 6.0 %collective-permute-start.24 = (bf16[128,768]{1,0:T(8,128)(2,1)S(1)}, bf16[128,768]{1,0:T(8,128)(2,1)S(1)}, u32[]{:S(2)}, u32[]{:S(2)}) collective-permute-start(bf16[128,768]{1,0:T(8,128)(2,1)S(1)} %get-tuple-element.122), channel_id=1, source_target_pairs={{0,2},{1,3},{2,0},{3,1},{4,6},{5,7},{6,4},{7,5},{8,10},{9,11},{10,... | collective-permute-start | bytes 589832 | tf_op jit(solution)/shard_map/ppermute | solution.py:429
  81.1 9.8 %collective-permute-start.25 = (bf16[160,896]{1,0:T(8,128)(2,1)S(1)}, bf16[160,896]{1,0:T(8,128)(2,1)S(1)}, u32[]{:S(2)}, u32[]{:S(2)}) collective-permute-start(bf16[160,896]{1,0:T(8,128)(2,1)S(1)} %get-tuple-element.130), channel_id=1, source_target_pairs={{0,8},{8,0},{16,24},{24,16},{1,9},{9,1},{17,25},{25,17},{2,10},{10... | collective-permute-start | bytes 860168 | tf_op jit(solution)/shard_map/ppermute | solution.py:429
  81.8 14.4 %collective-permute-start.26 = (bf16[160,896]{1,0:T(8,128)(2,1)S(1)}, bf16[160,896]{1,0:T(8,128)(2,1)S(1)}, u32[]{:S(2)}, u32[]{:S(2)}) collective-permute-start(bf16[160,896]{1,0:T(8,128)(2,1)S(1)} %get-tuple-element.131), channel_id=1, source_target_pairs={{0,16},{8,24},{16,0},{24,8},{1,17},{9,25},{17,1},{25,9},{2,18},{10... | collective-permute-start | bytes 860168 | tf_op jit(solution)/shard_map/ppermute | solution.py:429
  83.2 13.0 %collective-permute-start.27 = (bf16[160,896]{1,0:T(8,128)(2,1)S(1)}, bf16[160,896]{1,0:T(8,128)(2,1)S(1)}, u32[]{:S(2)}, u32[]{:S(2)}) collective-permute-start(bf16[160,896]{1,0:T(8,128)(2,1)S(1)} %get-tuple-element.132), channel_id=1, source_target_pairs={{0,24},{8,16},{16,8},{24,0},{1,25},{9,17},{17,9},{25,1},{2,26},{10... | collective-permute-start | bytes 860168 | tf_op jit(solution)/shard_map/ppermute | solution.py:429
  84.7 16.7 %collective-permute-start.28 = (bf16[128,768]{1,0:T(8,128)(2,1)S(1)}, bf16[128,768]{1,0:T(8,128)(2,1)S(1)}, u32[]{:S(2)}, u32[]{:S(2)}) collective-permute-start(bf16[128,768]{1,0:T(8,128)(2,1)S(1)} %get-tuple-element.136), channel_id=1, source_target_pairs={{0,4},{1,5},{2,6},{3,7},{4,0},{5,1},{6,2},{7,3},{8,12},{9,13},{10,... | collective-permute-start | bytes 589832 | tf_op jit(solution)/shard_map/ppermute | solution.py:429
  84.7 16.7 %collective-permute-start.29 = (bf16[128,768]{1,0:T(8,128)(2,1)S(1)}, bf16[128,768]{1,0:T(8,128)(2,1)S(1)}, u32[]{:S(2)}, u32[]{:S(2)}) collective-permute-start(bf16[128,768]{1,0:T(8,128)(2,1)S(1)} %get-tuple-element.138), channel_id=1, source_target_pairs={{0,6},{1,7},{2,4},{3,5},{4,2},{5,3},{6,0},{7,1},{8,14},{9,15},{10,... | collective-permute-start | bytes 589832 | tf_op jit(solution)/shard_map/ppermute | solution.py:429
  96.9 6.6 %collective-permute-start.32 = (bf16[40,896]{1,0:T(8,128)(2,1)S(1)}, bf16[40,896]{1,0:T(8,128)(2,1)S(1)}, u32[]{:S(2)}, u32[]{:S(2)}) collective-permute-start(bf16[40,896]{1,0:T(8,128)(2,1)S(1)} %get-tuple-element.197), channel_id=1, source_target_pairs={{0,6},{1,7},{2,4},{3,5},{4,2},{5,3},{6,0},{7,1},{8,14},{9,15},{10,... | collective-permute-start | bytes 215048 | tf_op jit(solution)/shard_map/ppermute | solution.py:429
  97.3 12.0 %collective-permute-start.31 = (bf16[40,896]{1,0:T(8,128)(2,1)S(1)}, bf16[40,896]{1,0:T(8,128)(2,1)S(1)}, u32[]{:S(2)}, u32[]{:S(2)}) collective-permute-start(bf16[40,896]{1,0:T(8,128)(2,1)S(1)} %get-tuple-element.198), channel_id=1, source_target_pairs={{0,4},{1,5},{2,6},{3,7},{4,0},{5,1},{6,2},{7,3},{8,12},{9,13},{10,... | collective-permute-start | bytes 215048 | tf_op jit(solution)/shard_map/ppermute | solution.py:429
  98.0 11.4 %collective-permute-start.30 = (bf16[40,896]{1,0:T(8,128)(2,1)S(1)}, bf16[40,896]{1,0:T(8,128)(2,1)S(1)}, u32[]{:S(2)}, u32[]{:S(2)}) collective-permute-start(bf16[40,896]{1,0:T(8,128)(2,1)S(1)} %get-tuple-element.199), channel_id=1, source_target_pairs={{0,2},{1,3},{2,0},{3,1},{4,6},{5,7},{6,4},{7,5},{8,10},{9,11},{10,... | collective-permute-start | bytes 215048 | tf_op jit(solution)/shard_map/ppermute | solution.py:429
  110.2 5.2 %collective-permute-start.33 = (bf16[128,896]{1,0:T(8,128)(2,1)S(1)}, bf16[128,896]{1,0:T(8,128)(2,1)S(1)}, u32[]{:S(2)}, u32[]{:S(2)}) collective-permute-start(bf16[128,896]{1,0:T(8,128)(2,1)S(1)} %get-tuple-element.141), channel_id=1, source_target_pairs={{0,1},{1,0},{2,3},{3,2},{4,5},{5,4},{6,7},{7,6},{8,9},{9,8},{10,11... | collective-permute-start | bytes 688136 | tf_op jit(solution)/shard_map/ppermute | solution.py:429
  111.9 10.7 %collective-permute-start.34 = (bf16[160,768]{1,0:T(8,128)(2,1)S(1)}, bf16[160,768]{1,0:T(8,128)(2,1)S(1)}, u32[]{:S(2)}, u32[]{:S(2)}) collective-permute-start(bf16[160,768]{1,0:T(8,128)(2,1)S(1)} %get-tuple-element.151), channel_id=1, source_target_pairs={{0,8},{8,0},{16,24},{24,16},{1,9},{9,1},{17,25},{25,17},{2,10},{10... | collective-permute-start | bytes 737288 | tf_op jit(solution)/shard_map/ppermute | solution.py:429
  112.3 13.3 %collective-permute-start.35 = (bf16[160,768]{1,0:T(8,128)(2,1)S(1)}, bf16[160,768]{1,0:T(8,128)(2,1)S(1)}, u32[]{:S(2)}, u32[]{:S(2)}) collective-permute-start(bf16[160,768]{1,0:T(8,128)(2,1)S(1)} %get-tuple-element.152), channel_id=1, source_target_pairs={{0,16},{8,24},{16,0},{24,8},{1,17},{9,25},{17,1},{25,9},{2,18},{10... | collective-permute-start | bytes 737288 | tf_op jit(solution)/shard_map/ppermute | solution.py:429
  113.9 11.7 %collective-permute-start.36 = (bf16[160,768]{1,0:T(8,128)(2,1)S(1)}, bf16[160,768]{1,0:T(8,128)(2,1)S(1)}, u32[]{:S(2)}, u32[]{:S(2)}) collective-permute-start(bf16[160,768]{1,0:T(8,128)(2,1)S(1)} %get-tuple-element.153), channel_id=1, source_target_pairs={{0,24},{8,16},{16,8},{24,0},{1,25},{9,17},{17,9},{25,1},{2,26},{10... | collective-permute-start | bytes 737288 | tf_op jit(solution)/shard_map/ppermute | solution.py:429
  120.6 9.4 %collective-permute-start.37 = (bf16[128,768]{1,0:T(8,128)(2,1)S(1)}, bf16[128,768]{1,0:T(8,128)(2,1)S(1)}, u32[]{:S(2)}, u32[]{:S(2)}) collective-permute-start(bf16[128,768]{1,0:T(8,128)(2,1)S(1)} %get-tuple-element.154), channel_id=1, source_target_pairs={{0,2},{1,3},{2,0},{3,1},{4,6},{5,7},{6,4},{7,5},{8,10},{9,11},{10,... | collective-permute-start | bytes 589832 | tf_op jit(solution)/shard_map/ppermute | solution.py:429
  120.7 17.2 %collective-permute-start.38 = (bf16[128,768]{1,0:T(8,128)(2,1)S(1)}, bf16[128,768]{1,0:T(8,128)(2,1)S(1)}, u32[]{:S(2)}, u32[]{:S(2)}) collective-permute-start(bf16[128,768]{1,0:T(8,128)(2,1)S(1)} %get-tuple-element.163), channel_id=1, source_target_pairs={{0,4},{1,5},{2,6},{3,7},{4,0},{5,1},{6,2},{7,3},{8,12},{9,13},{10,... | collective-permute-start | bytes 589832 | tf_op jit(solution)/shard_map/ppermute | solution.py:429
  122.6 15.3 %collective-permute-start.39 = (bf16[128,768]{1,0:T(8,128)(2,1)S(1)}, bf16[128,768]{1,0:T(8,128)(2,1)S(1)}, u32[]{:S(2)}, u32[]{:S(2)}) collective-permute-start(bf16[128,768]{1,0:T(8,128)(2,1)S(1)} %get-tuple-element.164), channel_id=1, source_target_pairs={{0,6},{1,7},{2,4},{3,5},{4,2},{5,3},{6,0},{7,1},{8,14},{9,15},{10,... | collective-permute-start | bytes 589832 | tf_op jit(solution)/shard_map/ppermute | solution.py:429
  139.9 2.1 %collective-permute-start.40 = (bf16[768,384]{1,0:T(8,128)(2,1)S(1)}, bf16[768,384]{1,0:T(8,128)(2,1)S(1)}, u32[]{:S(2)}, u32[]{:S(2)}) collective-permute-start(bf16[768,384]{1,0:T(8,128)(2,1)S(1)} %get-tuple-element.166), channel_id=1, source_target_pairs={{0,1},{1,0},{2,3},{3,2},{4,5},{5,4},{6,7},{7,6},{8,9},{9,8},{10,11... | collective-permute-start | bytes 1769480 | tf_op jit(solution)/shard_map/ppermute | solution.py:429
  143.2 7.3 %collective-permute-start.41 = (bf16[224,384]{1,0:T(8,128)(2,1)S(1)}, bf16[224,384]{1,0:T(8,128)(2,1)S(1)}, u32[]{:S(2)}, u32[]{:S(2)}) collective-permute-start(bf16[224,384]{1,0:T(8,128)(2,1)S(1)} %get-tuple-element.169), channel_id=1, source_target_pairs={{0,8},{8,0},{16,24},{24,16},{1,9},{9,1},{17,25},{25,17},{2,10},{10... | collective-permute-start | bytes 516104 | tf_op jit(solution)/shard_map/ppermute | solution.py:429
  143.6 9.8 %collective-permute-start.42 = (bf16[224,384]{1,0:T(8,128)(2,1)S(1)}, bf16[224,384]{1,0:T(8,128)(2,1)S(1)}, u32[]{:S(2)}, u32[]{:S(2)}) collective-permute-start(bf16[224,384]{1,0:T(8,128)(2,1)S(1)} %get-tuple-element.170), channel_id=1, source_target_pairs={{0,16},{8,24},{16,0},{24,8},{1,17},{9,25},{17,1},{25,9},{2,18},{10... | collective-permute-start | bytes 516104 | tf_op jit(solution)/shard_map/ppermute | solution.py:429
  145.3 8.2 %collective-permute-start.43 = (bf16[224,384]{1,0:T(8,128)(2,1)S(1)}, bf16[224,384]{1,0:T(8,128)(2,1)S(1)}, u32[]{:S(2)}, u32[]{:S(2)}) collective-permute-start(bf16[224,384]{1,0:T(8,128)(2,1)S(1)} %get-tuple-element.171), channel_id=1, source_target_pairs={{0,24},{8,16},{16,8},{24,0},{1,25},{9,17},{17,9},{25,1},{2,26},{10... | collective-permute-start | bytes 516104 | tf_op jit(solution)/shard_map/ppermute | solution.py:429
  154.1 8.7 %collective-permute-start.46 = (bf16[40,768]{1,0:T(8,128)(2,1)S(1)}, bf16[40,768]{1,0:T(8,128)(2,1)S(1)}, u32[]{:S(2)}, u32[]{:S(2)}) collective-permute-start(bf16[40,768]{1,0:T(8,128)(2,1)S(1)} %get-tuple-element.205), channel_id=1, source_target_pairs={{0,6},{1,7},{2,4},{3,5},{4,2},{5,3},{6,0},{7,1},{8,14},{9,15},{10,... | collective-permute-start | bytes 184328 | tf_op jit(solution)/shard_map/ppermute | solution.py:429
  155.3 15.9 %collective-permute-start.45 = (bf16[40,768]{1,0:T(8,128)(2,1)S(1)}, bf16[40,768]{1,0:T(8,128)(2,1)S(1)}, u32[]{:S(2)}, u32[]{:S(2)}) collective-permute-start(bf16[40,768]{1,0:T(8,128)(2,1)S(1)} %get-tuple-element.206), channel_id=1, source_target_pairs={{0,4},{1,5},{2,6},{3,7},{4,0},{5,1},{6,2},{7,3},{8,12},{9,13},{10,... | collective-permute-start | bytes 184328 | tf_op jit(solution)/shard_map/ppermute | solution.py:429
  159.1 12.1 %collective-permute-start.44 = (bf16[40,768]{1,0:T(8,128)(2,1)S(1)}, bf16[40,768]{1,0:T(8,128)(2,1)S(1)}, u32[]{:S(2)}, u32[]{:S(2)}) collective-permute-start(bf16[40,768]{1,0:T(8,128)(2,1)S(1)} %get-tuple-element.207), channel_id=1, source_target_pairs={{0,2},{1,3},{2,0},{3,1},{4,6},{5,7},{6,4},{7,5},{8,10},{9,11},{10,... | collective-permute-start | bytes 184328 | tf_op jit(solution)/shard_map/ppermute | solution.py:429
  159.3 18.9 %collective-permute-start.50 = (bf16[224,384]{1,0:T(8,128)(2,1)S(1)}, bf16[224,384]{1,0:T(8,128)(2,1)S(1)}, u32[]{:S(2)}, u32[]{:S(2)}) collective-permute-start(bf16[224,384]{1,0:T(8,128)(2,1)S(1)} %sum_share.1.a0), channel_id=1, source_target_pairs={{0,6},{1,7},{2,4},{3,5},{4,2},{5,3},{6,0},{7,1},{8,14},{9,15},{10,... | collective-permute-start | bytes 516104 | tf_op jit(solution)/shard_map/ppermute | solution.py:429
  160.8 17.4 %collective-permute-start.49 = (bf16[224,384]{1,0:T(8,128)(2,1)S(1)}, bf16[224,384]{1,0:T(8,128)(2,1)S(1)}, u32[]{:S(2)}, u32[]{:S(2)}) collective-permute-start(bf16[224,384]{1,0:T(8,128)(2,1)S(1)} %sum_share.1.a0), channel_id=1, source_target_pairs={{0,4},{1,5},{2,6},{3,7},{4,0},{5,1},{6,2},{7,3},{8,12},{9,13},{10,... | collective-permute-start | bytes 516104 | tf_op jit(solution)/shard_map/ppermute | solution.py:429
  162.8 15.8 %collective-permute-start.48 = (bf16[224,384]{1,0:T(8,128)(2,1)S(1)}, bf16[224,384]{1,0:T(8,128)(2,1)S(1)}, u32[]{:S(2)}, u32[]{:S(2)}) collective-permute-start(bf16[224,384]{1,0:T(8,128)(2,1)S(1)} %sum_share.1.a0), channel_id=1, source_target_pairs={{0,2},{1,3},{2,0},{3,1},{4,6},{5,7},{6,4},{7,5},{8,10},{9,11},{10,... | collective-permute-start | bytes 516104 | tf_op jit(solution)/shard_map/ppermute | solution.py:429
  172.1 6.7 %collective-permute-start.47 = (bf16[128,768]{1,0:T(8,128)(2,1)S(1)}, bf16[128,768]{1,0:T(8,128)(2,1)S(1)}, u32[]{:S(2)}, u32[]{:S(2)}) collective-permute-start(bf16[128,768]{1,0:T(8,128)(2,1)S(1)} %get-tuple-element.174), channel_id=1, source_target_pairs={{0,1},{1,0},{2,3},{3,2},{4,5},{5,4},{6,7},{7,6},{8,9},{9,8},{10,11... | collective-permute-start | bytes 589832 | tf_op jit(solution)/shard_map/ppermute | solution.py:429
  (24 other events, 172.2 us)

commit v3 on v2

--- a/solution.py
+++ b/solution.py
@@ -148,9 +148,10 @@
     small = jnp.zeros((smalls, width), f32)
     table_t = jnp.zeros((smalls, 128), f32)
     shard = 32 // 4
-    for k, piece, start in ((0, s0, 0), (1, s1, 0), (2, da, rows), (3, da, rows + smalls)):
+    for k, part in (
+        (0, s0[...]), (1, s1[...]), (2, da[rows : rows + smalls, 0:256]), (3, da[rows : rows + smalls, 256:512])
+    ):
         j = mine ^ k
-        part = piece[start : start + smalls, 0:256]
         r, c = iota((256, width), 0), iota((256, width), 1)
         small = small + nn(part, ((r < rows) & (c == r + rows * j)).astype(f32).astype(bf16))
         r, c = iota((256, 128), 0), iota((256, 128), 1)
@@ -453,7 +454,7 @@
         (w_router.T, norm1_gain, norm2_gain, bias_table, cotangent, routes, segments, parcel)
     )[:-1]
     small_own = call(
-        "pack", 1, partial(pack_body, experts, smalls), [((smalls, width), bf16)], idx,
+        "pack", 1, partial(pack_body, experts, smalls), [((smalls, 256), bf16)], idx,
         wr_t, gain_a[None], gain_b[None], tab,
     )[0]
     small_x = along(small_own, "dp", 1)
@@ -474,7 +475,9 @@
     hx, hy, place, g_here, seg_c, seg_r, route_c, small_own, small_x = lax.optimization_barrier(
         (hx, hy, place, g_here, seg_c, seg_r, route_c, small_own, small_x)
     )
-    da = along(jnp.concatenate([hx[0:rows], small_own, small_x], axis=0), "dp", 2)
+    tail = jnp.zeros((smalls, width - 512), bf16)
+    tail = jnp.concatenate([small_own, small_x, tail], axis=1)
+    da = along(jnp.concatenate([hx[0:rows], tail], axis=0), "dp", 2)
     db = along(hy[rows:], "dp", 1)
     tx, ty = twin(hx), twin(hy)
     ta, tb = twin(da), twin(db)
@@ -497,11 +500,10 @@
 
     x_rows = call("place_x", 1, place_rows_body, [((slots, wide), bf16)], idx, place, hcat, twin(hcat))[0]
     x_here = chip_exchange(x_rows)
-    x_here = after(x_here, *g_set)
     x_set = [x_here] + [along(x_here, "dp", kk) for kk in (1, 2, 3)]
     if chips == 4:
         left = [left[0]] + [along(after(left[zr], x_here), "expert", 2 * zr) for zr in range(1, 4)]
-        x_set[3] = after(x_set[3], left[1])
+        x_set[3] = after(x_set[3], left[1], left[2])
     *d_parts, hid, dpre = call(
         "expert", 4, expert_body,
         [((slots, wide), bf16)] * 4 + [((4, slots, width), bf16)] * 2,

time: 184 us -> 172 us (0.935)
  waiting for transfers between devices: 80 us -> 59.8 us
  starting transfers between devices: 57.5 us -> 64.9 us
    ppermute x55, waiting for transfers between devices: 80 us -> 59.8 us  [along(): return lax.ppermute(x, axis, [(s, s ^ mask) for s in range(n)])]
    ppermute x55, starting transfers between devices: 57.5 us -> 64.9 us  [along(): return lax.ppermute(x, axis, [(s, s ^ mask) for s in range(n)])]
  transfers between devices with their start and end apart: 55 -> 55, of which waited for: 28 -> 26; matrix products, arithmetic and copies ran while one was open for 1% -> 1% of each run, Pallas kernels for 11% -> 13%
where the time goes in v3:
time: 172 us; the launch traced here: 171 us
  starting transfers between devices  64.9 us (38%)
  waiting for transfers between devices  59.8 us (35%)
  Pallas kernels  39.8 us (23%)
  local copies, waits for them, and re-layouts  3.28 us (2%)
  other arithmetic  2.43 us (1%)
    ppermute x55, starting transfers between devices, along(): return lax.ppermute(x, axis, [(s, s ^ mask) for s in range(n)])  64.9 us
    ppermute x55, waiting for transfers between devices, along(): return lax.ppermute(x, axis, [(s, s ^ mask) for s in range(n)])  59.8 us
    pallas_call x18, Pallas kernels, call(): pl.pallas_call(body, name=name, cost_estimate=pl.CostEstimate(flops=int(m...  39.8 us
  transfers between devices with their start and end apart: 55, of which 26 were waited for; matrix products, arithmetic and copies ran while one was open for 1% of the time, Pallas kernels for 13%

profile of v3, /device:TPU:0, one launch (start us, length us, event | category | flops | bytes accessed | tf_op | source)
XLA Modules:
  0.0 171.3 jit_solution(12227189555139230050)
XLA Ops:
  2.0 3.0 %collective-permute-start.1 = (bf16[384,768]{1,0:T(8,128)(2,1)S(1)}, bf16[384,768]{1,0:T(8,128)(2,1)S(1)}, u32[]{:S(2)}, u32[]{:S(2)}) collective-permute-start(bf16[384,768]{1,0:T(8,128)(2,1)S(1)} %pad_maximum_fusion), channel_id=1, source_target_pairs={{0,16},{8,24},{16,0},{24,8},{1,17},{9,25},{17,1},{25,9},{2,18},{10... | collective-permute-start | bytes 1769480 | tf_op jit(solution)/shard_map/ppermute | solution.py:430
  5.0 1.5 collective-permute-start
  9.1 3.7 %collective-permute-start.6 = (bf16[40,768]{1,0:T(8,128)(2,1)S(1)}, bf16[40,768]{1,0:T(8,128)(2,1)S(1)}, u32[]{:S(2)}, u32[]{:S(2)}) collective-permute-start(bf16[40,768]{1,0:T(8,128)(2,1)S(1)} %get-tuple-element.207), channel_id=1, source_target_pairs={{0,6},{1,7},{2,4},{3,5},{4,2},{5,3},{6,0},{7,1},{8,14},{9,15},{10,... | collective-permute-start | bytes 184328 | tf_op jit(solution)/shard_map/ppermute | solution.py:430
  16.0 2.4 %collective-permute-done.5 = bf16[40,768]{1,0:T(8,128)(2,1)S(1)} collective-permute-done((bf16[40,768]{1,0:T(8,128)(2,1)S(1)}, bf16[40,768]{1,0:T(8,128)(2,1)S(1)}, u32[]{:S(2)}, u32[]{:S(2)}) %collective-permute-start.5) | collective-permute-done | bytes 61472 | tf_op jit(solution)/shard_map/ppermute | solution.py:430
  18.5 1.7 collective-permute-done.7.s1
  20.7 1.7 collective-permute-start.9
  22.9 6.1 %collective-permute-done.8.da = bf16[224,768]{1,0:T(8,128)(2,1)} collective-permute-done((bf16[224,768]{1,0:T(8,128)(2,1)S(1)}, bf16[224,768]{1,0:T(8,128)(2,1)}, u32[]{:S(2)}, u32[]{:S(2)}) %collective-permute-start.8) | collective-permute-done | bytes 344096 | tf_op jit(solution)/shard_map/ppermute | solution.py:430
  29.8 1.7 collective-permute-done.13.tb
  32.4 7.3 %attend.1 = (bf16[4,768,768]{2,1,0:T(8,128)(2,1)S(1)}, f32[32,768]{1,0:T(8,128)S(1)}, bf16[128,768]{1,0:T(8,128)(2,1)S(1)}, bf16[128,768]{1,0:T(8,128)(2,1)S(1)}...) custom-call(s32[4]{0:T(128)S(1)} %pad_add_fusion.1.idx, ...), custom_call_target="tpu_custom_call" | custom-call | flops 7699999744 | bytes 7000000 | tf_op jit(solution)/shard_map/attend/pallas_call | solution.py:43
  39.9 1.5 collective-permute-start.16
  42.3 3.7 %collective-permute-start.20 = (bf16[40,896]{1,0:T(8,128)(2,1)S(1)}, bf16[40,896]{1,0:T(8,128)(2,1)S(1)}, u32[]{:S(2)}, u32[]{:S(2)}) collective-permute-start(bf16[40,896]{1,0:T(8,128)(2,1)S(1)} %get-tuple-element.199), channel_id=1, source_target_pairs={{0,6},{1,7},{2,4},{3,5},{4,2},{5,3},{6,0},{7,1},{8,14},{9,15},{10,... | collective-permute-start | bytes 215048 | tf_op jit(solution)/shard_map/ppermute | solution.py:430
  46.7 1.5 collective-permute-start.15
  50.2 2.0 %collective-permute-done.19 = bf16[40,896]{1,0:T(8,128)(2,1)S(1)} collective-permute-done((bf16[40,896]{1,0:T(8,128)(2,1)S(1)}, bf16[40,896]{1,0:T(8,128)(2,1)S(1)}, u32[]{:S(2)}, u32[]{:S(2)}) %collective-permute-start.19) | collective-permute-done | bytes 71712 | tf_op jit(solution)/shard_map/ppermute | solution.py:430
  52.3 1.6 collective-permute-start.23
  53.8 1.4 collective-permute-start.22
  57.0 4.1 %collective-permute-start.25 = (bf16[128,768]{1,0:T(8,128)(2,1)S(1)}, bf16[128,768]{1,0:T(8,128)(2,1)S(1)}, u32[]{:S(2)}, u32[]{:S(2)}) collective-permute-start(bf16[128,768]{1,0:T(8,128)(2,1)S(1)} %get-tuple-element.122), channel_id=1, source_target_pairs={{0,4},{1,5},{2,6},{3,7},{4,0},{5,1},{6,2},{7,3},{8,12},{9,13},{10,... | collective-permute-start | bytes 589832 | tf_op jit(solution)/shard_map/ppermute | solution.py:430
  61.1 2.2 %g_back.1.g_all = f32[4,160,768]{2,1,0:T(8,128)S(1)} custom-call(s32[4]{0:T(128)S(1)} %pad_add_fusion.1.idx, bf16[768,768]{1,0:T(8,128)(2,1)S(1)} %bitcast.21, bf16[160,768]{1,0:T(8,128)(2,1)S(1)} %pad_maximum_fusion.3.refs_0_.g0, bf16[160,768]{1,0:T(8,128)(2,1)S(1)} %collective-permute-done.14.refs_1_.g1, ...), custom_call_target="tpu_custom_call" | custom-call | flops 2200000000 | bytes 2000000 | tf_op jit(solution)/shard_map/g_back/pallas_call | solution.py:43
  63.5 3.2 %collective-permute-done.25.l2 = bf16[128,768]{1,0:T(8,128)(2,1)S(1)} collective-permute-done((bf16[128,768]{1,0:T(8,128)(2,1)S(1)}, bf16[128,768]{1,0:T(8,128)(2,1)S(1)}, u32[]{:S(2)}, u32[]{:S(2)}) %collective-permute-start.25) | collective-permute-done | bytes 196640 | tf_op jit(solution)/shard_map/ppermute | solution.py:430
  67.8 3.8 %expert.1 = (bf16[160,896]{1,0:T(8,128)(2,1)S(1)}, bf16[160,896]{1,0:T(8,128)(2,1)S(1)}, bf16[160,896]{1,0:T(8,128)(2,1)S(1)}, bf16[160,896]{1,0:T(8,128)(2,1)S(...) custom-call(s32[4]{0:T(128)S(1)} %pad_add_fusion.1.idx, bf16[768,768]{1,0:T(8,128)(2,1)S(1)} %bitcast.20, ...), custom_call_target="tpu_custom_call" | custom-call | flops 4400000000 | bytes 4000000 | tf_op jit(solution)/shard_map/expert/pallas_call | solution.py:43
  71.5 1.5 collective-permute-start.26
  73.6 1.5 collective-permute-start.28
  75.1 3.6 %collective-permute-start.29 = (bf16[128,768]{1,0:T(8,128)(2,1)S(1)}, bf16[128,768]{1,0:T(8,128)(2,1)S(1)}, u32[]{:S(2)}, u32[]{:S(2)}) collective-permute-start(bf16[128,768]{1,0:T(8,128)(2,1)S(1)} %get-tuple-element.136), channel_id=1, source_target_pairs={{0,6},{1,7},{2,4},{3,5},{4,2},{5,3},{6,0},{7,1},{8,14},{9,15},{10,... | collective-permute-start | bytes 589832 | tf_op jit(solution)/shard_map/ppermute | solution.py:430
  78.7 2.6 %collective-permute-done.26.b = bf16[160,896]{1,0:T(8,128)(2,1)S(1)} collective-permute-done((bf16[160,896]{1,0:T(8,128)(2,1)S(1)}, bf16[160,896]{1,0:T(8,128)(2,1)S(1)}, u32[]{:S(2)}, u32[]{:S(2)}) %collective-permute-start.26) | collective-permute-done | bytes 286752 | tf_op jit(solution)/shard_map/ppermute | solution.py:430
  81.4 6.3 %collective-permute-done.27.c = bf16[160,896]{1,0:T(8,128)(2,1)S(1)} collective-permute-done((bf16[160,896]{1,0:T(8,128)(2,1)S(1)}, bf16[160,896]{1,0:T(8,128)(2,1)S(1)}, u32[]{:S(2)}, u32[]{:S(2)}) %collective-permute-start.27) | collective-permute-done | bytes 286752 | tf_op jit(solution)/shard_map/ppermute | solution.py:430
  88.3 1.7 %collective-permute-start.32 = (bf16[40,896]{1,0:T(8,128)(2,1)S(1)}, bf16[40,896]{1,0:T(8,128)(2,1)S(1)}, u32[]{:S(2)}, u32[]{:S(2)}) collective-permute-start(bf16[40,896]{1,0:T(8,128)(2,1)S(1)} %get-tuple-element.195), channel_id=1, source_target_pairs={{0,6},{1,7},{2,4},{3,5},{4,2},{5,3},{6,0},{7,1},{8,14},{9,15},{10,... | collective-permute-start | bytes 215048 | tf_op jit(solution)/shard_map/ppermute | solution.py:430
  90.1 2.7 %collective-permute-start.30 = (bf16[40,896]{1,0:T(8,128)(2,1)S(1)}, bf16[40,896]{1,0:T(8,128)(2,1)S(1)}, u32[]{:S(2)}, u32[]{:S(2)}) collective-permute-start(bf16[40,896]{1,0:T(8,128)(2,1)S(1)} %get-tuple-element.197), channel_id=1, source_target_pairs={{0,2},{1,3},{2,0},{3,1},{4,6},{5,7},{6,4},{7,5},{8,10},{9,11},{10,... | collective-permute-start | bytes 215048 | tf_op jit(solution)/shard_map/ppermute | solution.py:430
  92.8 2.0 %collective-permute-done.32 = bf16[40,896]{1,0:T(8,128)(2,1)S(1)} collective-permute-done((bf16[40,896]{1,0:T(8,128)(2,1)S(1)}, bf16[40,896]{1,0:T(8,128)(2,1)S(1)}, u32[]{:S(2)}, u32[]{:S(2)}) %collective-permute-start.32) | collective-permute-done | bytes 71712 | tf_op jit(solution)/shard_map/ppermute | solution.py:430
  94.8 1.5 collective-permute-done.31
  97.2 1.5 expert_out.1
  99.5 1.4 collective-permute-start.35
  102.3 5.2 %attend_back.1 = (f32[128,768]{1,0:T(8,128)S(1)}, bf16[4,128,768]{2,1,0:T(8,128)(2,1)S(1)}, f32[8,768]{1,0:T(8,128)S(1)}, f32[1,768]{1,0:T(1,128)S(1)}, f32[12,1...) custom-call(s32[4]{0:T(128)S(1)} %pad_add_fusion.1.idx, ...), custom_call_target="tpu_custom_call" | custom-call | flops 6049999872 | bytes 5500000 | tf_op jit(solution)/shard_map/attend_back/pallas_call | solution.py:43
  108.4 1.8 %collective-permute-start.38 = (bf16[128,768]{1,0:T(8,128)(2,1)S(1)}, bf16[128,768]{1,0:T(8,128)(2,1)S(1)}, u32[]{:S(2)}, u32[]{:S(2)}) collective-permute-start(bf16[128,768]{1,0:T(8,128)(2,1)S(1)} %get-tuple-element.161), channel_id=1, source_target_pairs={{0,4},{1,5},{2,6},{3,7},{4,0},{5,1},{6,2},{7,3},{8,12},{9,13},{10,... | collective-permute-start | bytes 589832 | tf_op jit(solution)/shard_map/ppermute | solution.py:430
  110.3 1.7 collective-permute-start.39
  113.5 2.7 %token_grad.1 = (f32[128,768]{1,0:T(8,128)}, bf16[32,768]{1,0:T(8,128)(2,1)S(1)}, bf16[32,128]{1,0:T(8,128)(2,1)S(1)}) custom-call(s32[4]{0:T(128)S(1)} %pad_add_fusion.1.idx, bf16[128,768]{1,0:T(8,128)(2,1)S(1)} %copy-done.10, f32[128,768]{1,0:T(8,128)S(1)} %get-tuple-element.147.dmixed, bf16[4,128,768]{2,1,0:T(8,128)(2,1)S(1)} %get-tuple-element.153.d, ...), custom_call_target="tpu_custom_call" | custom-call | flops 3300000000 | bytes 3000000 | tf_op jit(solution)/shard_map/token_grad/pallas_call | solution.py:43
  117.0 8.6 %collective-permute-done.38.d2 = bf16[128,768]{1,0:T(8,128)(2,1)S(1)} collective-permute-done((bf16[128,768]{1,0:T(8,128)(2,1)S(1)}, bf16[128,768]{1,0:T(8,128)(2,1)S(1)}, u32[]{:S(2)}, u32[]{:S(2)}) %collective-permute-start.38) | collective-permute-done | bytes 196640 | tf_op jit(solution)/shard_map/ppermute | solution.py:430
  125.6 2.0 %mixer_grad.1 = (f32[768,384]{1,0:T(8,128)S(1)}, bf16[768,384]{1,0:T(8,128)(2,1)S(1)}) custom-call(s32[4]{0:T(128)S(1)} %pad_add_fusion.1.idx, f32[32,768]{1,0:T(8,128)S(1)} %get-tuple-element.158.small_all, bf16[128,768]{1,0:T(8,128)(2,1)S(1)} %get-tuple-element.134.l0, bf16[128,768]{1,0:T(8,128)(2,1)S(1)} %collective-permute-done.24.l1, ...), custom_call_target="tpu_custom_call" | custom-call | flops 2200000000 | bytes 2000000 | tf_op jit(solution)/shard_map/mixer_grad/pallas_call | solution.py:43
  127.7 2.0 %collective-permute-done.40.got = bf16[768,384]{1,0:T(8,128)(2,1)S(1)} collective-permute-done((bf16[768,384]{1,0:T(8,128)(2,1)S(1)}, bf16[768,384]{1,0:T(8,128)(2,1)S(1)}, u32[]{:S(2)}, u32[]{:S(2)}) %collective-permute-start.40) | collective-permute-done | bytes 589856 | tf_op jit(solution)/shard_map/ppermute | solution.py:430
  131.3 1.6 collective-permute-start.42
  133.0 1.5 collective-permute-start.43
  134.5 3.7 %collective-permute-done.41.b = bf16[224,384]{1,0:T(8,128)(2,1)S(1)} collective-permute-done((bf16[224,384]{1,0:T(8,128)(2,1)S(1)}, bf16[224,384]{1,0:T(8,128)(2,1)S(1)}, u32[]{:S(2)}, u32[]{:S(2)}) %collective-permute-start.41) | collective-permute-done | bytes 172064 | tf_op jit(solution)/shard_map/ppermute | solution.py:430
  138.2 3.0 %collective-permute-done.42.c = bf16[224,384]{1,0:T(8,128)(2,1)S(1)} collective-permute-done((bf16[224,384]{1,0:T(8,128)(2,1)S(1)}, bf16[224,384]{1,0:T(8,128)(2,1)S(1)}, u32[]{:S(2)}, u32[]{:S(2)}) %collective-permute-start.42) | collective-permute-done | bytes 172064 | tf_op jit(solution)/shard_map/ppermute | solution.py:430
  141.8 2.4 %collective-permute-start.46 = (bf16[40,768]{1,0:T(8,128)(2,1)S(1)}, bf16[40,768]{1,0:T(8,128)(2,1)S(1)}, u32[]{:S(2)}, u32[]{:S(2)}) collective-permute-start(bf16[40,768]{1,0:T(8,128)(2,1)S(1)} %get-tuple-element.203), channel_id=1, source_target_pairs={{0,6},{1,7},{2,4},{3,5},{4,2},{5,3},{6,0},{7,1},{8,14},{9,15},{10,... | collective-permute-start | bytes 184328 | tf_op jit(solution)/shard_map/ppermute | solution.py:430
  144.2 2.3 %collective-permute-start.45 = (bf16[40,768]{1,0:T(8,128)(2,1)S(1)}, bf16[40,768]{1,0:T(8,128)(2,1)S(1)}, u32[]{:S(2)}, u32[]{:S(2)}) collective-permute-start(bf16[40,768]{1,0:T(8,128)(2,1)S(1)} %get-tuple-element.204), channel_id=1, source_target_pairs={{0,4},{1,5},{2,6},{3,7},{4,0},{5,1},{6,2},{7,3},{8,12},{9,13},{10,... | collective-permute-start | bytes 184328 | tf_op jit(solution)/shard_map/ppermute | solution.py:430
  147.1 2.4 %collective-permute-start.50 = (bf16[224,384]{1,0:T(8,128)(2,1)S(1)}, bf16[224,384]{1,0:T(8,128)(2,1)S(1)}, u32[]{:S(2)}, u32[]{:S(2)}) collective-permute-start(bf16[224,384]{1,0:T(8,128)(2,1)S(1)} %sum_share.1.a0), channel_id=1, source_target_pairs={{0,6},{1,7},{2,4},{3,5},{4,2},{5,3},{6,0},{7,1},{8,14},{9,15},{10,... | collective-permute-start | bytes 516104 | tf_op jit(solution)/shard_map/ppermute | solution.py:430
  151.5 5.7 %collective-permute-done.45 = bf16[40,768]{1,0:T(8,128)(2,1)S(1)} collective-permute-done((bf16[40,768]{1,0:T(8,128)(2,1)S(1)}, bf16[40,768]{1,0:T(8,128)(2,1)S(1)}, u32[]{:S(2)}, u32[]{:S(2)}) %collective-permute-start.45) | collective-permute-done | bytes 61472 | tf_op jit(solution)/shard_map/ppermute | solution.py:430
  158.2 5.5 %expert_grad.1 = (f32[1,768,768]{2,1,0:T(8,128)}, f32[1,768,768]{2,1,0:T(8,128)}) custom-call(s32[4]{0:T(128)S(1)} %pad_add_fusion.1.idx, bf16[4,160,768]{2,1,0:T(8,128)(2,1)S(1)} %get-tuple-element.124.hid, bf16[4,160,768]{2,1,0:T(8,128)(2,1)S(1)} %get-tuple-element.179.dpre, bf16[160,896]{1,0:T(8,128)(2,1)S(1)} %pad_maximum_fusion.1.x0, ...), custom_call_target="tpu_custom_call" | custom-call | flops 6049999872 | bytes 5500000 | tf_op jit(solution)/shard_map/expert_grad/pallas_call | solution.py:43
  164.2 1.4 collective-permute-done.49.a2
  167.2 2.2 %finish.1 = (f32[192,768]{1,0:T(8,128)}, f32[192,768]{1,0:T(8,128)}, f32[192,768]{1,0:T(8,128)}, f32[192,768]{1,0:T(8,128)}, f32[32,384]{1,0:T(8,128)S(1)}) custom-call(s32[4]{0:T(128)S(1)} %pad_add_fusion.1.idx, bf16[224,384]{1,0:T(8,128)(2,1)S(1)} %sum_share.1.a0, bf16[224,384]{1,0:T(8,128)(2,1)S(1)} %collective-permute-done.48.a1, ...), custom_call_target="tpu_custom_call" | custom-call | flops 2200000000 | bytes 2000000 | tf_op jit(solution)/shard_map/finish/pallas_call | solution.py:43
  (142 shorter events, 34.3 us)
Async XLA Ops:
  2.0 18.2 %collective-permute-start.1 = (bf16[384,768]{1,0:T(8,128)(2,1)S(1)}, bf16[384,768]{1,0:T(8,128)(2,1)S(1)}, u32[]{:S(2)}, u32[]{:S(2)}) collective-permute-start(bf16[384,768]{1,0:T(8,128)(2,1)S(1)} %pad_maximum_fusion), channel_id=1, source_target_pairs={{0,16},{8,24},{16,0},{24,8},{1,17},{9,25},{17,1},{25,9},{2,18},{10... | collective-permute-start | bytes 1769480 | tf_op jit(solution)/shard_map/ppermute | solution.py:430
  5.0 15.2 %collective-permute-start = (bf16[384,768]{1,0:T(8,128)(2,1)S(1)}, bf16[384,768]{1,0:T(8,128)(2,1)S(1)}, u32[]{:S(2)}, u32[]{:S(2)}) collective-permute-start(bf16[384,768]{1,0:T(8,128)(2,1)S(1)} %pad_maximum_fusion), channel_id=1, source_target_pairs={{0,8},{8,0},{16,24},{24,16},{1,9},{9,1},{17,25},{25,17},{2,10},{10... | collective-permute-start | bytes 1769480 | tf_op jit(solution)/shard_map/ppermute | solution.py:430
  9.1 6.4 %collective-permute-start.6 = (bf16[40,768]{1,0:T(8,128)(2,1)S(1)}, bf16[40,768]{1,0:T(8,128)(2,1)S(1)}, u32[]{:S(2)}, u32[]{:S(2)}) collective-permute-start(bf16[40,768]{1,0:T(8,128)(2,1)S(1)} %get-tuple-element.207), channel_id=1, source_target_pairs={{0,6},{1,7},{2,4},{3,5},{4,2},{5,3},{6,0},{7,1},{8,14},{9,15},{10,... | collective-permute-start | bytes 184328 | tf_op jit(solution)/shard_map/ppermute | solution.py:430
  12.8 5.6 %collective-permute-start.5 = (bf16[40,768]{1,0:T(8,128)(2,1)S(1)}, bf16[40,768]{1,0:T(8,128)(2,1)S(1)}, u32[]{:S(2)}, u32[]{:S(2)}) collective-permute-start(bf16[40,768]{1,0:T(8,128)(2,1)S(1)} %get-tuple-element.208), channel_id=1, source_target_pairs={{0,4},{1,5},{2,6},{3,7},{4,0},{5,1},{6,2},{7,3},{8,12},{9,13},{10,... | collective-permute-start | bytes 184328 | tf_op jit(solution)/shard_map/ppermute | solution.py:430
  12.8 5.6 %collective-permute-start.4 = (bf16[40,768]{1,0:T(8,128)(2,1)S(1)}, bf16[40,768]{1,0:T(8,128)(2,1)S(1)}, u32[]{:S(2)}, u32[]{:S(2)}) collective-permute-start(bf16[40,768]{1,0:T(8,128)(2,1)S(1)} %get-tuple-element.209), channel_id=1, source_target_pairs={{0,2},{1,3},{2,0},{3,1},{4,6},{5,7},{6,4},{7,5},{8,10},{9,11},{10,... | collective-permute-start | bytes 184328 | tf_op jit(solution)/shard_map/ppermute | solution.py:430
  15.5 4.7 %collective-permute-start.7 = (bf16[32,256]{1,0:T(8,128)(2,1)S(1)}, bf16[32,256]{1,0:T(8,128)(2,1)S(1)}, u32[]{:S(2)}, u32[]{:S(2)}) collective-permute-start(bf16[32,256]{1,0:T(8,128)(2,1)S(1)} %pack.1.s0), channel_id=1, source_target_pairs={{0,8},{8,0},{16,24},{24,16},{1,9},{9,1},{17,25},{25,17},{2,10},{10... | collective-permute-start | bytes 49160 | tf_op jit(solution)/shard_map/ppermute | solution.py:430
  20.3 8.8 %collective-permute-start.8 = (bf16[224,768]{1,0:T(8,128)(2,1)S(1)}, bf16[224,768]{1,0:T(8,128)(2,1)}, u32[]{:S(2)}, u32[]{:S(2)}) collective-permute-start(bf16[224,768]{1,0:T(8,128)(2,1)S(1)} %maximum_maximum_fusion), channel_id=1, source_target_pairs={{0,16},{8,24},{16,0},{24,8},{1,17},{9,25},{17,1},{25,9},{2,18},{10... | collective-permute-start | bytes 1032200 | tf_op jit(solution)/shard_map/ppermute | solution.py:430
  20.7 8.3 %collective-permute-start.9 = (bf16[192,768]{1,0:T(8,128)(2,1)S(1)}, bf16[192,768]{1,0:T(8,128)(2,1)}, u32[]{:S(2)}, u32[]{:S(2)}) collective-permute-start(bf16[192,768]{1,0:T(8,128)(2,1)S(1)} %slice.71), channel_id=1, source_target_pairs={{0,8},{8,0},{16,24},{24,16},{1,9},{9,1},{17,25},{25,17},{2,10},{10... | collective-permute-start | bytes 884744 | tf_op jit(solution)/shard_map/ppermute | solution.py:430
  22.4 9.1 %collective-permute-start.10 = (bf16[384,768]{1,0:T(8,128)(2,1)S(1)}, bf16[384,768]{1,0:T(8,128)(2,1)S(1)}, u32[]{:S(2)}, u32[]{:S(2)}) collective-permute-start(bf16[384,768]{1,0:T(8,128)(2,1)S(1)} %collective-permute-done.hx), channel_id=1, source_target_pairs={{0,1},{1,0},{2,3},{3,2},{4,5},{5,4},{6,7},{7,6},{8,9},{9,8},{10,11... | collective-permute-start | bytes 1769480 | tf_op jit(solution)/shard_map/ppermute | solution.py:430
  22.4 9.1 %collective-permute-start.11 = (bf16[384,768]{1,0:T(8,128)(2,1)S(1)}, bf16[384,768]{1,0:T(8,128)(2,1)}, u32[]{:S(2)}, u32[]{:S(2)}) collective-permute-start(bf16[384,768]{1,0:T(8,128)(2,1)S(1)} %collective-permute-done.1.hy), channel_id=1, source_target_pairs={{0,1},{1,0},{2,3},{3,2},{4,5},{5,4},{6,7},{7,6},{8,9},{9,8},{10,11... | collective-permute-start | bytes 1769480 | tf_op jit(solution)/shard_map/ppermute | solution.py:430
  29.0 2.4 %collective-permute-start.12 = (bf16[224,768]{1,0:T(8,128)(2,1)}, bf16[224,768]{1,0:T(8,128)(2,1)}, u32[]{:S(2)}, u32[]{:S(2)}) collective-permute-start(bf16[224,768]{1,0:T(8,128)(2,1)} %collective-permute-done.8.da), channel_id=1, source_target_pairs={{0,1},{1,0},{2,3},{3,2},{4,5},{5,4},{6,7},{7,6},{8,9},{9,8},{10,11... | collective-permute-start | bytes 1032200 | tf_op jit(solution)/shard_map/ppermute | solution.py:430
  39.9 15.3 %collective-permute-start.16 = (bf16[160,768]{1,0:T(8,128)(2,1)S(1)}, bf16[160,768]{1,0:T(8,128)(2,1)S(1)}, u32[]{:S(2)}, u32[]{:S(2)}) collective-permute-start(bf16[160,768]{1,0:T(8,128)(2,1)S(1)} %pad_maximum_fusion.3.refs_0_.g0), channel_id=1, source_target_pairs={{0,24},{8,16},{16,8},{24,0},{1,25},{9,17},{17,9},{25,1},{2,26},{10... | collective-permute-start | bytes 737288 | tf_op jit(solution)/shard_map/ppermute | solution.py:430
  42.3 6.6 %collective-permute-start.20 = (bf16[40,896]{1,0:T(8,128)(2,1)S(1)}, bf16[40,896]{1,0:T(8,128)(2,1)S(1)}, u32[]{:S(2)}, u32[]{:S(2)}) collective-permute-start(bf16[40,896]{1,0:T(8,128)(2,1)S(1)} %get-tuple-element.199), channel_id=1, source_target_pairs={{0,6},{1,7},{2,4},{3,5},{4,2},{5,3},{6,0},{7,1},{8,14},{9,15},{10,... | collective-permute-start | bytes 215048 | tf_op jit(solution)/shard_map/ppermute | solution.py:430
  45.9 6.3 %collective-permute-start.19 = (bf16[40,896]{1,0:T(8,128)(2,1)S(1)}, bf16[40,896]{1,0:T(8,128)(2,1)S(1)}, u32[]{:S(2)}, u32[]{:S(2)}) collective-permute-start(bf16[40,896]{1,0:T(8,128)(2,1)S(1)} %get-tuple-element.200), channel_id=1, source_target_pairs={{0,4},{1,5},{2,6},{3,7},{4,0},{5,1},{6,2},{7,3},{8,12},{9,13},{10,... | collective-permute-start | bytes 215048 | tf_op jit(solution)/shard_map/ppermute | solution.py:430
  45.9 6.3 %collective-permute-start.18 = (bf16[40,896]{1,0:T(8,128)(2,1)S(1)}, bf16[40,896]{1,0:T(8,128)(2,1)S(1)}, u32[]{:S(2)}, u32[]{:S(2)}) collective-permute-start(bf16[40,896]{1,0:T(8,128)(2,1)S(1)} %get-tuple-element.201), channel_id=1, source_target_pairs={{0,2},{1,3},{2,0},{3,1},{4,6},{5,7},{6,4},{7,5},{8,10},{9,11},{10,... | collective-permute-start | bytes 215048 | tf_op jit(solution)/shard_map/ppermute | solution.py:430
  46.7 9.1 %collective-permute-start.15 = (bf16[160,768]{1,0:T(8,128)(2,1)S(1)}, bf16[160,768]{1,0:T(8,128)(2,1)S(1)}, u32[]{:S(2)}, u32[]{:S(2)}) collective-permute-start(bf16[160,768]{1,0:T(8,128)(2,1)S(1)} %pad_maximum_fusion.3.refs_0_.g0), channel_id=1, source_target_pairs={{0,16},{8,24},{16,0},{24,8},{1,17},{9,25},{17,1},{25,9},{2,18},{10... | collective-permute-start | bytes 737288 | tf_op jit(solution)/shard_map/ppermute | solution.py:430
  48.8 8.1 %collective-permute-start.14 = (bf16[160,768]{1,0:T(8,128)(2,1)S(1)}, bf16[160,768]{1,0:T(8,128)(2,1)S(1)}, u32[]{:S(2)}, u32[]{:S(2)}) collective-permute-start(bf16[160,768]{1,0:T(8,128)(2,1)S(1)} %pad_maximum_fusion.3.refs_0_.g0), channel_id=1, source_target_pairs={{0,8},{8,0},{16,24},{24,16},{1,9},{9,1},{17,25},{25,17},{2,10},{10... | collective-permute-start | bytes 737288 | tf_op jit(solution)/shard_map/ppermute | solution.py:430
  52.3 14.3 %collective-permute-start.23 = (bf16[160,896]{1,0:T(8,128)(2,1)S(1)}, bf16[160,896]{1,0:T(8,128)(2,1)S(1)}, u32[]{:S(2)}, u32[]{:S(2)}) collective-permute-start(bf16[160,896]{1,0:T(8,128)(2,1)S(1)} %pad_maximum_fusion.1.x0), channel_id=1, source_target_pairs={{0,24},{8,16},{16,8},{24,0},{1,25},{9,17},{17,9},{25,1},{2,26},{10... | collective-permute-start | bytes 860168 | tf_op jit(solution)/shard_map/ppermute | solution.py:430
  53.8 13.9 %collective-permute-start.22 = (bf16[160,896]{1,0:T(8,128)(2,1)S(1)}, bf16[160,896]{1,0:T(8,128)(2,1)S(1)}, u32[]{:S(2)}, u32[]{:S(2)}) collective-permute-start(bf16[160,896]{1,0:T(8,128)(2,1)S(1)} %pad_maximum_fusion.1.x0), channel_id=1, source_target_pairs={{0,16},{8,24},{16,0},{24,8},{1,17},{9,25},{17,1},{25,9},{2,18},{10... | collective-permute-start | bytes 860168 | tf_op jit(solution)/shard_map/ppermute | solution.py:430
  55.2 12.5 %collective-permute-start.21 = (bf16[160,896]{1,0:T(8,128)(2,1)S(1)}, bf16[160,896]{1,0:T(8,128)(2,1)S(1)}, u32[]{:S(2)}, u32[]{:S(2)}) collective-permute-start(bf16[160,896]{1,0:T(8,128)(2,1)S(1)} %pad_maximum_fusion.1.x0), channel_id=1, source_target_pairs={{0,8},{8,0},{16,24},{24,16},{1,9},{9,1},{17,25},{25,17},{2,10},{10... | collective-permute-start | bytes 860168 | tf_op jit(solution)/shard_map/ppermute | solution.py:430
  55.8 7.6 %collective-permute-start.24 = (bf16[128,768]{1,0:T(8,128)(2,1)S(1)}, bf16[128,768]{1,0:T(8,128)(2,1)S(1)}, u32[]{:S(2)}, u32[]{:S(2)}) collective-permute-start(bf16[128,768]{1,0:T(8,128)(2,1)S(1)} %get-tuple-element.120), channel_id=1, source_target_pairs={{0,2},{1,3},{2,0},{3,1},{4,6},{5,7},{6,4},{7,5},{8,10},{9,11},{10,... | collective-permute-start | bytes 589832 | tf_op jit(solution)/shard_map/ppermute | solution.py:430
  57.0 9.6 %collective-permute-start.25 = (bf16[128,768]{1,0:T(8,128)(2,1)S(1)}, bf16[128,768]{1,0:T(8,128)(2,1)S(1)}, u32[]{:S(2)}, u32[]{:S(2)}) collective-permute-start(bf16[128,768]{1,0:T(8,128)(2,1)S(1)} %get-tuple-element.122), channel_id=1, source_target_pairs={{0,4},{1,5},{2,6},{3,7},{4,0},{5,1},{6,2},{7,3},{8,12},{9,13},{10,... | collective-permute-start | bytes 589832 | tf_op jit(solution)/shard_map/ppermute | solution.py:430
  71.5 9.8 %collective-permute-start.26 = (bf16[160,896]{1,0:T(8,128)(2,1)S(1)}, bf16[160,896]{1,0:T(8,128)(2,1)S(1)}, u32[]{:S(2)}, u32[]{:S(2)}) collective-permute-start(bf16[160,896]{1,0:T(8,128)(2,1)S(1)} %get-tuple-element.130), channel_id=1, source_target_pairs={{0,8},{8,0},{16,24},{24,16},{1,9},{9,1},{17,25},{25,17},{2,10},{10... | collective-permute-start | bytes 860168 | tf_op jit(solution)/shard_map/ppermute | solution.py:430
  73.0 14.6 %collective-permute-start.27 = (bf16[160,896]{1,0:T(8,128)(2,1)S(1)}, bf16[160,896]{1,0:T(8,128)(2,1)S(1)}, u32[]{:S(2)}, u32[]{:S(2)}) collective-permute-start(bf16[160,896]{1,0:T(8,128)(2,1)S(1)} %get-tuple-element.131), channel_id=1, source_target_pairs={{0,16},{8,24},{16,0},{24,8},{1,17},{9,25},{17,1},{25,9},{2,18},{10... | collective-permute-start | bytes 860168 | tf_op jit(solution)/shard_map/ppermute | solution.py:430
  73.6 14.0 %collective-permute-start.28 = (bf16[160,896]{1,0:T(8,128)(2,1)S(1)}, bf16[160,896]{1,0:T(8,128)(2,1)S(1)}, u32[]{:S(2)}, u32[]{:S(2)}) collective-permute-start(bf16[160,896]{1,0:T(8,128)(2,1)S(1)} %get-tuple-element.132), channel_id=1, source_target_pairs={{0,24},{8,16},{16,8},{24,0},{1,25},{9,17},{17,9},{25,1},{2,26},{10... | collective-permute-start | bytes 860168 | tf_op jit(solution)/shard_map/ppermute | solution.py:430
  75.1 17.7 %collective-permute-start.29 = (bf16[128,768]{1,0:T(8,128)(2,1)S(1)}, bf16[128,768]{1,0:T(8,128)(2,1)S(1)}, u32[]{:S(2)}, u32[]{:S(2)}) collective-permute-start(bf16[128,768]{1,0:T(8,128)(2,1)S(1)} %get-tuple-element.136), channel_id=1, source_target_pairs={{0,6},{1,7},{2,4},{3,5},{4,2},{5,3},{6,0},{7,1},{8,14},{9,15},{10,... | collective-permute-start | bytes 589832 | tf_op jit(solution)/shard_map/ppermute | solution.py:430
  88.3 6.4 %collective-permute-start.32 = (bf16[40,896]{1,0:T(8,128)(2,1)S(1)}, bf16[40,896]{1,0:T(8,128)(2,1)S(1)}, u32[]{:S(2)}, u32[]{:S(2)}) collective-permute-start(bf16[40,896]{1,0:T(8,128)(2,1)S(1)} %get-tuple-element.195), channel_id=1, source_target_pairs={{0,6},{1,7},{2,4},{3,5},{4,2},{5,3},{6,0},{7,1},{8,14},{9,15},{10,... | collective-permute-start | bytes 215048 | tf_op jit(solution)/shard_map/ppermute | solution.py:430
  90.1 6.2 %collective-permute-start.31 = (bf16[40,896]{1,0:T(8,128)(2,1)S(1)}, bf16[40,896]{1,0:T(8,128)(2,1)S(1)}, u32[]{:S(2)}, u32[]{:S(2)}) collective-permute-start(bf16[40,896]{1,0:T(8,128)(2,1)S(1)} %get-tuple-element.196), channel_id=1, source_target_pairs={{0,4},{1,5},{2,6},{3,7},{4,0},{5,1},{6,2},{7,3},{8,12},{9,13},{10,... | collective-permute-start | bytes 215048 | tf_op jit(solution)/shard_map/ppermute | solution.py:430
  90.1 6.2 %collective-permute-start.30 = (bf16[40,896]{1,0:T(8,128)(2,1)S(1)}, bf16[40,896]{1,0:T(8,128)(2,1)S(1)}, u32[]{:S(2)}, u32[]{:S(2)}) collective-permute-start(bf16[40,896]{1,0:T(8,128)(2,1)S(1)} %get-tuple-element.197), channel_id=1, source_target_pairs={{0,2},{1,3},{2,0},{3,1},{4,6},{5,7},{6,4},{7,5},{8,10},{9,11},{10,... | collective-permute-start | bytes 215048 | tf_op jit(solution)/shard_map/ppermute | solution.py:430
  97.2 5.2 %collective-permute-start.33 = (bf16[128,896]{1,0:T(8,128)(2,1)S(1)}, bf16[128,896]{1,0:T(8,128)(2,1)S(1)}, u32[]{:S(2)}, u32[]{:S(2)}) collective-permute-start(bf16[128,896]{1,0:T(8,128)(2,1)S(1)} %get-tuple-element.139), channel_id=1, source_target_pairs={{0,1},{1,0},{2,3},{3,2},{4,5},{5,4},{6,7},{7,6},{8,9},{9,8},{10,11... | collective-permute-start | bytes 688136 | tf_op jit(solution)/shard_map/ppermute | solution.py:430
  98.8 11.5 %collective-permute-start.34 = (bf16[160,768]{1,0:T(8,128)(2,1)S(1)}, bf16[160,768]{1,0:T(8,128)(2,1)S(1)}, u32[]{:S(2)}, u32[]{:S(2)}) collective-permute-start(bf16[160,768]{1,0:T(8,128)(2,1)S(1)} %get-tuple-element.149), channel_id=1, source_target_pairs={{0,8},{8,0},{16,24},{24,16},{1,9},{9,1},{17,25},{25,17},{2,10},{10... | collective-permute-start | bytes 737288 | tf_op jit(solution)/shard_map/ppermute | solution.py:430
  99.5 13.3 %collective-permute-start.35 = (bf16[160,768]{1,0:T(8,128)(2,1)S(1)}, bf16[160,768]{1,0:T(8,128)(2,1)S(1)}, u32[]{:S(2)}, u32[]{:S(2)}) collective-permute-start(bf16[160,768]{1,0:T(8,128)(2,1)S(1)} %get-tuple-element.150), channel_id=1, source_target_pairs={{0,16},{8,24},{16,0},{24,8},{1,17},{9,25},{17,1},{25,9},{2,18},{10... | collective-permute-start | bytes 737288 | tf_op jit(solution)/shard_map/ppermute | solution.py:430
  101.0 11.9 %collective-permute-start.36 = (bf16[160,768]{1,0:T(8,128)(2,1)S(1)}, bf16[160,768]{1,0:T(8,128)(2,1)S(1)}, u32[]{:S(2)}, u32[]{:S(2)}) collective-permute-start(bf16[160,768]{1,0:T(8,128)(2,1)S(1)} %get-tuple-element.151), channel_id=1, source_target_pairs={{0,24},{8,16},{16,8},{24,0},{1,25},{9,17},{17,9},{25,1},{2,26},{10... | collective-permute-start | bytes 737288 | tf_op jit(solution)/shard_map/ppermute | solution.py:430
  107.5 9.5 %collective-permute-start.37 = (bf16[128,768]{1,0:T(8,128)(2,1)S(1)}, bf16[128,768]{1,0:T(8,128)(2,1)S(1)}, u32[]{:S(2)}, u32[]{:S(2)}) collective-permute-start(bf16[128,768]{1,0:T(8,128)(2,1)S(1)} %get-tuple-element.152), channel_id=1, source_target_pairs={{0,2},{1,3},{2,0},{3,1},{4,6},{5,7},{6,4},{7,5},{8,10},{9,11},{10,... | collective-permute-start | bytes 589832 | tf_op jit(solution)/shard_map/ppermute | solution.py:430
  108.4 17.2 %collective-permute-start.38 = (bf16[128,768]{1,0:T(8,128)(2,1)S(1)}, bf16[128,768]{1,0:T(8,128)(2,1)S(1)}, u32[]{:S(2)}, u32[]{:S(2)}) collective-permute-start(bf16[128,768]{1,0:T(8,128)(2,1)S(1)} %get-tuple-element.161), channel_id=1, source_target_pairs={{0,4},{1,5},{2,6},{3,7},{4,0},{5,1},{6,2},{7,3},{8,12},{9,13},{10,... | collective-permute-start | bytes 589832 | tf_op jit(solution)/shard_map/ppermute | solution.py:430
  110.3 15.3 %collective-permute-start.39 = (bf16[128,768]{1,0:T(8,128)(2,1)S(1)}, bf16[128,768]{1,0:T(8,128)(2,1)S(1)}, u32[]{:S(2)}, u32[]{:S(2)}) collective-permute-start(bf16[128,768]{1,0:T(8,128)(2,1)S(1)} %get-tuple-element.162), channel_id=1, source_target_pairs={{0,6},{1,7},{2,4},{3,5},{4,2},{5,3},{6,0},{7,1},{8,14},{9,15},{10,... | collective-permute-start | bytes 589832 | tf_op jit(solution)/shard_map/ppermute | solution.py:430
  130.9 7.3 %collective-permute-start.41 = (bf16[224,384]{1,0:T(8,128)(2,1)S(1)}, bf16[224,384]{1,0:T(8,128)(2,1)S(1)}, u32[]{:S(2)}, u32[]{:S(2)}) collective-permute-start(bf16[224,384]{1,0:T(8,128)(2,1)S(1)} %get-tuple-element.167), channel_id=1, source_target_pairs={{0,8},{8,0},{16,24},{24,16},{1,9},{9,1},{17,25},{25,17},{2,10},{10... | collective-permute-start | bytes 516104 | tf_op jit(solution)/shard_map/ppermute | solution.py:430
  131.3 9.8 %collective-permute-start.42 = (bf16[224,384]{1,0:T(8,128)(2,1)S(1)}, bf16[224,384]{1,0:T(8,128)(2,1)S(1)}, u32[]{:S(2)}, u32[]{:S(2)}) collective-permute-start(bf16[224,384]{1,0:T(8,128)(2,1)S(1)} %get-tuple-element.168), channel_id=1, source_target_pairs={{0,16},{8,24},{16,0},{24,8},{1,17},{9,25},{17,1},{25,9},{2,18},{10... | collective-permute-start | bytes 516104 | tf_op jit(solution)/shard_map/ppermute | solution.py:430
  133.0 8.2 %collective-permute-start.43 = (bf16[224,384]{1,0:T(8,128)(2,1)S(1)}, bf16[224,384]{1,0:T(8,128)(2,1)S(1)}, u32[]{:S(2)}, u32[]{:S(2)}) collective-permute-start(bf16[224,384]{1,0:T(8,128)(2,1)S(1)} %get-tuple-element.169), channel_id=1, source_target_pairs={{0,24},{8,16},{16,8},{24,0},{1,25},{9,17},{17,9},{25,1},{2,26},{10... | collective-permute-start | bytes 516104 | tf_op jit(solution)/shard_map/ppermute | solution.py:430
  141.8 8.4 %collective-permute-start.46 = (bf16[40,768]{1,0:T(8,128)(2,1)S(1)}, bf16[40,768]{1,0:T(8,128)(2,1)S(1)}, u32[]{:S(2)}, u32[]{:S(2)}) collective-permute-start(bf16[40,768]{1,0:T(8,128)(2,1)S(1)} %get-tuple-element.203), channel_id=1, source_target_pairs={{0,6},{1,7},{2,4},{3,5},{4,2},{5,3},{6,0},{7,1},{8,14},{9,15},{10,... | collective-permute-start | bytes 184328 | tf_op jit(solution)/shard_map/ppermute | solution.py:430
  144.2 13.0 %collective-permute-start.45 = (bf16[40,768]{1,0:T(8,128)(2,1)S(1)}, bf16[40,768]{1,0:T(8,128)(2,1)S(1)}, u32[]{:S(2)}, u32[]{:S(2)}) collective-permute-start(bf16[40,768]{1,0:T(8,128)(2,1)S(1)} %get-tuple-element.204), channel_id=1, source_target_pairs={{0,4},{1,5},{2,6},{3,7},{4,0},{5,1},{6,2},{7,3},{8,12},{9,13},{10,... | collective-permute-start | bytes 184328 | tf_op jit(solution)/shard_map/ppermute | solution.py:430
  146.5 10.7 %collective-permute-start.44 = (bf16[40,768]{1,0:T(8,128)(2,1)S(1)}, bf16[40,768]{1,0:T(8,128)(2,1)S(1)}, u32[]{:S(2)}, u32[]{:S(2)}) collective-permute-start(bf16[40,768]{1,0:T(8,128)(2,1)S(1)} %get-tuple-element.205), channel_id=1, source_target_pairs={{0,2},{1,3},{2,0},{3,1},{4,6},{5,7},{6,4},{7,5},{8,10},{9,11},{10,... | collective-permute-start | bytes 184328 | tf_op jit(solution)/shard_map/ppermute | solution.py:430
  147.1 17.1 %collective-permute-start.50 = (bf16[224,384]{1,0:T(8,128)(2,1)S(1)}, bf16[224,384]{1,0:T(8,128)(2,1)S(1)}, u32[]{:S(2)}, u32[]{:S(2)}) collective-permute-start(bf16[224,384]{1,0:T(8,128)(2,1)S(1)} %sum_share.1.a0), channel_id=1, source_target_pairs={{0,6},{1,7},{2,4},{3,5},{4,2},{5,3},{6,0},{7,1},{8,14},{9,15},{10,... | collective-permute-start | bytes 516104 | tf_op jit(solution)/shard_map/ppermute | solution.py:430
  149.5 16.1 %collective-permute-start.49 = (bf16[224,384]{1,0:T(8,128)(2,1)S(1)}, bf16[224,384]{1,0:T(8,128)(2,1)S(1)}, u32[]{:S(2)}, u32[]{:S(2)}) collective-permute-start(bf16[224,384]{1,0:T(8,128)(2,1)S(1)} %sum_share.1.a0), channel_id=1, source_target_pairs={{0,4},{1,5},{2,6},{3,7},{4,0},{5,1},{6,2},{7,3},{8,12},{9,13},{10,... | collective-permute-start | bytes 516104 | tf_op jit(solution)/shard_map/ppermute | solution.py:430
  150.2 15.3 %collective-permute-start.48 = (bf16[224,384]{1,0:T(8,128)(2,1)S(1)}, bf16[224,384]{1,0:T(8,128)(2,1)S(1)}, u32[]{:S(2)}, u32[]{:S(2)}) collective-permute-start(bf16[224,384]{1,0:T(8,128)(2,1)S(1)} %sum_share.1.a0), channel_id=1, source_target_pairs={{0,2},{1,3},{2,0},{3,1},{4,6},{5,7},{6,4},{7,5},{8,10},{9,11},{10,... | collective-permute-start | bytes 516104 | tf_op jit(solution)/shard_map/ppermute | solution.py:430
  158.1 8.0 %collective-permute-start.47 = (bf16[128,768]{1,0:T(8,128)(2,1)S(1)}, bf16[128,768]{1,0:T(8,128)(2,1)S(1)}, u32[]{:S(2)}, u32[]{:S(2)}) collective-permute-start(bf16[128,768]{1,0:T(8,128)(2,1)S(1)} %get-tuple-element.172), channel_id=1, source_target_pairs={{0,1},{1,0},{2,3},{3,2},{4,5},{5,4},{6,7},{7,6},{8,9},{9,8},{10,11... | collective-permute-start | bytes 589832 | tf_op jit(solution)/shard_map/ppermute | solution.py:430
  163.7 3.2 %collective-permute-start.51 = (bf16[224,384]{1,0:T(8,128)(2,1)S(1)}, bf16[224,384]{1,0:T(8,128)(2,1)S(1)}, u32[]{:S(2)}, u32[]{:S(2)}) collective-permute-start(bf16[224,384]{1,0:T(8,128)(2,1)S(1)} %sum_share.1.a0), channel_id=1, source_target_pairs={{0,1},{1,0},{2,3},{3,2},{4,5},{5,4},{6,7},{7,6},{8,9},{9,8},{10,11... | collective-permute-start | bytes 516104 | tf_op jit(solution)/shard_map/ppermute | solution.py:430
  164.2 2.7 %collective-permute-start.54 = (bf16[224,384]{1,0:T(8,128)(2,1)S(1)}, bf16[224,384]{1,0:T(8,128)(2,1)S(1)}, u32[]{:S(2)}, u32[]{:S(2)}) collective-permute-start(bf16[224,384]{1,0:T(8,128)(2,1)S(1)} %collective-permute-done.50.a3), channel_id=1, source_target_pairs={{0,1},{1,0},{2,3},{3,2},{4,5},{5,4},{6,7},{7,6},{8,9},{9,8},{10,11... | collective-permute-start | bytes 516104 | tf_op jit(solution)/shard_map/ppermute | solution.py:430
  (24 other events, 156.4 us)

commit v4 on v3

--- a/solution.py
+++ b/solution.py
@@ -194,12 +194,7 @@
     e = jnp.exp(logits - jnp.max(logits, axis=-1, keepdims=True))
     rp = e / jnp.sum(e, axis=-1, keepdims=True)
     rp_o[...] = rp
-    gate = jnp.sum(jnp.where(routes_c[...] == iota((length, experts), 1), rp, 0.0), axis=-1, keepdims=True)
-    hcat_o[:, 0:width] = h2
-    high = gate.astype(bf16).astype(f32)
-    lane = iota((length, 128), 1)
-    tail = jnp.where(lane == 0, high, jnp.where(lane == 1, gate - high, 0.0))
-    hcat_o[:, width : width + 128] = tail.astype(bf16)
+    hcat_o[...] = h2
     for zr, item in enumerate(left):
 
         @pl.when((idx[3] ^ zr) == owner_of[3])
@@ -216,13 +211,18 @@
         refs[4][k] = nt(refs[k][...], w_out[...])
 
 
-def expert_body(idx, w_in, g_all, x0, x1, x2, x3, y0, y1, y2, y3, hid_o, dpre_o):
+def expert_body(experts, idx, w_in, g_all, small_all, x0, x1, x2, x3, y0, y1, y2, y3, hid_o, dpre_o, gate_o):
     width = w_in.shape[0]
-    lane = iota((x0.shape[0], 128), 1)
+    slots = x0.shape[0]
+    lane = iota((slots, 128), 1)
+    wr_t = small_all[0:experts, :].astype(bf16)
+    mine = iota((slots, experts), 1) == idx[1]
     for k, (x, y) in enumerate(((x0, y0), (x1, y1), (x2, y2), (x3, y3))):
-        pre = nn(x[:, 0:width], w_in[...])
-        tail = x[:, width : width + 128].astype(f32)
-        gate = jnp.sum(jnp.where(lane < 2, tail, 0.0), axis=-1, keepdims=True)
+        pre = nn(x[...], w_in[...])
+        logits = nt(x[...], wr_t)
+        e = jnp.exp(logits - jnp.max(logits, axis=-1, keepdims=True))
+        gate = jnp.sum(jnp.where(mine, e, 0.0), axis=-1, keepdims=True) / jnp.sum(e, axis=-1, keepdims=True)
+        gate_o[k] = jnp.broadcast_to(gate, (slots, 128))
         sq = pre * pre
         t = jnp.tanh(gelu_a * (pre + gelu_b * sq * pre))
         hid = (0.5 * pre * (1.0 + t)).astype(bf16)
@@ -241,18 +241,15 @@
         y[...] = nn(hid[k], w_out[...]).astype(bf16)
 
 
-def expert_grad_body(idx, hid, dpre, x0, x1, x2, x3, g0, g1, g2, g3, gi, go):
+def expert_grad_body(idx, hid, dpre, gate, x0, x1, x2, x3, g0, g1, g2, g3, gi, go):
     width = gi.shape[1]
-    lane = iota((x0.shape[0], 128), 1)
     acc_i = jnp.zeros((width, dpre.shape[2]), f32)
     for k, x in enumerate((x0, x1, x2, x3)):
-        acc_i = acc_i + tn(x[:, 0:width], dpre[k])
+        acc_i = acc_i + tn(x[...], dpre[k])
     gi[0] = acc_i
     acc_o = jnp.zeros((hid.shape[2], width), f32)
-    for k, (x, g) in enumerate(((x0, g0), (x1, g1), (x2, g2), (x3, g3))):
-        tail = x[:, width : width + 128].astype(f32)
-        gate = jnp.sum(jnp.where(lane < 2, tail, 0.0), axis=-1, keepdims=True)
-        acc_o = acc_o + tn(hid[k], (gate * g[...].astype(f32)).astype(bf16))
+    for k, g in enumerate((g0, g1, g2, g3)):
+        acc_o = acc_o + tn(hid[k], (gate[k, :, 0:1] * g[...].astype(f32)).astype(bf16))
     go[0] = acc_o
 
 
@@ -390,7 +387,7 @@
     ).astype(bf16)
 
 
-def finish_body(idx, a0, a1, a2, a3, b0, b1, b2, b3, gq, gk, gv, go, small):
+def finish_body(experts, idx, a0, a1, a2, a3, b0, b1, b2, b3, gq, gk, gv, go, router_t, gain_a, gain_b, tab):
     z, core = idx[3], idx[2]
     half = a0.shape[1]
     rows = gq.shape[0]
@@ -404,10 +401,18 @@
                 out[:, pl.ds(at, half)] = a[0:rows, :].astype(f32)
                 out[:, pl.ds(off, half)] = b[0:rows, :].astype(f32)
 
-    total = jnp.zeros(small.shape, f32)
+    total = jnp.zeros((a0.shape[0] - rows, half), f32)
     for item in (a0, a1, a2, a3, b0, b1, b2, b3):
-        total = total + item[rows : rows + small.shape[0], :].astype(f32)
-    small[...] = total
+        total = total + item[rows:, :].astype(f32)
+    router_t[...] = total[0:experts, 0:rows]
+    gain_a[...] = total[experts : experts + 1, 0:rows]
+    gain_b[...] = total[experts + 1 : experts + 2, 0:rows]
+    shard, heads = tab.shape
+    lane = (iota((shard, half), 1) == iota((shard, half), 0) + rows).astype(f32)
+    line = (iota((heads, total.shape[0]), 1) == iota((heads, total.shape[0]), 0) + experts + 2).astype(f32)
+    dims = (((1,), (1,)), ((), ()))
+    turned = lax.dot_general(lane, total, dims, precision=lax.Precision.HIGHEST, preferred_element_type=f32)
+    tab[...] = lax.dot_general(turned, line, dims, precision=lax.Precision.HIGHEST, preferred_element_type=f32)
 
 
 def on_device(
@@ -472,8 +477,8 @@
     )
     seg_c, seg_r = seg.reshape(length, 1), seg.reshape(1, length)
     g_here = chip_exchange(g_rows)
-    hx, hy, place, g_here, seg_c, seg_r, route_c, small_own, small_x = lax.optimization_barrier(
-        (hx, hy, place, g_here, seg_c, seg_r, route_c, small_own, small_x)
+    hx, hy, place, g_here, seg_c, seg_r, route_c = lax.optimization_barrier(
+        (hx, hy, place, g_here, seg_c, seg_r, route_c)
     )
     tail = jnp.zeros((smalls, width - 512), bf16)
     tail = jnp.concatenate([small_own, small_x, tail], axis=1)
@@ -491,30 +496,30 @@
             ((4, width, width), bf16), ((smalls, width), f32),
             ((length, width), bf16), ((length, width), bf16), ((length, width), bf16),
             ((heads, length, length), f32), ((length, width), bf16), ((length, width), f32),
-            ((length, wide), bf16), ((length, experts), f32),
+            ((length, width), bf16), ((length, experts), f32),
         ]
         + ([((length, width), bf16)] * 4 if chips == 4 else []),
         idx, tokens, seg_c, seg_r, route_c,
         w_query, w_key, w_value, w_attn_out, small_own, small_x, hx, hy, da, db, tx, ty, ta, tb,
     )
 
-    x_rows = call("place_x", 1, place_rows_body, [((slots, wide), bf16)], idx, place, hcat, twin(hcat))[0]
+    x_rows = call("place_x", 1, place_rows_body, [((slots, width), bf16)], idx, place, hcat, twin(hcat))[0]
     x_here = chip_exchange(x_rows)
     x_set = [x_here] + [along(x_here, "dp", kk) for kk in (1, 2, 3)]
     if chips == 4:
         left = [left[0]] + [along(after(left[zr], x_here), "expert", 2 * zr) for zr in range(1, 4)]
         x_set[3] = after(x_set[3], left[1], left[2])
-    *d_parts, hid, dpre = call(
-        "expert", 4, expert_body,
-        [((slots, wide), bf16)] * 4 + [((4, slots, width), bf16)] * 2,
-        idx, weight_in, g_back, *x_set,
+    *d_parts, hid, dpre, gates = call(
+        "expert", 4, partial(expert_body, experts),
+        [((slots, wide), bf16)] * 4 + [((4, slots, width), bf16)] * 2 + [((4, slots, 128), f32)],
+        idx, weight_in, g_back, small_all, *x_set,
     )
     d_got = [d_parts[0]] + [along(d_parts[kk], "dp", kk) for kk in (1, 2, 3)]
     y_parts = call("expert_out", 1, expert_out_body, [((slots, width), bf16)] * 4, idx, weight_out, hid)
     grad_in, grad_out = call(
         "expert_grad", 5.5, expert_grad_body,
         [((1, width, weight_in.shape[1]), f32), ((1, weight_out.shape[0], width), f32)], idx,
-        hid, dpre, *x_set, *g_set,
+        hid, dpre, gates, *x_set, *g_set,
     )
     d_here = call("sum_d", 0.7, sum_body, [((slots, wide), bf16)], idx, *d_got)[0]
     y_parts = list(lax.optimization_barrier((*y_parts, d_here))[:-1])
@@ -562,7 +567,7 @@
         )
         got = [parts[0]] + [along(parts[kk], "dp", kk) for kk in (1, 2, 3)]
         total = call("sum_share", 0.7, sum_body, [((rows + smalls, width // 2), bf16)], idx, *got)[0]
-        y_here = after(y_here, total)
+        y_here = after(y_here, got[2])
     y_rows = chip_exchange(y_here)
     y_own, y_other = call(
         "unplace_y", 1, unplace_body, [((length, width), f32), ((length, width), bf16)], idx, place, y_rows
@@ -574,13 +579,13 @@
     if chips == 4:
         a_set = [total] + [along(total, "expert", 2 * zr) for zr in range(1, 4)]
         b_set = [twin(a) for a in a_set]
-        g_q, g_k, g_v, g_o, small_t = call(
-            "finish", 2, finish_body, [((rows, width), f32)] * 4 + [((smalls, width // 2), f32)], idx, *a_set, *b_set
+        g_q, g_k, g_v, g_o, r_out, gain1_out, gain2_out, table_out = call(
+            "finish", 2, partial(finish_body, experts),
+            [((rows, width), f32)] * 4
+            + [((experts, rows), f32), ((1, rows), f32), ((1, rows), f32), ((shard, heads), f32)],
+            idx, *a_set, *b_set,
         )
-        r_out = small_t[0:experts, 0:rows].T
-        gain1_out = small_t[experts, 0:rows]
-        gain2_out = small_t[experts + 1, 0:rows]
-        table_out = small_t[experts + 2 : experts + 2 + heads, rows : rows + shard].T
+        r_out, gain1_out, gain2_out = r_out.T, gain1_out[0], gain2_out[0]
     else:
         gain1 = small_all[experts : experts + 1]
         x = tokens.astype(f32)

time: 172 us -> 165 us (0.959)
  waiting for transfers between devices: 59.8 us -> 56.7 us
  starting transfers between devices: 64.9 us -> 62 us
  local copies, waits for them, and re-layouts: 3.28 us -> 1.36 us
    ppermute x55, waiting for transfers between devices: 59.8 us -> 56.7 us  [along(): return lax.ppermute(x, axis, [(s, s ^ mask) for s in range(n)])]
    ppermute x55, starting transfers between devices: 64.9 us -> 62 us  [along(): return lax.ppermute(x, axis, [(s, s ^ mask) for s in range(n)])]
  transfers between devices with their start and end apart: 55 -> 55, of which waited for: 26 -> 25; matrix products, arithmetic and copies ran while one was open for 1% -> 1% of each run, Pallas kernels for 13% -> 14%
where the time goes in v4:
time: 165 us; the launch traced here: 164 us
  starting transfers between devices  62 us (38%)
  waiting for transfers between devices  56.7 us (34%)
  Pallas kernels  40.8 us (25%)
  other arithmetic  2.42 us (1%)
    ppermute x55, starting transfers between devices, along(): return lax.ppermute(x, axis, [(s, s ^ mask) for s in range(n)])  62 us
    ppermute x55, waiting for transfers between devices, along(): return lax.ppermute(x, axis, [(s, s ^ mask) for s in range(n)])  56.7 us
    pallas_call x18, Pallas kernels, call(): pl.pallas_call(body, name=name, cost_estimate=pl.CostEstimate(flops=int(m...  40.8 us
  transfers between devices with their start and end apart: 55, of which 25 were waited for; matrix products, arithmetic and copies ran while one was open for 1% of the time, Pallas kernels for 14%

profile of v4, /device:TPU:0, one launch (start us, length us, event | category | flops | bytes accessed | tf_op | source)
XLA Modules:
  0.0 164.4 jit_solution(2694338185600034498)
XLA Ops:
  2.0 3.0 %collective-permute-start.1 = (bf16[384,768]{1,0:T(8,128)(2,1)S(1)}, bf16[384,768]{1,0:T(8,128)(2,1)S(1)}, u32[]{:S(2)}, u32[]{:S(2)}) collective-permute-start(bf16[384,768]{1,0:T(8,128)(2,1)S(1)} %pad_maximum_fusion), channel_id=1, source_target_pairs={{0,16},{8,24},{16,0},{24,8},{1,17},{9,25},{17,1},{25,9},{2,18},{10... | collective-permute-start | bytes 1769480 | tf_op jit(solution)/shard_map/ppermute | solution.py:435
  5.0 1.5 collective-permute-start
  9.1 3.7 %collective-permute-start.6 = (bf16[40,768]{1,0:T(8,128)(2,1)S(1)}, bf16[40,768]{1,0:T(8,128)(2,1)S(1)}, u32[]{:S(2)}, u32[]{:S(2)}) collective-permute-start(bf16[40,768]{1,0:T(8,128)(2,1)S(1)} %get-tuple-element.199), channel_id=1, source_target_pairs={{0,6},{1,7},{2,4},{3,5},{4,2},{5,3},{6,0},{7,1},{8,14},{9,15},{10,... | collective-permute-start | bytes 184328 | tf_op jit(solution)/shard_map/ppermute | solution.py:435
  16.0 2.4 %collective-permute-done.5 = bf16[40,768]{1,0:T(8,128)(2,1)S(1)} collective-permute-done((bf16[40,768]{1,0:T(8,128)(2,1)S(1)}, bf16[40,768]{1,0:T(8,128)(2,1)S(1)}, u32[]{:S(2)}, u32[]{:S(2)}) %collective-permute-start.5) | collective-permute-done | bytes 61472 | tf_op jit(solution)/shard_map/ppermute | solution.py:435
  18.5 1.5 collective-permute-done.hx
  20.7 1.7 %collective-permute-start.9 = (bf16[192,768]{1,0:T(8,128)(2,1)S(1)}, bf16[192,768]{1,0:T(8,128)(2,1)}, u32[]{:S(2)}, u32[]{:S(2)}) collective-permute-start(bf16[192,768]{1,0:T(8,128)(2,1)S(1)} %slice.59), channel_id=1, source_target_pairs={{0,8},{8,0},{16,24},{24,16},{1,9},{9,1},{17,25},{25,17},{2,10},{10... | collective-permute-start | bytes 884744 | tf_op jit(solution)/shard_map/ppermute | solution.py:435
  22.9 6.1 %collective-permute-done.8.da = bf16[224,768]{1,0:T(8,128)(2,1)} collective-permute-done((bf16[224,768]{1,0:T(8,128)(2,1)S(1)}, bf16[224,768]{1,0:T(8,128)(2,1)}, u32[]{:S(2)}, u32[]{:S(2)}) %collective-permute-start.8) | collective-permute-done | bytes 344096 | tf_op jit(solution)/shard_map/ppermute | solution.py:435
  29.7 1.7 %collective-permute-done.13.tb = bf16[192,768]{1,0:T(8,128)(2,1)} collective-permute-done((bf16[192,768]{1,0:T(8,128)(2,1)}, bf16[192,768]{1,0:T(8,128)(2,1)}, u32[]{:S(2)}, u32[]{:S(2)}) %collective-permute-start.13) | collective-permute-done | bytes 294944 | tf_op jit(solution)/shard_map/ppermute | solution.py:435
  32.4 7.2 %attend.1 = (bf16[4,768,768]{2,1,0:T(8,128)(2,1)S(1)}, f32[32,768]{1,0:T(8,128)S(1)}, bf16[128,768]{1,0:T(8,128)(2,1)S(1)}, bf16[128,768]{1,0:T(8,128)(2,1)S(1)}...) custom-call(s32[4]{0:T(128)S(1)} %pad_add_fusion.1.idx, ...), custom_call_target="tpu_custom_call" | custom-call | flops 7699999744 | bytes 7000000 | tf_op jit(solution)/shard_map/attend/pallas_call | solution.py:43
  39.8 1.4 collective-permute-start.16
  42.1 3.7 %collective-permute-start.20 = (bf16[40,768]{1,0:T(8,128)(2,1)S(1)}, bf16[40,768]{1,0:T(8,128)(2,1)S(1)}, u32[]{:S(2)}, u32[]{:S(2)}) collective-permute-start(bf16[40,768]{1,0:T(8,128)(2,1)S(1)} %get-tuple-element.195), channel_id=1, source_target_pairs={{0,6},{1,7},{2,4},{3,5},{4,2},{5,3},{6,0},{7,1},{8,14},{9,15},{10,... | collective-permute-start | bytes 184328 | tf_op jit(solution)/shard_map/ppermute | solution.py:435
  45.8 1.5 collective-permute-start.15
  49.2 3.8 %collective-permute-done.19 = bf16[40,768]{1,0:T(8,128)(2,1)S(1)} collective-permute-done((bf16[40,768]{1,0:T(8,128)(2,1)S(1)}, bf16[40,768]{1,0:T(8,128)(2,1)S(1)}, u32[]{:S(2)}, u32[]{:S(2)}) %collective-permute-start.19) | collective-permute-done | bytes 61472 | tf_op jit(solution)/shard_map/ppermute | solution.py:435
  53.2 1.6 collective-permute-start.23
  57.0 3.3 %collective-permute-start.25 = (bf16[128,768]{1,0:T(8,128)(2,1)S(1)}, bf16[128,768]{1,0:T(8,128)(2,1)S(1)}, u32[]{:S(2)}, u32[]{:S(2)}) collective-permute-start(bf16[128,768]{1,0:T(8,128)(2,1)S(1)} %get-tuple-element.123), channel_id=1, source_target_pairs={{0,4},{1,5},{2,6},{3,7},{4,0},{5,1},{6,2},{7,3},{8,12},{9,13},{10,... | collective-permute-start | bytes 589832 | tf_op jit(solution)/shard_map/ppermute | solution.py:435
  60.4 2.2 %g_back.1.g_all = f32[4,160,768]{2,1,0:T(8,128)S(1)} custom-call(s32[4]{0:T(128)S(1)} %pad_add_fusion.1.idx, bf16[768,768]{1,0:T(8,128)(2,1)S(1)} %bitcast.18, bf16[160,768]{1,0:T(8,128)(2,1)S(1)} %pad_maximum_fusion.2.refs_0_.g0, bf16[160,768]{1,0:T(8,128)(2,1)S(1)} %collective-permute-done.14.refs_1_.g1, ...), custom_call_target="tpu_custom_call" | custom-call | flops 2200000000 | bytes 2000000 | tf_op jit(solution)/shard_map/g_back/pallas_call | solution.py:43
  62.6 1.9 %collective-permute-done.24.l1 = bf16[128,768]{1,0:T(8,128)(2,1)S(1)} collective-permute-done((bf16[128,768]{1,0:T(8,128)(2,1)S(1)}, bf16[128,768]{1,0:T(8,128)(2,1)S(1)}, u32[]{:S(2)}, u32[]{:S(2)}) %collective-permute-start.24) | collective-permute-done | bytes 196640 | tf_op jit(solution)/shard_map/ppermute | solution.py:435
  64.5 3.4 %collective-permute-done.25.l2 = bf16[128,768]{1,0:T(8,128)(2,1)S(1)} collective-permute-done((bf16[128,768]{1,0:T(8,128)(2,1)S(1)}, bf16[128,768]{1,0:T(8,128)(2,1)S(1)}, u32[]{:S(2)}, u32[]{:S(2)}) %collective-permute-start.25) | collective-permute-done | bytes 196640 | tf_op jit(solution)/shard_map/ppermute | solution.py:435
  67.9 4.7 %expert.1 = (bf16[160,896]{1,0:T(8,128)(2,1)S(1)}, bf16[160,896]{1,0:T(8,128)(2,1)S(1)}, bf16[160,896]{1,0:T(8,128)(2,1)S(1)}, bf16[160,896]{1,0:T(8,128)(2,1)S(...) custom-call(s32[4]{0:T(128)S(1)} %pad_add_fusion.1.idx, ...), custom_call_target="tpu_custom_call" | custom-call | flops 4400000000 | bytes 4000000 | tf_op jit(solution)/shard_map/expert/pallas_call | solution.py:43
  72.6 1.6 collective-permute-start.26
  74.7 1.5 collective-permute-start.28
  76.1 2.2 %collective-permute-start.29 = (bf16[128,768]{1,0:T(8,128)(2,1)S(1)}, bf16[128,768]{1,0:T(8,128)(2,1)S(1)}, u32[]{:S(2)}, u32[]{:S(2)}) collective-permute-start(bf16[128,768]{1,0:T(8,128)(2,1)S(1)} %get-tuple-element.137), channel_id=1, source_target_pairs={{0,6},{1,7},{2,4},{3,5},{4,2},{5,3},{6,0},{7,1},{8,14},{9,15},{10,... | collective-permute-start | bytes 589832 | tf_op jit(solution)/shard_map/ppermute | solution.py:435
  78.3 2.7 %collective-permute-done.26.b = bf16[160,896]{1,0:T(8,128)(2,1)S(1)} collective-permute-done((bf16[160,896]{1,0:T(8,128)(2,1)S(1)}, bf16[160,896]{1,0:T(8,128)(2,1)S(1)}, u32[]{:S(2)}, u32[]{:S(2)}) %collective-permute-start.26) | collective-permute-done | bytes 286752 | tf_op jit(solution)/shard_map/ppermute | solution.py:435
  81.1 4.8 %collective-permute-done.27.c = bf16[160,896]{1,0:T(8,128)(2,1)S(1)} collective-permute-done((bf16[160,896]{1,0:T(8,128)(2,1)S(1)}, bf16[160,896]{1,0:T(8,128)(2,1)S(1)}, u32[]{:S(2)}, u32[]{:S(2)}) %collective-permute-start.27) | collective-permute-done | bytes 286752 | tf_op jit(solution)/shard_map/ppermute | solution.py:435
  86.6 3.3 %collective-permute-start.32 = (bf16[40,896]{1,0:T(8,128)(2,1)S(1)}, bf16[40,896]{1,0:T(8,128)(2,1)S(1)}, u32[]{:S(2)}, u32[]{:S(2)}) collective-permute-start(bf16[40,896]{1,0:T(8,128)(2,1)S(1)} %get-tuple-element.187), channel_id=1, source_target_pairs={{0,6},{1,7},{2,4},{3,5},{4,2},{5,3},{6,0},{7,1},{8,14},{9,15},{10,... | collective-permute-start | bytes 215048 | tf_op jit(solution)/shard_map/ppermute | solution.py:435
  91.1 2.3 %collective-permute-done.32 = bf16[40,896]{1,0:T(8,128)(2,1)S(1)} collective-permute-done((bf16[40,896]{1,0:T(8,128)(2,1)S(1)}, bf16[40,896]{1,0:T(8,128)(2,1)S(1)}, u32[]{:S(2)}, u32[]{:S(2)}) %collective-permute-start.32) | collective-permute-done | bytes 71712 | tf_op jit(solution)/shard_map/ppermute | solution.py:435
  93.4 1.8 %collective-permute-done.31 = bf16[40,896]{1,0:T(8,128)(2,1)S(1)} collective-permute-done((bf16[40,896]{1,0:T(8,128)(2,1)S(1)}, bf16[40,896]{1,0:T(8,128)(2,1)S(1)}, u32[]{:S(2)}, u32[]{:S(2)}) %collective-permute-start.31) | collective-permute-done | bytes 71712 | tf_op jit(solution)/shard_map/ppermute | solution.py:435
  96.2 1.5 expert_out.1
  97.9 1.7 %collective-permute-start.35 = (bf16[160,768]{1,0:T(8,128)(2,1)S(1)}, bf16[160,768]{1,0:T(8,128)(2,1)S(1)}, u32[]{:S(2)}, u32[]{:S(2)}) collective-permute-start(bf16[160,768]{1,0:T(8,128)(2,1)S(1)} %get-tuple-element.150), channel_id=1, source_target_pairs={{0,16},{8,24},{16,0},{24,8},{1,17},{9,25},{17,1},{25,9},{2,18},{10... | collective-permute-start | bytes 737288 | tf_op jit(solution)/shard_map/ppermute | solution.py:435
  99.6 1.6 collective-permute-start.36
  101.2 5.2 %attend_back.1 = (f32[128,768]{1,0:T(8,128)S(1)}, bf16[4,128,768]{2,1,0:T(8,128)(2,1)S(1)}, f32[8,768]{1,0:T(8,128)S(1)}, f32[1,768]{1,0:T(1,128)S(1)}, f32[12,1...) custom-call(s32[4]{0:T(128)S(1)} %pad_add_fusion.1.idx, ...), custom_call_target="tpu_custom_call" | custom-call | flops 6049999872 | bytes 5500000 | tf_op jit(solution)/shard_map/attend_back/pallas_call | solution.py:43
  107.1 2.0 %collective-permute-start.38 = (bf16[128,768]{1,0:T(8,128)(2,1)S(1)}, bf16[128,768]{1,0:T(8,128)(2,1)S(1)}, u32[]{:S(2)}, u32[]{:S(2)}) collective-permute-start(bf16[128,768]{1,0:T(8,128)(2,1)S(1)} %get-tuple-element.161), channel_id=1, source_target_pairs={{0,4},{1,5},{2,6},{3,7},{4,0},{5,1},{6,2},{7,3},{8,12},{9,13},{10,... | collective-permute-start | bytes 589832 | tf_op jit(solution)/shard_map/ppermute | solution.py:435
  109.2 1.7 %collective-permute-start.39 = (bf16[128,768]{1,0:T(8,128)(2,1)S(1)}, bf16[128,768]{1,0:T(8,128)(2,1)S(1)}, u32[]{:S(2)}, u32[]{:S(2)}) collective-permute-start(bf16[128,768]{1,0:T(8,128)(2,1)S(1)} %get-tuple-element.162), channel_id=1, source_target_pairs={{0,6},{1,7},{2,4},{3,5},{4,2},{5,3},{6,0},{7,1},{8,14},{9,15},{10,... | collective-permute-start | bytes 589832 | tf_op jit(solution)/shard_map/ppermute | solution.py:435
  112.1 2.7 %token_grad.1 = (f32[128,768]{1,0:T(8,128)}, bf16[32,768]{1,0:T(8,128)(2,1)S(1)}, bf16[32,128]{1,0:T(8,128)(2,1)S(1)}) custom-call(s32[4]{0:T(128)S(1)} %pad_add_fusion.1.idx, bf16[128,768]{1,0:T(8,128)(2,1)S(1)} %copy-done.10, f32[128,768]{1,0:T(8,128)S(1)} %get-tuple-element.147.dmixed, bf16[4,128,768]{2,1,0:T(8,128)(2,1)S(1)} %get-tuple-element.153.d, ...), custom_call_target="tpu_custom_call" | custom-call | flops 3300000000 | bytes 3000000 | tf_op jit(solution)/shard_map/token_grad/pallas_call | solution.py:43
  114.8 1.6 %collective-permute-done.37.d1 = bf16[128,768]{1,0:T(8,128)(2,1)S(1)} collective-permute-done((bf16[128,768]{1,0:T(8,128)(2,1)S(1)}, bf16[128,768]{1,0:T(8,128)(2,1)S(1)}, u32[]{:S(2)}, u32[]{:S(2)}) %collective-permute-start.37) | collective-permute-done | bytes 196640 | tf_op jit(solution)/shard_map/ppermute | solution.py:435
  116.5 7.8 %collective-permute-done.38.d2 = bf16[128,768]{1,0:T(8,128)(2,1)S(1)} collective-permute-done((bf16[128,768]{1,0:T(8,128)(2,1)S(1)}, bf16[128,768]{1,0:T(8,128)(2,1)S(1)}, u32[]{:S(2)}, u32[]{:S(2)}) %collective-permute-start.38) | collective-permute-done | bytes 196640 | tf_op jit(solution)/shard_map/ppermute | solution.py:435
  124.3 2.0 %mixer_grad.1 = (f32[768,384]{1,0:T(8,128)S(1)}, bf16[768,384]{1,0:T(8,128)(2,1)S(1)}) custom-call(s32[4]{0:T(128)S(1)} %pad_add_fusion.1.idx, f32[32,768]{1,0:T(8,128)S(1)} %get-tuple-element.158.small_all, bf16[128,768]{1,0:T(8,128)(2,1)S(1)} %get-tuple-element.135.l0, bf16[128,768]{1,0:T(8,128)(2,1)S(1)} %collective-permute-done.24.l1, ...), custom_call_target="tpu_custom_call" | custom-call | flops 2200000000 | bytes 2000000 | tf_op jit(solution)/shard_map/mixer_grad/pallas_call | solution.py:43
  126.4 2.0 %collective-permute-done.40.got = bf16[768,384]{1,0:T(8,128)(2,1)S(1)} collective-permute-done((bf16[768,384]{1,0:T(8,128)(2,1)S(1)}, bf16[768,384]{1,0:T(8,128)(2,1)S(1)}, u32[]{:S(2)}, u32[]{:S(2)}) %collective-permute-start.40) | collective-permute-done | bytes 589856 | tf_op jit(solution)/shard_map/ppermute | solution.py:435
  130.0 1.7 %collective-permute-start.46 = (bf16[224,384]{1,0:T(8,128)(2,1)S(1)}, bf16[224,384]{1,0:T(8,128)(2,1)S(1)}, u32[]{:S(2)}, u32[]{:S(2)}) collective-permute-start(bf16[224,384]{1,0:T(8,128)(2,1)S(1)} %get-tuple-element.172), channel_id=1, source_target_pairs={{0,8},{8,0},{16,24},{24,16},{1,9},{9,1},{17,25},{25,17},{2,10},{10... | collective-permute-start | bytes 516104 | tf_op jit(solution)/shard_map/ppermute | solution.py:435
  131.8 1.6 collective-permute-start.47
  133.4 2.7 %collective-permute-done.41.c = bf16[224,384]{1,0:T(8,128)(2,1)S(1)} collective-permute-done((bf16[224,384]{1,0:T(8,128)(2,1)S(1)}, bf16[224,384]{1,0:T(8,128)(2,1)S(1)}, u32[]{:S(2)}, u32[]{:S(2)}) %collective-permute-start.41) | collective-permute-done | bytes 172064 | tf_op jit(solution)/shard_map/ppermute | solution.py:435
  136.1 2.4 %collective-permute-start.44 = (bf16[40,768]{1,0:T(8,128)(2,1)S(1)}, bf16[40,768]{1,0:T(8,128)(2,1)S(1)}, u32[]{:S(2)}, u32[]{:S(2)}) collective-permute-start(bf16[40,768]{1,0:T(8,128)(2,1)S(1)} %get-tuple-element.191), channel_id=1, source_target_pairs={{0,6},{1,7},{2,4},{3,5},{4,2},{5,3},{6,0},{7,1},{8,14},{9,15},{10,... | collective-permute-start | bytes 184328 | tf_op jit(solution)/shard_map/ppermute | solution.py:435
  138.6 2.2 %collective-permute-start.43 = (bf16[40,768]{1,0:T(8,128)(2,1)S(1)}, bf16[40,768]{1,0:T(8,128)(2,1)S(1)}, u32[]{:S(2)}, u32[]{:S(2)}) collective-permute-start(bf16[40,768]{1,0:T(8,128)(2,1)S(1)} %get-tuple-element.192), channel_id=1, source_target_pairs={{0,4},{1,5},{2,6},{3,7},{4,0},{5,1},{6,2},{7,3},{8,12},{9,13},{10,... | collective-permute-start | bytes 184328 | tf_op jit(solution)/shard_map/ppermute | solution.py:435
  141.9 2.4 %collective-permute-start.50 = (bf16[224,384]{1,0:T(8,128)(2,1)S(1)}, bf16[224,384]{1,0:T(8,128)(2,1)S(1)}, u32[]{:S(2)}, u32[]{:S(2)}) collective-permute-start(bf16[224,384]{1,0:T(8,128)(2,1)S(1)} %sum_share.1.a0), channel_id=1, source_target_pairs={{0,6},{1,7},{2,4},{3,5},{4,2},{5,3},{6,0},{7,1},{8,14},{9,15},{10,... | collective-permute-start | bytes 516104 | tf_op jit(solution)/shard_map/ppermute | solution.py:435
  144.3 2.2 %collective-permute-start.49 = (bf16[224,384]{1,0:T(8,128)(2,1)S(1)}, bf16[224,384]{1,0:T(8,128)(2,1)S(1)}, u32[]{:S(2)}, u32[]{:S(2)}) collective-permute-start(bf16[224,384]{1,0:T(8,128)(2,1)S(1)} %sum_share.1.a0), channel_id=1, source_target_pairs={{0,4},{1,5},{2,6},{3,7},{4,0},{5,1},{6,2},{7,3},{8,12},{9,13},{10,... | collective-permute-start | bytes 516104 | tf_op jit(solution)/shard_map/ppermute | solution.py:435
  147.9 5.6 %expert_grad.1 = (f32[1,768,768]{2,1,0:T(8,128)}, f32[1,768,768]{2,1,0:T(8,128)}) custom-call(s32[4]{0:T(128)S(1)} %pad_add_fusion.1.idx, bf16[4,160,768]{2,1,0:T(8,128)(2,1)S(1)} %get-tuple-element.125.hid, bf16[4,160,768]{2,1,0:T(8,128)(2,1)S(1)} %get-tuple-element.182.dpre, f32[4,160,128]{2,1,0:T(8,128)S(1)} %get-tuple-element.183.gate, ...), custom_call_target="tpu_custom_call" | custom-call | flops 6049999872 | bytes 5500000 | tf_op jit(solution)/shard_map/expert_grad/pallas_call | solution.py:43
  154.0 6.5 %collective-permute-done.49.a2 = bf16[224,384]{1,0:T(8,128)(2,1)S(1)} collective-permute-done((bf16[224,384]{1,0:T(8,128)(2,1)S(1)}, bf16[224,384]{1,0:T(8,128)(2,1)S(1)}, u32[]{:S(2)}, u32[]{:S(2)}) %collective-permute-start.49) | collective-permute-done | bytes 172064 | tf_op jit(solution)/shard_map/ppermute | solution.py:435
  162.2 2.2 %finish.1 = (f32[192,768]{1,0:T(8,128)}, f32[192,768]{1,0:T(8,128)}, f32[192,768]{1,0:T(8,128)}, f32[192,768]{1,0:T(8,128)}, f32[8,192]{1,0:T(8,128)}, /*index=5...) custom-call(s32[4]{0:T(128)S(1)} %pad_add_fusion.1.idx, bf16[224,384]{1,0:T(8,128)(2,1)S(1)} %sum_share.1.a0, ...), custom_call_target="tpu_custom_call" | custom-call | flops 2200000000 | bytes 2000000 | tf_op jit(solution)/shard_map/finish/pallas_call | solution.py:43
  (138 shorter events, 27.3 us)
Async XLA Ops:
  2.0 16.5 %collective-permute-start.1 = (bf16[384,768]{1,0:T(8,128)(2,1)S(1)}, bf16[384,768]{1,0:T(8,128)(2,1)S(1)}, u32[]{:S(2)}, u32[]{:S(2)}) collective-permute-start(bf16[384,768]{1,0:T(8,128)(2,1)S(1)} %pad_maximum_fusion), channel_id=1, source_target_pairs={{0,16},{8,24},{16,0},{24,8},{1,17},{9,25},{17,1},{25,9},{2,18},{10... | collective-permute-start | bytes 1769480 | tf_op jit(solution)/shard_map/ppermute | solution.py:435
  5.0 15.0 %collective-permute-start = (bf16[384,768]{1,0:T(8,128)(2,1)S(1)}, bf16[384,768]{1,0:T(8,128)(2,1)S(1)}, u32[]{:S(2)}, u32[]{:S(2)}) collective-permute-start(bf16[384,768]{1,0:T(8,128)(2,1)S(1)} %pad_maximum_fusion), channel_id=1, source_target_pairs={{0,8},{8,0},{16,24},{24,16},{1,9},{9,1},{17,25},{25,17},{2,10},{10... | collective-permute-start | bytes 1769480 | tf_op jit(solution)/shard_map/ppermute | solution.py:435
  9.1 6.4 %collective-permute-start.6 = (bf16[40,768]{1,0:T(8,128)(2,1)S(1)}, bf16[40,768]{1,0:T(8,128)(2,1)S(1)}, u32[]{:S(2)}, u32[]{:S(2)}) collective-permute-start(bf16[40,768]{1,0:T(8,128)(2,1)S(1)} %get-tuple-element.199), channel_id=1, source_target_pairs={{0,6},{1,7},{2,4},{3,5},{4,2},{5,3},{6,0},{7,1},{8,14},{9,15},{10,... | collective-permute-start | bytes 184328 | tf_op jit(solution)/shard_map/ppermute | solution.py:435
  12.8 5.6 %collective-permute-start.5 = (bf16[40,768]{1,0:T(8,128)(2,1)S(1)}, bf16[40,768]{1,0:T(8,128)(2,1)S(1)}, u32[]{:S(2)}, u32[]{:S(2)}) collective-permute-start(bf16[40,768]{1,0:T(8,128)(2,1)S(1)} %get-tuple-element.200), channel_id=1, source_target_pairs={{0,4},{1,5},{2,6},{3,7},{4,0},{5,1},{6,2},{7,3},{8,12},{9,13},{10,... | collective-permute-start | bytes 184328 | tf_op jit(solution)/shard_map/ppermute | solution.py:435
  12.8 5.6 %collective-permute-start.4 = (bf16[40,768]{1,0:T(8,128)(2,1)S(1)}, bf16[40,768]{1,0:T(8,128)(2,1)S(1)}, u32[]{:S(2)}, u32[]{:S(2)}) collective-permute-start(bf16[40,768]{1,0:T(8,128)(2,1)S(1)} %get-tuple-element.201), channel_id=1, source_target_pairs={{0,2},{1,3},{2,0},{3,1},{4,6},{5,7},{6,4},{7,5},{8,10},{9,11},{10,... | collective-permute-start | bytes 184328 | tf_op jit(solution)/shard_map/ppermute | solution.py:435
  15.5 4.7 %collective-permute-start.7 = (bf16[32,256]{1,0:T(8,128)(2,1)S(1)}, bf16[32,256]{1,0:T(8,128)(2,1)S(1)}, u32[]{:S(2)}, u32[]{:S(2)}) collective-permute-start(bf16[32,256]{1,0:T(8,128)(2,1)S(1)} %pack.1.s0), channel_id=1, source_target_pairs={{0,8},{8,0},{16,24},{24,16},{1,9},{9,1},{17,25},{25,17},{2,10},{10... | collective-permute-start | bytes 49160 | tf_op jit(solution)/shard_map/ppermute | solution.py:435
  20.2 8.8 %collective-permute-start.8 = (bf16[224,768]{1,0:T(8,128)(2,1)S(1)}, bf16[224,768]{1,0:T(8,128)(2,1)}, u32[]{:S(2)}, u32[]{:S(2)}) collective-permute-start(bf16[224,768]{1,0:T(8,128)(2,1)S(1)} %maximum_maximum_fusion), channel_id=1, source_target_pairs={{0,16},{8,24},{16,0},{24,8},{1,17},{9,25},{17,1},{25,9},{2,18},{10... | collective-permute-start | bytes 1032200 | tf_op jit(solution)/shard_map/ppermute | solution.py:435
  20.7 8.3 %collective-permute-start.9 = (bf16[192,768]{1,0:T(8,128)(2,1)S(1)}, bf16[192,768]{1,0:T(8,128)(2,1)}, u32[]{:S(2)}, u32[]{:S(2)}) collective-permute-start(bf16[192,768]{1,0:T(8,128)(2,1)S(1)} %slice.59), channel_id=1, source_target_pairs={{0,8},{8,0},{16,24},{24,16},{1,9},{9,1},{17,25},{25,17},{2,10},{10... | collective-permute-start | bytes 884744 | tf_op jit(solution)/shard_map/ppermute | solution.py:435
  22.4 9.1 %collective-permute-start.10 = (bf16[384,768]{1,0:T(8,128)(2,1)S(1)}, bf16[384,768]{1,0:T(8,128)(2,1)S(1)}, u32[]{:S(2)}, u32[]{:S(2)}) collective-permute-start(bf16[384,768]{1,0:T(8,128)(2,1)S(1)} %collective-permute-done.hx), channel_id=1, source_target_pairs={{0,1},{1,0},{2,3},{3,2},{4,5},{5,4},{6,7},{7,6},{8,9},{9,8},{10,11... | collective-permute-start | bytes 1769480 | tf_op jit(solution)/shard_map/ppermute | solution.py:435
  22.4 9.1 %collective-permute-start.11 = (bf16[384,768]{1,0:T(8,128)(2,1)S(1)}, bf16[384,768]{1,0:T(8,128)(2,1)}, u32[]{:S(2)}, u32[]{:S(2)}) collective-permute-start(bf16[384,768]{1,0:T(8,128)(2,1)S(1)} %collective-permute-done.1.hy), channel_id=1, source_target_pairs={{0,1},{1,0},{2,3},{3,2},{4,5},{5,4},{6,7},{7,6},{8,9},{9,8},{10,11... | collective-permute-start | bytes 1769480 | tf_op jit(solution)/shard_map/ppermute | solution.py:435
  29.0 2.4 %collective-permute-start.12 = (bf16[224,768]{1,0:T(8,128)(2,1)}, bf16[224,768]{1,0:T(8,128)(2,1)}, u32[]{:S(2)}, u32[]{:S(2)}) collective-permute-start(bf16[224,768]{1,0:T(8,128)(2,1)} %collective-permute-done.8.da), channel_id=1, source_target_pairs={{0,1},{1,0},{2,3},{3,2},{4,5},{5,4},{6,7},{7,6},{8,9},{9,8},{10,11... | collective-permute-start | bytes 1032200 | tf_op jit(solution)/shard_map/ppermute | solution.py:435
  39.8 16.2 %collective-permute-start.16 = (bf16[160,768]{1,0:T(8,128)(2,1)S(1)}, bf16[160,768]{1,0:T(8,128)(2,1)S(1)}, u32[]{:S(2)}, u32[]{:S(2)}) collective-permute-start(bf16[160,768]{1,0:T(8,128)(2,1)S(1)} %pad_maximum_fusion.2.refs_0_.g0), channel_id=1, source_target_pairs={{0,24},{8,16},{16,8},{24,0},{1,25},{9,17},{17,9},{25,1},{2,26},{10... | collective-permute-start | bytes 737288 | tf_op jit(solution)/shard_map/ppermute | solution.py:435
  42.1 6.1 %collective-permute-start.20 = (bf16[40,768]{1,0:T(8,128)(2,1)S(1)}, bf16[40,768]{1,0:T(8,128)(2,1)S(1)}, u32[]{:S(2)}, u32[]{:S(2)}) collective-permute-start(bf16[40,768]{1,0:T(8,128)(2,1)S(1)} %get-tuple-element.195), channel_id=1, source_target_pairs={{0,6},{1,7},{2,4},{3,5},{4,2},{5,3},{6,0},{7,1},{8,14},{9,15},{10,... | collective-permute-start | bytes 184328 | tf_op jit(solution)/shard_map/ppermute | solution.py:435
  45.8 10.9 %collective-permute-start.15 = (bf16[160,768]{1,0:T(8,128)(2,1)S(1)}, bf16[160,768]{1,0:T(8,128)(2,1)S(1)}, u32[]{:S(2)}, u32[]{:S(2)}) collective-permute-start(bf16[160,768]{1,0:T(8,128)(2,1)S(1)} %pad_maximum_fusion.2.refs_0_.g0), channel_id=1, source_target_pairs={{0,16},{8,24},{16,0},{24,8},{1,17},{9,25},{17,1},{25,9},{2,18},{10... | collective-permute-start | bytes 737288 | tf_op jit(solution)/shard_map/ppermute | solution.py:435
  47.3 9.8 %collective-permute-start.14 = (bf16[160,768]{1,0:T(8,128)(2,1)S(1)}, bf16[160,768]{1,0:T(8,128)(2,1)S(1)}, u32[]{:S(2)}, u32[]{:S(2)}) collective-permute-start(bf16[160,768]{1,0:T(8,128)(2,1)S(1)} %pad_maximum_fusion.2.refs_0_.g0), channel_id=1, source_target_pairs={{0,8},{8,0},{16,24},{24,16},{1,9},{9,1},{17,25},{25,17},{2,10},{10... | collective-permute-start | bytes 737288 | tf_op jit(solution)/shard_map/ppermute | solution.py:435
  47.8 5.2 %collective-permute-start.19 = (bf16[40,768]{1,0:T(8,128)(2,1)S(1)}, bf16[40,768]{1,0:T(8,128)(2,1)S(1)}, u32[]{:S(2)}, u32[]{:S(2)}) collective-permute-start(bf16[40,768]{1,0:T(8,128)(2,1)S(1)} %get-tuple-element.196), channel_id=1, source_target_pairs={{0,4},{1,5},{2,6},{3,7},{4,0},{5,1},{6,2},{7,3},{8,12},{9,13},{10,... | collective-permute-start | bytes 184328 | tf_op jit(solution)/shard_map/ppermute | solution.py:435
  48.3 4.9 %collective-permute-start.18 = (bf16[40,768]{1,0:T(8,128)(2,1)S(1)}, bf16[40,768]{1,0:T(8,128)(2,1)S(1)}, u32[]{:S(2)}, u32[]{:S(2)}) collective-permute-start(bf16[40,768]{1,0:T(8,128)(2,1)S(1)} %get-tuple-element.197), channel_id=1, source_target_pairs={{0,2},{1,3},{2,0},{3,1},{4,6},{5,7},{6,4},{7,5},{8,10},{9,11},{10,... | collective-permute-start | bytes 184328 | tf_op jit(solution)/shard_map/ppermute | solution.py:435
  53.2 14.7 %collective-permute-start.23 = (bf16[160,768]{1,0:T(8,128)(2,1)S(1)}, bf16[160,768]{1,0:T(8,128)(2,1)S(1)}, u32[]{:S(2)}, u32[]{:S(2)}) collective-permute-start(bf16[160,768]{1,0:T(8,128)(2,1)S(1)} %pad_maximum_fusion.3.x0), channel_id=1, source_target_pairs={{0,24},{8,16},{16,8},{24,0},{1,25},{9,17},{17,9},{25,1},{2,26},{10... | collective-permute-start | bytes 737288 | tf_op jit(solution)/shard_map/ppermute | solution.py:435
  54.7 13.2 %collective-permute-start.22 = (bf16[160,768]{1,0:T(8,128)(2,1)S(1)}, bf16[160,768]{1,0:T(8,128)(2,1)S(1)}, u32[]{:S(2)}, u32[]{:S(2)}) collective-permute-start(bf16[160,768]{1,0:T(8,128)(2,1)S(1)} %pad_maximum_fusion.3.x0), channel_id=1, source_target_pairs={{0,16},{8,24},{16,0},{24,8},{1,17},{9,25},{17,1},{25,9},{2,18},{10... | collective-permute-start | bytes 737288 | tf_op jit(solution)/shard_map/ppermute | solution.py:435
  56.0 11.8 %collective-permute-start.21 = (bf16[160,768]{1,0:T(8,128)(2,1)S(1)}, bf16[160,768]{1,0:T(8,128)(2,1)S(1)}, u32[]{:S(2)}, u32[]{:S(2)}) collective-permute-start(bf16[160,768]{1,0:T(8,128)(2,1)S(1)} %pad_maximum_fusion.3.x0), channel_id=1, source_target_pairs={{0,8},{8,0},{16,24},{24,16},{1,9},{9,1},{17,25},{25,17},{2,10},{10... | collective-permute-start | bytes 737288 | tf_op jit(solution)/shard_map/ppermute | solution.py:435
  56.7 7.8 %collective-permute-start.24 = (bf16[128,768]{1,0:T(8,128)(2,1)S(1)}, bf16[128,768]{1,0:T(8,128)(2,1)S(1)}, u32[]{:S(2)}, u32[]{:S(2)}) collective-permute-start(bf16[128,768]{1,0:T(8,128)(2,1)S(1)} %get-tuple-element.121), channel_id=1, source_target_pairs={{0,2},{1,3},{2,0},{3,1},{4,6},{5,7},{6,4},{7,5},{8,10},{9,11},{10,... | collective-permute-start | bytes 589832 | tf_op jit(solution)/shard_map/ppermute | solution.py:435
  57.0 10.8 %collective-permute-start.25 = (bf16[128,768]{1,0:T(8,128)(2,1)S(1)}, bf16[128,768]{1,0:T(8,128)(2,1)S(1)}, u32[]{:S(2)}, u32[]{:S(2)}) collective-permute-start(bf16[128,768]{1,0:T(8,128)(2,1)S(1)} %get-tuple-element.123), channel_id=1, source_target_pairs={{0,4},{1,5},{2,6},{3,7},{4,0},{5,1},{6,2},{7,3},{8,12},{9,13},{10,... | collective-permute-start | bytes 589832 | tf_op jit(solution)/shard_map/ppermute | solution.py:435
  72.6 8.5 %collective-permute-start.26 = (bf16[160,896]{1,0:T(8,128)(2,1)S(1)}, bf16[160,896]{1,0:T(8,128)(2,1)S(1)}, u32[]{:S(2)}, u32[]{:S(2)}) collective-permute-start(bf16[160,896]{1,0:T(8,128)(2,1)S(1)} %get-tuple-element.131), channel_id=1, source_target_pairs={{0,8},{8,0},{16,24},{24,16},{1,9},{9,1},{17,25},{25,17},{2,10},{10... | collective-permute-start | bytes 860168 | tf_op jit(solution)/shard_map/ppermute | solution.py:435
  74.1 11.8 %collective-permute-start.27 = (bf16[160,896]{1,0:T(8,128)(2,1)S(1)}, bf16[160,896]{1,0:T(8,128)(2,1)S(1)}, u32[]{:S(2)}, u32[]{:S(2)}) collective-permute-start(bf16[160,896]{1,0:T(8,128)(2,1)S(1)} %get-tuple-element.132), channel_id=1, source_target_pairs={{0,16},{8,24},{16,0},{24,8},{1,17},{9,25},{17,1},{25,9},{2,18},{10... | collective-permute-start | bytes 860168 | tf_op jit(solution)/shard_map/ppermute | solution.py:435
  74.7 11.3 %collective-permute-start.28 = (bf16[160,896]{1,0:T(8,128)(2,1)S(1)}, bf16[160,896]{1,0:T(8,128)(2,1)S(1)}, u32[]{:S(2)}, u32[]{:S(2)}) collective-permute-start(bf16[160,896]{1,0:T(8,128)(2,1)S(1)} %get-tuple-element.133), channel_id=1, source_target_pairs={{0,24},{8,16},{16,8},{24,0},{1,25},{9,17},{17,9},{25,1},{2,26},{10... | collective-permute-start | bytes 860168 | tf_op jit(solution)/shard_map/ppermute | solution.py:435
  76.1 14.9 %collective-permute-start.29 = (bf16[128,768]{1,0:T(8,128)(2,1)S(1)}, bf16[128,768]{1,0:T(8,128)(2,1)S(1)}, u32[]{:S(2)}, u32[]{:S(2)}) collective-permute-start(bf16[128,768]{1,0:T(8,128)(2,1)S(1)} %get-tuple-element.137), channel_id=1, source_target_pairs={{0,6},{1,7},{2,4},{3,5},{4,2},{5,3},{6,0},{7,1},{8,14},{9,15},{10,... | collective-permute-start | bytes 589832 | tf_op jit(solution)/shard_map/ppermute | solution.py:435
  86.6 6.8 %collective-permute-start.32 = (bf16[40,896]{1,0:T(8,128)(2,1)S(1)}, bf16[40,896]{1,0:T(8,128)(2,1)S(1)}, u32[]{:S(2)}, u32[]{:S(2)}) collective-permute-start(bf16[40,896]{1,0:T(8,128)(2,1)S(1)} %get-tuple-element.187), channel_id=1, source_target_pairs={{0,6},{1,7},{2,4},{3,5},{4,2},{5,3},{6,0},{7,1},{8,14},{9,15},{10,... | collective-permute-start | bytes 215048 | tf_op jit(solution)/shard_map/ppermute | solution.py:435
  89.9 5.2 %collective-permute-start.31 = (bf16[40,896]{1,0:T(8,128)(2,1)S(1)}, bf16[40,896]{1,0:T(8,128)(2,1)S(1)}, u32[]{:S(2)}, u32[]{:S(2)}) collective-permute-start(bf16[40,896]{1,0:T(8,128)(2,1)S(1)} %get-tuple-element.188), channel_id=1, source_target_pairs={{0,4},{1,5},{2,6},{3,7},{4,0},{5,1},{6,2},{7,3},{8,12},{9,13},{10,... | collective-permute-start | bytes 215048 | tf_op jit(solution)/shard_map/ppermute | solution.py:435
  89.9 5.2 %collective-permute-start.30 = (bf16[40,896]{1,0:T(8,128)(2,1)S(1)}, bf16[40,896]{1,0:T(8,128)(2,1)S(1)}, u32[]{:S(2)}, u32[]{:S(2)}) collective-permute-start(bf16[40,896]{1,0:T(8,128)(2,1)S(1)} %get-tuple-element.189), channel_id=1, source_target_pairs={{0,2},{1,3},{2,0},{3,1},{4,6},{5,7},{6,4},{7,5},{8,10},{9,11},{10,... | collective-permute-start | bytes 215048 | tf_op jit(solution)/shard_map/ppermute | solution.py:435
  96.1 5.1 %collective-permute-start.33 = (bf16[128,896]{1,0:T(8,128)(2,1)S(1)}, bf16[128,896]{1,0:T(8,128)(2,1)S(1)}, u32[]{:S(2)}, u32[]{:S(2)}) collective-permute-start(bf16[128,896]{1,0:T(8,128)(2,1)S(1)} %get-tuple-element.140), channel_id=1, source_target_pairs={{0,1},{1,0},{2,3},{3,2},{4,5},{5,4},{6,7},{7,6},{8,9},{9,8},{10,11... | collective-permute-start | bytes 688136 | tf_op jit(solution)/shard_map/ppermute | solution.py:435
  97.7 11.5 %collective-permute-start.34 = (bf16[160,768]{1,0:T(8,128)(2,1)S(1)}, bf16[160,768]{1,0:T(8,128)(2,1)S(1)}, u32[]{:S(2)}, u32[]{:S(2)}) collective-permute-start(bf16[160,768]{1,0:T(8,128)(2,1)S(1)} %get-tuple-element.149), channel_id=1, source_target_pairs={{0,8},{8,0},{16,24},{24,16},{1,9},{9,1},{17,25},{25,17},{2,10},{10... | collective-permute-start | bytes 737288 | tf_op jit(solution)/shard_map/ppermute | solution.py:435
  97.9 13.5 %collective-permute-start.35 = (bf16[160,768]{1,0:T(8,128)(2,1)S(1)}, bf16[160,768]{1,0:T(8,128)(2,1)S(1)}, u32[]{:S(2)}, u32[]{:S(2)}) collective-permute-start(bf16[160,768]{1,0:T(8,128)(2,1)S(1)} %get-tuple-element.150), channel_id=1, source_target_pairs={{0,16},{8,24},{16,0},{24,8},{1,17},{9,25},{17,1},{25,9},{2,18},{10... | collective-permute-start | bytes 737288 | tf_op jit(solution)/shard_map/ppermute | solution.py:435
  99.6 11.8 %collective-permute-start.36 = (bf16[160,768]{1,0:T(8,128)(2,1)S(1)}, bf16[160,768]{1,0:T(8,128)(2,1)S(1)}, u32[]{:S(2)}, u32[]{:S(2)}) collective-permute-start(bf16[160,768]{1,0:T(8,128)(2,1)S(1)} %get-tuple-element.151), channel_id=1, source_target_pairs={{0,24},{8,16},{16,8},{24,0},{1,25},{9,17},{17,9},{25,1},{2,26},{10... | collective-permute-start | bytes 737288 | tf_op jit(solution)/shard_map/ppermute | solution.py:435
  106.4 10.0 %collective-permute-start.37 = (bf16[128,768]{1,0:T(8,128)(2,1)S(1)}, bf16[128,768]{1,0:T(8,128)(2,1)S(1)}, u32[]{:S(2)}, u32[]{:S(2)}) collective-permute-start(bf16[128,768]{1,0:T(8,128)(2,1)S(1)} %get-tuple-element.152), channel_id=1, source_target_pairs={{0,2},{1,3},{2,0},{3,1},{4,6},{5,7},{6,4},{7,5},{8,10},{9,11},{10,... | collective-permute-start | bytes 589832 | tf_op jit(solution)/shard_map/ppermute | solution.py:435
  107.1 17.2 %collective-permute-start.38 = (bf16[128,768]{1,0:T(8,128)(2,1)S(1)}, bf16[128,768]{1,0:T(8,128)(2,1)S(1)}, u32[]{:S(2)}, u32[]{:S(2)}) collective-permute-start(bf16[128,768]{1,0:T(8,128)(2,1)S(1)} %get-tuple-element.161), channel_id=1, source_target_pairs={{0,4},{1,5},{2,6},{3,7},{4,0},{5,1},{6,2},{7,3},{8,12},{9,13},{10,... | collective-permute-start | bytes 589832 | tf_op jit(solution)/shard_map/ppermute | solution.py:435
  109.2 15.1 %collective-permute-start.39 = (bf16[128,768]{1,0:T(8,128)(2,1)S(1)}, bf16[128,768]{1,0:T(8,128)(2,1)S(1)}, u32[]{:S(2)}, u32[]{:S(2)}) collective-permute-start(bf16[128,768]{1,0:T(8,128)(2,1)S(1)} %get-tuple-element.162), channel_id=1, source_target_pairs={{0,6},{1,7},{2,4},{3,5},{4,2},{5,3},{6,0},{7,1},{8,14},{9,15},{10,... | collective-permute-start | bytes 589832 | tf_op jit(solution)/shard_map/ppermute | solution.py:435
  129.6 6.5 %collective-permute-start.41 = (bf16[224,384]{1,0:T(8,128)(2,1)S(1)}, bf16[224,384]{1,0:T(8,128)(2,1)S(1)}, u32[]{:S(2)}, u32[]{:S(2)}) collective-permute-start(bf16[224,384]{1,0:T(8,128)(2,1)S(1)} %get-tuple-element.166), channel_id=1, source_target_pairs={{0,16},{8,24},{16,0},{24,8},{1,17},{9,25},{17,1},{25,9},{2,18},{10... | collective-permute-start | bytes 516104 | tf_op jit(solution)/shard_map/ppermute | solution.py:435
  130.0 11.2 %collective-permute-start.46 = (bf16[224,384]{1,0:T(8,128)(2,1)S(1)}, bf16[224,384]{1,0:T(8,128)(2,1)S(1)}, u32[]{:S(2)}, u32[]{:S(2)}) collective-permute-start(bf16[224,384]{1,0:T(8,128)(2,1)S(1)} %get-tuple-element.172), channel_id=1, source_target_pairs={{0,8},{8,0},{16,24},{24,16},{1,9},{9,1},{17,25},{25,17},{2,10},{10... | collective-permute-start | bytes 516104 | tf_op jit(solution)/shard_map/ppermute | solution.py:435
  131.8 9.5 %collective-permute-start.47 = (bf16[224,384]{1,0:T(8,128)(2,1)S(1)}, bf16[224,384]{1,0:T(8,128)(2,1)S(1)}, u32[]{:S(2)}, u32[]{:S(2)}) collective-permute-start(bf16[224,384]{1,0:T(8,128)(2,1)S(1)} %get-tuple-element.173), channel_id=1, source_target_pairs={{0,24},{8,16},{16,8},{24,0},{1,25},{9,17},{17,9},{25,1},{2,26},{10... | collective-permute-start | bytes 516104 | tf_op jit(solution)/shard_map/ppermute | solution.py:435
  136.1 10.4 %collective-permute-start.44 = (bf16[40,768]{1,0:T(8,128)(2,1)S(1)}, bf16[40,768]{1,0:T(8,128)(2,1)S(1)}, u32[]{:S(2)}, u32[]{:S(2)}) collective-permute-start(bf16[40,768]{1,0:T(8,128)(2,1)S(1)} %get-tuple-element.191), channel_id=1, source_target_pairs={{0,6},{1,7},{2,4},{3,5},{4,2},{5,3},{6,0},{7,1},{8,14},{9,15},{10,... | collective-permute-start | bytes 184328 | tf_op jit(solution)/shard_map/ppermute | solution.py:435
  138.6 8.4 %collective-permute-start.43 = (bf16[40,768]{1,0:T(8,128)(2,1)S(1)}, bf16[40,768]{1,0:T(8,128)(2,1)S(1)}, u32[]{:S(2)}, u32[]{:S(2)}) collective-permute-start(bf16[40,768]{1,0:T(8,128)(2,1)S(1)} %get-tuple-element.192), channel_id=1, source_target_pairs={{0,4},{1,5},{2,6},{3,7},{4,0},{5,1},{6,2},{7,3},{8,12},{9,13},{10,... | collective-permute-start | bytes 184328 | tf_op jit(solution)/shard_map/ppermute | solution.py:435
  140.8 6.2 %collective-permute-start.42 = (bf16[40,768]{1,0:T(8,128)(2,1)S(1)}, bf16[40,768]{1,0:T(8,128)(2,1)S(1)}, u32[]{:S(2)}, u32[]{:S(2)}) collective-permute-start(bf16[40,768]{1,0:T(8,128)(2,1)S(1)} %get-tuple-element.193), channel_id=1, source_target_pairs={{0,2},{1,3},{2,0},{3,1},{4,6},{5,7},{6,4},{7,5},{8,10},{9,11},{10,... | collective-permute-start | bytes 184328 | tf_op jit(solution)/shard_map/ppermute | solution.py:435
  141.9 12.1 %collective-permute-start.50 = (bf16[224,384]{1,0:T(8,128)(2,1)S(1)}, bf16[224,384]{1,0:T(8,128)(2,1)S(1)}, u32[]{:S(2)}, u32[]{:S(2)}) collective-permute-start(bf16[224,384]{1,0:T(8,128)(2,1)S(1)} %sum_share.1.a0), channel_id=1, source_target_pairs={{0,6},{1,7},{2,4},{3,5},{4,2},{5,3},{6,0},{7,1},{8,14},{9,15},{10,... | collective-permute-start | bytes 516104 | tf_op jit(solution)/shard_map/ppermute | solution.py:435
  144.3 16.2 %collective-permute-start.49 = (bf16[224,384]{1,0:T(8,128)(2,1)S(1)}, bf16[224,384]{1,0:T(8,128)(2,1)S(1)}, u32[]{:S(2)}, u32[]{:S(2)}) collective-permute-start(bf16[224,384]{1,0:T(8,128)(2,1)S(1)} %sum_share.1.a0), channel_id=1, source_target_pairs={{0,4},{1,5},{2,6},{3,7},{4,0},{5,1},{6,2},{7,3},{8,12},{9,13},{10,... | collective-permute-start | bytes 516104 | tf_op jit(solution)/shard_map/ppermute | solution.py:435
  146.5 14.1 %collective-permute-start.48 = (bf16[224,384]{1,0:T(8,128)(2,1)S(1)}, bf16[224,384]{1,0:T(8,128)(2,1)S(1)}, u32[]{:S(2)}, u32[]{:S(2)}) collective-permute-start(bf16[224,384]{1,0:T(8,128)(2,1)S(1)} %sum_share.1.a0), channel_id=1, source_target_pairs={{0,2},{1,3},{2,0},{3,1},{4,6},{5,7},{6,4},{7,5},{8,10},{9,11},{10,... | collective-permute-start | bytes 516104 | tf_op jit(solution)/shard_map/ppermute | solution.py:435
  147.9 13.2 %collective-permute-start.45 = (bf16[128,768]{1,0:T(8,128)(2,1)S(1)}, bf16[128,768]{1,0:T(8,128)(2,1)S(1)}, u32[]{:S(2)}, u32[]{:S(2)}) collective-permute-start(bf16[128,768]{1,0:T(8,128)(2,1)S(1)} %get-tuple-element.169), channel_id=1, source_target_pairs={{0,1},{1,0},{2,3},{3,2},{4,5},{5,4},{6,7},{7,6},{8,9},{9,8},{10,11... | collective-permute-start | bytes 589832 | tf_op jit(solution)/shard_map/ppermute | solution.py:435
  153.5 8.4 %collective-permute-start.51 = (bf16[224,384]{1,0:T(8,128)(2,1)S(1)}, bf16[224,384]{1,0:T(8,128)(2,1)S(1)}, u32[]{:S(2)}, u32[]{:S(2)}) collective-permute-start(bf16[224,384]{1,0:T(8,128)(2,1)S(1)} %sum_share.1.a0), channel_id=1, source_target_pairs={{0,1},{1,0},{2,3},{3,2},{4,5},{5,4},{6,7},{7,6},{8,9},{9,8},{10,11... | collective-permute-start | bytes 516104 | tf_op jit(solution)/shard_map/ppermute | solution.py:435
  154.0 7.9 %collective-permute-start.54 = (bf16[224,384]{1,0:T(8,128)(2,1)S(1)}, bf16[224,384]{1,0:T(8,128)(2,1)S(1)}, u32[]{:S(2)}, u32[]{:S(2)}) collective-permute-start(bf16[224,384]{1,0:T(8,128)(2,1)S(1)} %collective-permute-done.50.a3), channel_id=1, source_target_pairs={{0,1},{1,0},{2,3},{3,2},{4,5},{5,4},{6,7},{7,6},{8,9},{9,8},{10,11... | collective-permute-start | bytes 516104 | tf_op jit(solution)/shard_map/ppermute | solution.py:435
  (24 other events, 156.1 us)

commit v5 on v4

--- a/solution.py
+++ b/solution.py
@@ -83,7 +83,7 @@
     width = out.shape[1]
     spread = (iota((rows, width), 0) == iota((rows, width), 1)).astype(f32).astype(bf16)
     whole = nn(part.astype(bf16), spread)
-    pick_t = (iota((smalls, heads), 0) == iota((smalls, heads), 1) + experts + 2).astype(f32)
+    pick_t = (iota((smalls, heads), 0) == iota((smalls, heads), 1)).astype(f32)
     table_t = nt(pick_t.astype(bf16), tab[...])
     spread_t = (iota((shard, width), 0) + rows == iota((shard, width), 1)).astype(f32)
     whole = whole + nn(table_t.astype(bf16), spread_t.astype(bf16))
@@ -177,7 +177,7 @@
         for t in range(2):
             h = 2 * p + t
             qh = jnp.where(low, q2, zero) if t == 0 else jnp.where(low, zero, q2)
-            line = per_offset[experts + 2 + h : experts + 3 + h, :]
+            line = per_offset[h : h + 1, :]
             bias = pltpu.roll(
                 jnp.broadcast_to(line, (length, 2 * length)), 0, 1, stride=1, stride_axis=0
             )[:, 0:length]
@@ -337,7 +337,7 @@
     out = out + jnp.where(line == experts, g_gain1, 0.0) + jnp.where(line == experts + 1, gain2[...], 0.0)
     small_o[...] = out.astype(bf16)
     heads = table.shape[0]
-    pick_t = (iota((smalls, heads), 0) == iota((smalls, heads), 1) + experts + 2).astype(f32)
+    pick_t = (iota((smalls, heads), 0) == iota((smalls, heads), 1)).astype(f32)
     table_o[...] = nn(pick_t.astype(bf16), table[...].astype(bf16)).astype(bf16)
 
 
@@ -409,7 +409,7 @@
     gain_b[...] = total[experts + 1 : experts + 2, 0:rows]
     shard, heads = tab.shape
     lane = (iota((shard, half), 1) == iota((shard, half), 0) + rows).astype(f32)
-    line = (iota((heads, total.shape[0]), 1) == iota((heads, total.shape[0]), 0) + experts + 2).astype(f32)
+    line = (iota((heads, total.shape[0]), 1) == iota((heads, total.shape[0]), 0)).astype(f32)
     dims = (((1,), (1,)), ((), ()))
     turned = lax.dot_general(lane, total, dims, precision=lax.Precision.HIGHEST, preferred_element_type=f32)
     tab[...] = lax.dot_general(turned, line, dims, precision=lax.Precision.HIGHEST, preferred_element_type=f32)
@@ -426,7 +426,7 @@
     rows = w_query.shape[0]
     shard = bias_table.shape[0]
     cap = 5 * length // (4 * experts)
-    smalls = -(-(experts + 2 + heads) // 16) * 16
+    smalls = -(-max(experts + 2, heads) // 16) * 16
     slots = experts * cap
     wide = width + 128
 
@@ -599,7 +599,7 @@
         rest = both[:, 4 * width :]
         r_out = rest[:, 0:experts]
         gain1_out, gain2_out = rest[:, experts], rest[:, experts + 1]
-        tab_g = table_g.T[0 : 4 * shard, experts + 2 : experts + 2 + heads].astype(f32)
+        tab_g = table_g.T[0 : 4 * shard, 0:heads].astype(f32)
         table_out = lax.psum(lax.psum_scatter(tab_g, "dp", scatter_dimension=0, tiled=True), "expert")
     return (
         layer_out, d_tokens, g_q, g_k, g_v, g_o, r_out, gain1_out, gain2_out, table_out, grad_in, grad_out,

time: 165 us -> 163 us (0.988)
  waiting for transfers between devices: 56.7 us -> 54.8 us
    ppermute x55, waiting for transfers between devices: 56.7 us -> 54.8 us  [along(): return lax.ppermute(x, axis, [(s, s ^ mask) for s in range(n)])]
where the time goes in v5:
time: 163 us
  starting transfers between devices  62 us (38%)
  waiting for transfers between devices  54.8 us (34%)
  Pallas kernels  40.7 us (25%)
  other arithmetic  3.23 us (2%)
    ppermute x55, starting transfers between devices, along(): return lax.ppermute(x, axis, [(s, s ^ mask) for s in range(n)])  62 us
    ppermute x55, waiting for transfers between devices, along(): return lax.ppermute(x, axis, [(s, s ^ mask) for s in range(n)])  54.8 us
    pallas_call x18, Pallas kernels, call(): pl.pallas_call(body, name=name, cost_estimate=pl.CostEstimate(flops=int(m...  40.7 us
  transfers between devices with their start and end apart: 55, of which 25 were waited for; matrix products, arithmetic and copies ran while one was open for 1% of the time, Pallas kernels for 14%

profile of v5, /device:TPU:0, one launch (start us, length us, event | category | flops | bytes accessed | tf_op | source)
XLA Modules:
  0.0 163.1 jit_solution(2423332759324965790)
XLA Ops:
  0.7 1.2 broadcast_select_fusion
  2.8 3.0 %collective-permute-start.1 = (bf16[384,768]{1,0:T(8,128)(2,1)}, bf16[384,768]{1,0:T(8,128)(2,1)S(1)}, u32[]{:S(2)}, u32[]{:S(2)}) collective-permute-start(bf16[384,768]{1,0:T(8,128)(2,1)} %pad_maximum_fusion), channel_id=1, source_target_pairs={{0,16},{8,24},{16,0},{24,8},{1,17},{9,25},{17,1},{25,9},{2,18},{10... | collective-permute-start | bytes 1769480 | tf_op jit(solution)/shard_map/ppermute | solution.py:435
  5.8 1.5 collective-permute-start
  9.9 3.7 %collective-permute-start.6 = (bf16[40,768]{1,0:T(8,128)(2,1)S(1)}, bf16[40,768]{1,0:T(8,128)(2,1)S(1)}, u32[]{:S(2)}, u32[]{:S(2)}) collective-permute-start(bf16[40,768]{1,0:T(8,128)(2,1)S(1)} %get-tuple-element.199), channel_id=1, source_target_pairs={{0,6},{1,7},{2,4},{3,5},{4,2},{5,3},{6,0},{7,1},{8,14},{9,15},{10,... | collective-permute-start | bytes 184328 | tf_op jit(solution)/shard_map/ppermute | solution.py:435
  16.8 2.4 %collective-permute-done.5 = bf16[40,768]{1,0:T(8,128)(2,1)S(1)} collective-permute-done((bf16[40,768]{1,0:T(8,128)(2,1)S(1)}, bf16[40,768]{1,0:T(8,128)(2,1)S(1)}, u32[]{:S(2)}, u32[]{:S(2)}) %collective-permute-start.5) | collective-permute-done | bytes 61472 | tf_op jit(solution)/shard_map/ppermute | solution.py:435
  19.3 1.6 collective-permute-done.hx
  21.4 1.8 %collective-permute-start.9 = (bf16[192,768]{1,0:T(8,128)(2,1)S(1)}, bf16[192,768]{1,0:T(8,128)(2,1)}, u32[]{:S(2)}, u32[]{:S(2)}) collective-permute-start(bf16[192,768]{1,0:T(8,128)(2,1)S(1)} %slice.59), channel_id=1, source_target_pairs={{0,8},{8,0},{16,24},{24,16},{1,9},{9,1},{17,25},{25,17},{2,10},{10... | collective-permute-start | bytes 884744 | tf_op jit(solution)/shard_map/ppermute | solution.py:435
  23.6 5.6 %collective-permute-done.8.da = bf16[208,768]{1,0:T(8,128)(2,1)} collective-permute-done((bf16[208,768]{1,0:T(8,128)(2,1)S(1)}, bf16[208,768]{1,0:T(8,128)(2,1)}, u32[]{:S(2)}, u32[]{:S(2)}) %collective-permute-start.8) | collective-permute-done | bytes 319520 | tf_op jit(solution)/shard_map/ppermute | solution.py:435
  30.0 1.6 %collective-permute-done.13.tb = bf16[192,768]{1,0:T(8,128)(2,1)} collective-permute-done((bf16[192,768]{1,0:T(8,128)(2,1)}, bf16[192,768]{1,0:T(8,128)(2,1)}, u32[]{:S(2)}, u32[]{:S(2)}) %collective-permute-start.13) | collective-permute-done | bytes 294944 | tf_op jit(solution)/shard_map/ppermute | solution.py:435
  32.6 7.2 %attend.1 = (bf16[4,768,768]{2,1,0:T(8,128)(2,1)S(1)}, f32[16,768]{1,0:T(8,128)S(1)}, bf16[128,768]{1,0:T(8,128)(2,1)S(1)}, bf16[128,768]{1,0:T(8,128)(2,1)S(1)}...) custom-call(s32[4]{0:T(128)S(1)} %pad_add_fusion.1.idx, ...), custom_call_target="tpu_custom_call" | custom-call | flops 7699999744 | bytes 7000000 | tf_op jit(solution)/shard_map/attend/pallas_call | solution.py:43
  40.0 1.8 %collective-permute-start.16 = (bf16[160,768]{1,0:T(8,128)(2,1)S(1)}, bf16[160,768]{1,0:T(8,128)(2,1)S(1)}, u32[]{:S(2)}, u32[]{:S(2)}) collective-permute-start(bf16[160,768]{1,0:T(8,128)(2,1)S(1)} %pad_maximum_fusion.2.refs_0_.g0), channel_id=1, source_target_pairs={{0,24},{8,16},{16,8},{24,0},{1,25},{9,17},{17,9},{25,1},{2,26},{10... | collective-permute-start | bytes 737288 | tf_op jit(solution)/shard_map/ppermute | solution.py:435
  42.7 3.7 %collective-permute-start.20 = (bf16[40,768]{1,0:T(8,128)(2,1)S(1)}, bf16[40,768]{1,0:T(8,128)(2,1)S(1)}, u32[]{:S(2)}, u32[]{:S(2)}) collective-permute-start(bf16[40,768]{1,0:T(8,128)(2,1)S(1)} %get-tuple-element.195), channel_id=1, source_target_pairs={{0,6},{1,7},{2,4},{3,5},{4,2},{5,3},{6,0},{7,1},{8,14},{9,15},{10,... | collective-permute-start | bytes 184328 | tf_op jit(solution)/shard_map/ppermute | solution.py:435
  46.3 1.2 collective-permute-start.15
  49.8 3.6 %collective-permute-done.19 = bf16[40,768]{1,0:T(8,128)(2,1)S(1)} collective-permute-done((bf16[40,768]{1,0:T(8,128)(2,1)S(1)}, bf16[40,768]{1,0:T(8,128)(2,1)S(1)}, u32[]{:S(2)}, u32[]{:S(2)}) %collective-permute-start.19) | collective-permute-done | bytes 61472 | tf_op jit(solution)/shard_map/ppermute | solution.py:435
  53.7 1.4 collective-permute-start.23
  55.1 1.2 collective-permute-start.22
  57.6 3.4 %collective-permute-start.25 = (bf16[128,768]{1,0:T(8,128)(2,1)S(1)}, bf16[128,768]{1,0:T(8,128)(2,1)S(1)}, u32[]{:S(2)}, u32[]{:S(2)}) collective-permute-start(bf16[128,768]{1,0:T(8,128)(2,1)S(1)} %get-tuple-element.123), channel_id=1, source_target_pairs={{0,4},{1,5},{2,6},{3,7},{4,0},{5,1},{6,2},{7,3},{8,12},{9,13},{10,... | collective-permute-start | bytes 589832 | tf_op jit(solution)/shard_map/ppermute | solution.py:435
  61.0 2.2 %g_back.1.g_all = f32[4,160,768]{2,1,0:T(8,128)S(1)} custom-call(s32[4]{0:T(128)S(1)} %pad_add_fusion.1.idx, bf16[768,768]{1,0:T(8,128)(2,1)S(1)} %bitcast.18, bf16[160,768]{1,0:T(8,128)(2,1)S(1)} %pad_maximum_fusion.2.refs_0_.g0, bf16[160,768]{1,0:T(8,128)(2,1)S(1)} %collective-permute-done.14.refs_1_.g1, ...), custom_call_target="tpu_custom_call" | custom-call | flops 2200000000 | bytes 2000000 | tf_op jit(solution)/shard_map/g_back/pallas_call | solution.py:43
  63.2 1.3 collective-permute-done.24.l1
  64.5 3.3 %collective-permute-done.25.l2 = bf16[128,768]{1,0:T(8,128)(2,1)S(1)} collective-permute-done((bf16[128,768]{1,0:T(8,128)(2,1)S(1)}, bf16[128,768]{1,0:T(8,128)(2,1)S(1)}, u32[]{:S(2)}, u32[]{:S(2)}) %collective-permute-start.25) | collective-permute-done | bytes 196640 | tf_op jit(solution)/shard_map/ppermute | solution.py:435
  67.9 4.7 %expert.1 = (bf16[160,896]{1,0:T(8,128)(2,1)S(1)}, bf16[160,896]{1,0:T(8,128)(2,1)S(1)}, bf16[160,896]{1,0:T(8,128)(2,1)S(1)}, bf16[160,896]{1,0:T(8,128)(2,1)S(...) custom-call(s32[4]{0:T(128)S(1)} %pad_add_fusion.1.idx, ...), custom_call_target="tpu_custom_call" | custom-call | flops 4400000000 | bytes 4000000 | tf_op jit(solution)/shard_map/expert/pallas_call | solution.py:43
  72.6 1.8 %collective-permute-start.26 = (bf16[160,896]{1,0:T(8,128)(2,1)S(1)}, bf16[160,896]{1,0:T(8,128)(2,1)S(1)}, u32[]{:S(2)}, u32[]{:S(2)}) collective-permute-start(bf16[160,896]{1,0:T(8,128)(2,1)S(1)} %get-tuple-element.131), channel_id=1, source_target_pairs={{0,8},{8,0},{16,24},{24,16},{1,9},{9,1},{17,25},{25,17},{2,10},{10... | collective-permute-start | bytes 860168 | tf_op jit(solution)/shard_map/ppermute | solution.py:435
  76.1 2.3 %collective-permute-start.29 = (bf16[128,768]{1,0:T(8,128)(2,1)S(1)}, bf16[128,768]{1,0:T(8,128)(2,1)S(1)}, u32[]{:S(2)}, u32[]{:S(2)}) collective-permute-start(bf16[128,768]{1,0:T(8,128)(2,1)S(1)} %get-tuple-element.137), channel_id=1, source_target_pairs={{0,6},{1,7},{2,4},{3,5},{4,2},{5,3},{6,0},{7,1},{8,14},{9,15},{10,... | collective-permute-start | bytes 589832 | tf_op jit(solution)/shard_map/ppermute | solution.py:435
  78.4 3.2 %collective-permute-done.26.b = bf16[160,896]{1,0:T(8,128)(2,1)S(1)} collective-permute-done((bf16[160,896]{1,0:T(8,128)(2,1)S(1)}, bf16[160,896]{1,0:T(8,128)(2,1)S(1)}, u32[]{:S(2)}, u32[]{:S(2)}) %collective-permute-start.26) | collective-permute-done | bytes 286752 | tf_op jit(solution)/shard_map/ppermute | solution.py:435
  81.6 4.4 %collective-permute-done.27.c = bf16[160,896]{1,0:T(8,128)(2,1)S(1)} collective-permute-done((bf16[160,896]{1,0:T(8,128)(2,1)S(1)}, bf16[160,896]{1,0:T(8,128)(2,1)S(1)}, u32[]{:S(2)}, u32[]{:S(2)}) %collective-permute-start.27) | collective-permute-done | bytes 286752 | tf_op jit(solution)/shard_map/ppermute | solution.py:435
  86.8 3.4 %collective-permute-start.32 = (bf16[40,896]{1,0:T(8,128)(2,1)S(1)}, bf16[40,896]{1,0:T(8,128)(2,1)S(1)}, u32[]{:S(2)}, u32[]{:S(2)}) collective-permute-start(bf16[40,896]{1,0:T(8,128)(2,1)S(1)} %get-tuple-element.187), channel_id=1, source_target_pairs={{0,6},{1,7},{2,4},{3,5},{4,2},{5,3},{6,0},{7,1},{8,14},{9,15},{10,... | collective-permute-start | bytes 215048 | tf_op jit(solution)/shard_map/ppermute | solution.py:435
  91.2 2.3 %collective-permute-done.32 = bf16[40,896]{1,0:T(8,128)(2,1)S(1)} collective-permute-done((bf16[40,896]{1,0:T(8,128)(2,1)S(1)}, bf16[40,896]{1,0:T(8,128)(2,1)S(1)}, u32[]{:S(2)}, u32[]{:S(2)}) %collective-permute-start.32) | collective-permute-done | bytes 71712 | tf_op jit(solution)/shard_map/ppermute | solution.py:435
  93.5 1.9 %collective-permute-done.31 = bf16[40,896]{1,0:T(8,128)(2,1)S(1)} collective-permute-done((bf16[40,896]{1,0:T(8,128)(2,1)S(1)}, bf16[40,896]{1,0:T(8,128)(2,1)S(1)}, u32[]{:S(2)}, u32[]{:S(2)}) %collective-permute-start.31) | collective-permute-done | bytes 71712 | tf_op jit(solution)/shard_map/ppermute | solution.py:435
  96.3 1.5 expert_out.1
  98.6 1.2 collective-permute-start.35
  99.8 1.6 collective-permute-start.36
  101.4 5.2 %attend_back.1 = (f32[128,768]{1,0:T(8,128)S(1)}, bf16[4,128,768]{2,1,0:T(8,128)(2,1)S(1)}, f32[8,768]{1,0:T(8,128)S(1)}, f32[1,768]{1,0:T(1,128)S(1)}, f32[12,1...) custom-call(s32[4]{0:T(128)S(1)} %pad_add_fusion.1.idx, ...), custom_call_target="tpu_custom_call" | custom-call | flops 6049999872 | bytes 5500000 | tf_op jit(solution)/shard_map/attend_back/pallas_call | solution.py:43
  107.3 2.0 %collective-permute-start.38 = (bf16[128,768]{1,0:T(8,128)(2,1)S(1)}, bf16[128,768]{1,0:T(8,128)(2,1)S(1)}, u32[]{:S(2)}, u32[]{:S(2)}) collective-permute-start(bf16[128,768]{1,0:T(8,128)(2,1)S(1)} %get-tuple-element.161), channel_id=1, source_target_pairs={{0,4},{1,5},{2,6},{3,7},{4,0},{5,1},{6,2},{7,3},{8,12},{9,13},{10,... | collective-permute-start | bytes 589832 | tf_op jit(solution)/shard_map/ppermute | solution.py:435
  109.3 1.8 %collective-permute-start.39 = (bf16[128,768]{1,0:T(8,128)(2,1)S(1)}, bf16[128,768]{1,0:T(8,128)(2,1)S(1)}, u32[]{:S(2)}, u32[]{:S(2)}) collective-permute-start(bf16[128,768]{1,0:T(8,128)(2,1)S(1)} %get-tuple-element.162), channel_id=1, source_target_pairs={{0,6},{1,7},{2,4},{3,5},{4,2},{5,3},{6,0},{7,1},{8,14},{9,15},{10,... | collective-permute-start | bytes 589832 | tf_op jit(solution)/shard_map/ppermute | solution.py:435
  112.6 2.7 %token_grad.1 = (f32[128,768]{1,0:T(8,128)}, bf16[16,768]{1,0:T(8,128)(2,1)S(1)}, bf16[16,128]{1,0:T(8,128)(2,1)S(1)}) custom-call(s32[4]{0:T(128)S(1)} %pad_add_fusion.1.idx, bf16[128,768]{1,0:T(8,128)(2,1)S(1)} %copy-done.9, f32[128,768]{1,0:T(8,128)S(1)} %get-tuple-element.147.dmixed, bf16[4,128,768]{2,1,0:T(8,128)(2,1)S(1)} %get-tuple-element.153.d, ...), custom_call_target="tpu_custom_call" | custom-call | flops 3300000000 | bytes 3000000 | tf_op jit(solution)/shard_map/token_grad/pallas_call | solution.py:43
  115.3 1.3 collective-permute-done.37.d1
  116.6 7.8 %collective-permute-done.38.d2 = bf16[128,768]{1,0:T(8,128)(2,1)S(1)} collective-permute-done((bf16[128,768]{1,0:T(8,128)(2,1)S(1)}, bf16[128,768]{1,0:T(8,128)(2,1)S(1)}, u32[]{:S(2)}, u32[]{:S(2)}) %collective-permute-start.38) | collective-permute-done | bytes 196640 | tf_op jit(solution)/shard_map/ppermute | solution.py:435
  124.5 2.0 %mixer_grad.1 = (f32[768,384]{1,0:T(8,128)S(1)}, bf16[768,384]{1,0:T(8,128)(2,1)S(1)}) custom-call(s32[4]{0:T(128)S(1)} %pad_add_fusion.1.idx, f32[16,768]{1,0:T(8,128)S(1)} %get-tuple-element.158.small_all, bf16[128,768]{1,0:T(8,128)(2,1)S(1)} %get-tuple-element.135.l0, bf16[128,768]{1,0:T(8,128)(2,1)S(1)} %collective-permute-done.24.l1, ...), custom_call_target="tpu_custom_call" | custom-call | flops 2200000000 | bytes 2000000 | tf_op jit(solution)/shard_map/mixer_grad/pallas_call | solution.py:43
  126.6 2.0 %collective-permute-done.40.got = bf16[768,384]{1,0:T(8,128)(2,1)S(1)} collective-permute-done((bf16[768,384]{1,0:T(8,128)(2,1)S(1)}, bf16[768,384]{1,0:T(8,128)(2,1)S(1)}, u32[]{:S(2)}, u32[]{:S(2)}) %collective-permute-start.40) | collective-permute-done | bytes 589856 | tf_op jit(solution)/shard_map/ppermute | solution.py:435
  131.9 1.6 %collective-permute-start.47 = (bf16[208,384]{1,0:T(8,128)(2,1)S(1)}, bf16[208,384]{1,0:T(8,128)(2,1)S(1)}, u32[]{:S(2)}, u32[]{:S(2)}) collective-permute-start(bf16[208,384]{1,0:T(8,128)(2,1)S(1)} %get-tuple-element.173), channel_id=1, source_target_pairs={{0,24},{8,16},{16,8},{24,0},{1,25},{9,17},{17,9},{25,1},{2,26},{10... | collective-permute-start | bytes 479240 | tf_op jit(solution)/shard_map/ppermute | solution.py:435
  133.5 2.4 %collective-permute-done.41.c = bf16[208,384]{1,0:T(8,128)(2,1)S(1)} collective-permute-done((bf16[208,384]{1,0:T(8,128)(2,1)S(1)}, bf16[208,384]{1,0:T(8,128)(2,1)S(1)}, u32[]{:S(2)}, u32[]{:S(2)}) %collective-permute-start.41) | collective-permute-done | bytes 159776 | tf_op jit(solution)/shard_map/ppermute | solution.py:435
  136.0 2.5 %collective-permute-start.44 = (bf16[40,768]{1,0:T(8,128)(2,1)S(1)}, bf16[40,768]{1,0:T(8,128)(2,1)S(1)}, u32[]{:S(2)}, u32[]{:S(2)}) collective-permute-start(bf16[40,768]{1,0:T(8,128)(2,1)S(1)} %get-tuple-element.191), channel_id=1, source_target_pairs={{0,6},{1,7},{2,4},{3,5},{4,2},{5,3},{6,0},{7,1},{8,14},{9,15},{10,... | collective-permute-start | bytes 184328 | tf_op jit(solution)/shard_map/ppermute | solution.py:435
  138.4 2.2 %collective-permute-start.43 = (bf16[40,768]{1,0:T(8,128)(2,1)S(1)}, bf16[40,768]{1,0:T(8,128)(2,1)S(1)}, u32[]{:S(2)}, u32[]{:S(2)}) collective-permute-start(bf16[40,768]{1,0:T(8,128)(2,1)S(1)} %get-tuple-element.192), channel_id=1, source_target_pairs={{0,4},{1,5},{2,6},{3,7},{4,0},{5,1},{6,2},{7,3},{8,12},{9,13},{10,... | collective-permute-start | bytes 184328 | tf_op jit(solution)/shard_map/ppermute | solution.py:435
  141.8 2.4 %collective-permute-start.50 = (bf16[208,384]{1,0:T(8,128)(2,1)S(1)}, bf16[208,384]{1,0:T(8,128)(2,1)S(1)}, u32[]{:S(2)}, u32[]{:S(2)}) collective-permute-start(bf16[208,384]{1,0:T(8,128)(2,1)S(1)} %sum_share.1.a0), channel_id=1, source_target_pairs={{0,6},{1,7},{2,4},{3,5},{4,2},{5,3},{6,0},{7,1},{8,14},{9,15},{10,... | collective-permute-start | bytes 479240 | tf_op jit(solution)/shard_map/ppermute | solution.py:435
  144.2 1.9 %collective-permute-start.49 = (bf16[208,384]{1,0:T(8,128)(2,1)S(1)}, bf16[208,384]{1,0:T(8,128)(2,1)S(1)}, u32[]{:S(2)}, u32[]{:S(2)}) collective-permute-start(bf16[208,384]{1,0:T(8,128)(2,1)S(1)} %sum_share.1.a0), channel_id=1, source_target_pairs={{0,4},{1,5},{2,6},{3,7},{4,0},{5,1},{6,2},{7,3},{8,12},{9,13},{10,... | collective-permute-start | bytes 479240 | tf_op jit(solution)/shard_map/ppermute | solution.py:435
  147.6 5.6 %expert_grad.1 = (f32[1,768,768]{2,1,0:T(8,128)}, f32[1,768,768]{2,1,0:T(8,128)}) custom-call(s32[4]{0:T(128)S(1)} %pad_add_fusion.1.idx, bf16[4,160,768]{2,1,0:T(8,128)(2,1)S(1)} %get-tuple-element.125.hid, bf16[4,160,768]{2,1,0:T(8,128)(2,1)S(1)} %get-tuple-element.182.dpre, f32[4,160,128]{2,1,0:T(8,128)S(1)} %get-tuple-element.183.gate, ...), custom_call_target="tpu_custom_call" | custom-call | flops 6049999872 | bytes 5500000 | tf_op jit(solution)/shard_map/expert_grad/pallas_call | solution.py:43
  153.7 5.7 %collective-permute-done.49.a2 = bf16[208,384]{1,0:T(8,128)(2,1)S(1)} collective-permute-done((bf16[208,384]{1,0:T(8,128)(2,1)S(1)}, bf16[208,384]{1,0:T(8,128)(2,1)S(1)}, u32[]{:S(2)}, u32[]{:S(2)}) %collective-permute-start.49) | collective-permute-done | bytes 159776 | tf_op jit(solution)/shard_map/ppermute | solution.py:435
  161.0 2.2 %finish.1 = (f32[192,768]{1,0:T(8,128)}, f32[192,768]{1,0:T(8,128)}, f32[192,768]{1,0:T(8,128)}, f32[192,768]{1,0:T(8,128)}, f32[8,192]{1,0:T(8,128)}, /*index=5...) custom-call(s32[4]{0:T(128)S(1)} %pad_add_fusion.1.idx, bf16[208,384]{1,0:T(8,128)(2,1)S(1)} %sum_share.1.a0, ...), custom_call_target="tpu_custom_call" | custom-call | flops 2200000000 | bytes 2000000 | tf_op jit(solution)/shard_map/finish/pallas_call | solution.py:43
  (140 shorter events, 30.0 us)
Async XLA Ops:
  2.8 16.5 %collective-permute-start.1 = (bf16[384,768]{1,0:T(8,128)(2,1)}, bf16[384,768]{1,0:T(8,128)(2,1)S(1)}, u32[]{:S(2)}, u32[]{:S(2)}) collective-permute-start(bf16[384,768]{1,0:T(8,128)(2,1)} %pad_maximum_fusion), channel_id=1, source_target_pairs={{0,16},{8,24},{16,0},{24,8},{1,17},{9,25},{17,1},{25,9},{2,18},{10... | collective-permute-start | bytes 1769480 | tf_op jit(solution)/shard_map/ppermute | solution.py:435
  5.8 15.1 %collective-permute-start = (bf16[384,768]{1,0:T(8,128)(2,1)}, bf16[384,768]{1,0:T(8,128)(2,1)S(1)}, u32[]{:S(2)}, u32[]{:S(2)}) collective-permute-start(bf16[384,768]{1,0:T(8,128)(2,1)} %pad_maximum_fusion), channel_id=1, source_target_pairs={{0,8},{8,0},{16,24},{24,16},{1,9},{9,1},{17,25},{25,17},{2,10},{10... | collective-permute-start | bytes 1769480 | tf_op jit(solution)/shard_map/ppermute | solution.py:435
  9.9 6.4 %collective-permute-start.6 = (bf16[40,768]{1,0:T(8,128)(2,1)S(1)}, bf16[40,768]{1,0:T(8,128)(2,1)S(1)}, u32[]{:S(2)}, u32[]{:S(2)}) collective-permute-start(bf16[40,768]{1,0:T(8,128)(2,1)S(1)} %get-tuple-element.199), channel_id=1, source_target_pairs={{0,6},{1,7},{2,4},{3,5},{4,2},{5,3},{6,0},{7,1},{8,14},{9,15},{10,... | collective-permute-start | bytes 184328 | tf_op jit(solution)/shard_map/ppermute | solution.py:435
  13.6 5.6 %collective-permute-start.5 = (bf16[40,768]{1,0:T(8,128)(2,1)S(1)}, bf16[40,768]{1,0:T(8,128)(2,1)S(1)}, u32[]{:S(2)}, u32[]{:S(2)}) collective-permute-start(bf16[40,768]{1,0:T(8,128)(2,1)S(1)} %get-tuple-element.200), channel_id=1, source_target_pairs={{0,4},{1,5},{2,6},{3,7},{4,0},{5,1},{6,2},{7,3},{8,12},{9,13},{10,... | collective-permute-start | bytes 184328 | tf_op jit(solution)/shard_map/ppermute | solution.py:435
  13.6 5.6 %collective-permute-start.4 = (bf16[40,768]{1,0:T(8,128)(2,1)S(1)}, bf16[40,768]{1,0:T(8,128)(2,1)S(1)}, u32[]{:S(2)}, u32[]{:S(2)}) collective-permute-start(bf16[40,768]{1,0:T(8,128)(2,1)S(1)} %get-tuple-element.201), channel_id=1, source_target_pairs={{0,2},{1,3},{2,0},{3,1},{4,6},{5,7},{6,4},{7,5},{8,10},{9,11},{10,... | collective-permute-start | bytes 184328 | tf_op jit(solution)/shard_map/ppermute | solution.py:435
  16.3 4.7 %collective-permute-start.7 = (bf16[16,256]{1,0:T(8,128)(2,1)S(1)}, bf16[16,256]{1,0:T(8,128)(2,1)S(1)}, u32[]{:S(2)}, u32[]{:S(2)}) collective-permute-start(bf16[16,256]{1,0:T(8,128)(2,1)S(1)} %pack.1.s0), channel_id=1, source_target_pairs={{0,8},{8,0},{16,24},{24,16},{1,9},{9,1},{17,25},{25,17},{2,10},{10... | collective-permute-start | bytes 24584 | tf_op jit(solution)/shard_map/ppermute | solution.py:435
  21.0 8.3 %collective-permute-start.8 = (bf16[208,768]{1,0:T(8,128)(2,1)S(1)}, bf16[208,768]{1,0:T(8,128)(2,1)}, u32[]{:S(2)}, u32[]{:S(2)}) collective-permute-start(bf16[208,768]{1,0:T(8,128)(2,1)S(1)} %maximum_maximum_fusion), channel_id=1, source_target_pairs={{0,16},{8,24},{16,0},{24,8},{1,17},{9,25},{17,1},{25,9},{2,18},{10... | collective-permute-start | bytes 958472 | tf_op jit(solution)/shard_map/ppermute | solution.py:435
  21.4 7.9 %collective-permute-start.9 = (bf16[192,768]{1,0:T(8,128)(2,1)S(1)}, bf16[192,768]{1,0:T(8,128)(2,1)}, u32[]{:S(2)}, u32[]{:S(2)}) collective-permute-start(bf16[192,768]{1,0:T(8,128)(2,1)S(1)} %slice.59), channel_id=1, source_target_pairs={{0,8},{8,0},{16,24},{24,16},{1,9},{9,1},{17,25},{25,17},{2,10},{10... | collective-permute-start | bytes 884744 | tf_op jit(solution)/shard_map/ppermute | solution.py:435
  23.1 8.5 %collective-permute-start.10 = (bf16[384,768]{1,0:T(8,128)(2,1)S(1)}, bf16[384,768]{1,0:T(8,128)(2,1)S(1)}, u32[]{:S(2)}, u32[]{:S(2)}) collective-permute-start(bf16[384,768]{1,0:T(8,128)(2,1)S(1)} %collective-permute-done.hx), channel_id=1, source_target_pairs={{0,1},{1,0},{2,3},{3,2},{4,5},{5,4},{6,7},{7,6},{8,9},{9,8},{10,11... | collective-permute-start | bytes 1769480 | tf_op jit(solution)/shard_map/ppermute | solution.py:435
  23.1 8.5 %collective-permute-start.11 = (bf16[384,768]{1,0:T(8,128)(2,1)S(1)}, bf16[384,768]{1,0:T(8,128)(2,1)}, u32[]{:S(2)}, u32[]{:S(2)}) collective-permute-start(bf16[384,768]{1,0:T(8,128)(2,1)S(1)} %collective-permute-done.1.hy), channel_id=1, source_target_pairs={{0,1},{1,0},{2,3},{3,2},{4,5},{5,4},{6,7},{7,6},{8,9},{9,8},{10,11... | collective-permute-start | bytes 1769480 | tf_op jit(solution)/shard_map/ppermute | solution.py:435
  29.2 2.4 %collective-permute-start.12 = (bf16[208,768]{1,0:T(8,128)(2,1)}, bf16[208,768]{1,0:T(8,128)(2,1)}, u32[]{:S(2)}, u32[]{:S(2)}) collective-permute-start(bf16[208,768]{1,0:T(8,128)(2,1)} %collective-permute-done.8.da), channel_id=1, source_target_pairs={{0,1},{1,0},{2,3},{3,2},{4,5},{5,4},{6,7},{7,6},{8,9},{9,8},{10,11... | collective-permute-start | bytes 958472 | tf_op jit(solution)/shard_map/ppermute | solution.py:435
  40.0 16.2 %collective-permute-start.16 = (bf16[160,768]{1,0:T(8,128)(2,1)S(1)}, bf16[160,768]{1,0:T(8,128)(2,1)S(1)}, u32[]{:S(2)}, u32[]{:S(2)}) collective-permute-start(bf16[160,768]{1,0:T(8,128)(2,1)S(1)} %pad_maximum_fusion.2.refs_0_.g0), channel_id=1, source_target_pairs={{0,24},{8,16},{16,8},{24,0},{1,25},{9,17},{17,9},{25,1},{2,26},{10... | collective-permute-start | bytes 737288 | tf_op jit(solution)/shard_map/ppermute | solution.py:435
  42.7 6.1 %collective-permute-start.20 = (bf16[40,768]{1,0:T(8,128)(2,1)S(1)}, bf16[40,768]{1,0:T(8,128)(2,1)S(1)}, u32[]{:S(2)}, u32[]{:S(2)}) collective-permute-start(bf16[40,768]{1,0:T(8,128)(2,1)S(1)} %get-tuple-element.195), channel_id=1, source_target_pairs={{0,6},{1,7},{2,4},{3,5},{4,2},{5,3},{6,0},{7,1},{8,14},{9,15},{10,... | collective-permute-start | bytes 184328 | tf_op jit(solution)/shard_map/ppermute | solution.py:435
  46.3 10.9 %collective-permute-start.15 = (bf16[160,768]{1,0:T(8,128)(2,1)S(1)}, bf16[160,768]{1,0:T(8,128)(2,1)S(1)}, u32[]{:S(2)}, u32[]{:S(2)}) collective-permute-start(bf16[160,768]{1,0:T(8,128)(2,1)S(1)} %pad_maximum_fusion.2.refs_0_.g0), channel_id=1, source_target_pairs={{0,16},{8,24},{16,0},{24,8},{1,17},{9,25},{17,1},{25,9},{2,18},{10... | collective-permute-start | bytes 737288 | tf_op jit(solution)/shard_map/ppermute | solution.py:435
  47.5 10.1 %collective-permute-start.14 = (bf16[160,768]{1,0:T(8,128)(2,1)S(1)}, bf16[160,768]{1,0:T(8,128)(2,1)S(1)}, u32[]{:S(2)}, u32[]{:S(2)}) collective-permute-start(bf16[160,768]{1,0:T(8,128)(2,1)S(1)} %pad_maximum_fusion.2.refs_0_.g0), channel_id=1, source_target_pairs={{0,8},{8,0},{16,24},{24,16},{1,9},{9,1},{17,25},{25,17},{2,10},{10... | collective-permute-start | bytes 737288 | tf_op jit(solution)/shard_map/ppermute | solution.py:435
  48.2 5.2 %collective-permute-start.19 = (bf16[40,768]{1,0:T(8,128)(2,1)S(1)}, bf16[40,768]{1,0:T(8,128)(2,1)S(1)}, u32[]{:S(2)}, u32[]{:S(2)}) collective-permute-start(bf16[40,768]{1,0:T(8,128)(2,1)S(1)} %get-tuple-element.196), channel_id=1, source_target_pairs={{0,4},{1,5},{2,6},{3,7},{4,0},{5,1},{6,2},{7,3},{8,12},{9,13},{10,... | collective-permute-start | bytes 184328 | tf_op jit(solution)/shard_map/ppermute | solution.py:435
  48.8 4.9 %collective-permute-start.18 = (bf16[40,768]{1,0:T(8,128)(2,1)S(1)}, bf16[40,768]{1,0:T(8,128)(2,1)S(1)}, u32[]{:S(2)}, u32[]{:S(2)}) collective-permute-start(bf16[40,768]{1,0:T(8,128)(2,1)S(1)} %get-tuple-element.197), channel_id=1, source_target_pairs={{0,2},{1,3},{2,0},{3,1},{4,6},{5,7},{6,4},{7,5},{8,10},{9,11},{10,... | collective-permute-start | bytes 184328 | tf_op jit(solution)/shard_map/ppermute | solution.py:435
  53.7 14.2 %collective-permute-start.23 = (bf16[160,768]{1,0:T(8,128)(2,1)S(1)}, bf16[160,768]{1,0:T(8,128)(2,1)S(1)}, u32[]{:S(2)}, u32[]{:S(2)}) collective-permute-start(bf16[160,768]{1,0:T(8,128)(2,1)S(1)} %pad_maximum_fusion.3.x0), channel_id=1, source_target_pairs={{0,24},{8,16},{16,8},{24,0},{1,25},{9,17},{17,9},{25,1},{2,26},{10... | collective-permute-start | bytes 737288 | tf_op jit(solution)/shard_map/ppermute | solution.py:435
  55.1 12.8 %collective-permute-start.22 = (bf16[160,768]{1,0:T(8,128)(2,1)S(1)}, bf16[160,768]{1,0:T(8,128)(2,1)S(1)}, u32[]{:S(2)}, u32[]{:S(2)}) collective-permute-start(bf16[160,768]{1,0:T(8,128)(2,1)S(1)} %pad_maximum_fusion.3.x0), channel_id=1, source_target_pairs={{0,16},{8,24},{16,0},{24,8},{1,17},{9,25},{17,1},{25,9},{2,18},{10... | collective-permute-start | bytes 737288 | tf_op jit(solution)/shard_map/ppermute | solution.py:435
  56.2 11.6 %collective-permute-start.21 = (bf16[160,768]{1,0:T(8,128)(2,1)S(1)}, bf16[160,768]{1,0:T(8,128)(2,1)S(1)}, u32[]{:S(2)}, u32[]{:S(2)}) collective-permute-start(bf16[160,768]{1,0:T(8,128)(2,1)S(1)} %pad_maximum_fusion.3.x0), channel_id=1, source_target_pairs={{0,8},{8,0},{16,24},{24,16},{1,9},{9,1},{17,25},{25,17},{2,10},{10... | collective-permute-start | bytes 737288 | tf_op jit(solution)/shard_map/ppermute | solution.py:435
  57.3 7.3 %collective-permute-start.24 = (bf16[128,768]{1,0:T(8,128)(2,1)S(1)}, bf16[128,768]{1,0:T(8,128)(2,1)S(1)}, u32[]{:S(2)}, u32[]{:S(2)}) collective-permute-start(bf16[128,768]{1,0:T(8,128)(2,1)S(1)} %get-tuple-element.121), channel_id=1, source_target_pairs={{0,2},{1,3},{2,0},{3,1},{4,6},{5,7},{6,4},{7,5},{8,10},{9,11},{10,... | collective-permute-start | bytes 589832 | tf_op jit(solution)/shard_map/ppermute | solution.py:435
  57.6 10.3 %collective-permute-start.25 = (bf16[128,768]{1,0:T(8,128)(2,1)S(1)}, bf16[128,768]{1,0:T(8,128)(2,1)S(1)}, u32[]{:S(2)}, u32[]{:S(2)}) collective-permute-start(bf16[128,768]{1,0:T(8,128)(2,1)S(1)} %get-tuple-element.123), channel_id=1, source_target_pairs={{0,4},{1,5},{2,6},{3,7},{4,0},{5,1},{6,2},{7,3},{8,12},{9,13},{10,... | collective-permute-start | bytes 589832 | tf_op jit(solution)/shard_map/ppermute | solution.py:435
  72.6 9.1 %collective-permute-start.26 = (bf16[160,896]{1,0:T(8,128)(2,1)S(1)}, bf16[160,896]{1,0:T(8,128)(2,1)S(1)}, u32[]{:S(2)}, u32[]{:S(2)}) collective-permute-start(bf16[160,896]{1,0:T(8,128)(2,1)S(1)} %get-tuple-element.131), channel_id=1, source_target_pairs={{0,8},{8,0},{16,24},{24,16},{1,9},{9,1},{17,25},{25,17},{2,10},{10... | collective-permute-start | bytes 860168 | tf_op jit(solution)/shard_map/ppermute | solution.py:435
  74.3 11.7 %collective-permute-start.27 = (bf16[160,896]{1,0:T(8,128)(2,1)S(1)}, bf16[160,896]{1,0:T(8,128)(2,1)S(1)}, u32[]{:S(2)}, u32[]{:S(2)}) collective-permute-start(bf16[160,896]{1,0:T(8,128)(2,1)S(1)} %get-tuple-element.132), channel_id=1, source_target_pairs={{0,16},{8,24},{16,0},{24,8},{1,17},{9,25},{17,1},{25,9},{2,18},{10... | collective-permute-start | bytes 860168 | tf_op jit(solution)/shard_map/ppermute | solution.py:435
  75.2 10.9 %collective-permute-start.28 = (bf16[160,896]{1,0:T(8,128)(2,1)S(1)}, bf16[160,896]{1,0:T(8,128)(2,1)S(1)}, u32[]{:S(2)}, u32[]{:S(2)}) collective-permute-start(bf16[160,896]{1,0:T(8,128)(2,1)S(1)} %get-tuple-element.133), channel_id=1, source_target_pairs={{0,24},{8,16},{16,8},{24,0},{1,25},{9,17},{17,9},{25,1},{2,26},{10... | collective-permute-start | bytes 860168 | tf_op jit(solution)/shard_map/ppermute | solution.py:435
  76.1 15.1 %collective-permute-start.29 = (bf16[128,768]{1,0:T(8,128)(2,1)S(1)}, bf16[128,768]{1,0:T(8,128)(2,1)S(1)}, u32[]{:S(2)}, u32[]{:S(2)}) collective-permute-start(bf16[128,768]{1,0:T(8,128)(2,1)S(1)} %get-tuple-element.137), channel_id=1, source_target_pairs={{0,6},{1,7},{2,4},{3,5},{4,2},{5,3},{6,0},{7,1},{8,14},{9,15},{10,... | collective-permute-start | bytes 589832 | tf_op jit(solution)/shard_map/ppermute | solution.py:435
  86.8 6.7 %collective-permute-start.32 = (bf16[40,896]{1,0:T(8,128)(2,1)S(1)}, bf16[40,896]{1,0:T(8,128)(2,1)S(1)}, u32[]{:S(2)}, u32[]{:S(2)}) collective-permute-start(bf16[40,896]{1,0:T(8,128)(2,1)S(1)} %get-tuple-element.187), channel_id=1, source_target_pairs={{0,6},{1,7},{2,4},{3,5},{4,2},{5,3},{6,0},{7,1},{8,14},{9,15},{10,... | collective-permute-start | bytes 215048 | tf_op jit(solution)/shard_map/ppermute | solution.py:435
  90.1 5.2 %collective-permute-start.31 = (bf16[40,896]{1,0:T(8,128)(2,1)S(1)}, bf16[40,896]{1,0:T(8,128)(2,1)S(1)}, u32[]{:S(2)}, u32[]{:S(2)}) collective-permute-start(bf16[40,896]{1,0:T(8,128)(2,1)S(1)} %get-tuple-element.188), channel_id=1, source_target_pairs={{0,4},{1,5},{2,6},{3,7},{4,0},{5,1},{6,2},{7,3},{8,12},{9,13},{10,... | collective-permute-start | bytes 215048 | tf_op jit(solution)/shard_map/ppermute | solution.py:435
  90.1 5.2 %collective-permute-start.30 = (bf16[40,896]{1,0:T(8,128)(2,1)S(1)}, bf16[40,896]{1,0:T(8,128)(2,1)S(1)}, u32[]{:S(2)}, u32[]{:S(2)}) collective-permute-start(bf16[40,896]{1,0:T(8,128)(2,1)S(1)} %get-tuple-element.189), channel_id=1, source_target_pairs={{0,2},{1,3},{2,0},{3,1},{4,6},{5,7},{6,4},{7,5},{8,10},{9,11},{10,... | collective-permute-start | bytes 215048 | tf_op jit(solution)/shard_map/ppermute | solution.py:435
  96.3 5.1 %collective-permute-start.33 = (bf16[128,896]{1,0:T(8,128)(2,1)S(1)}, bf16[128,896]{1,0:T(8,128)(2,1)S(1)}, u32[]{:S(2)}, u32[]{:S(2)}) collective-permute-start(bf16[128,896]{1,0:T(8,128)(2,1)S(1)} %get-tuple-element.140), channel_id=1, source_target_pairs={{0,1},{1,0},{2,3},{3,2},{4,5},{5,4},{6,7},{7,6},{8,9},{9,8},{10,11... | collective-permute-start | bytes 688136 | tf_op jit(solution)/shard_map/ppermute | solution.py:435
  97.8 11.4 %collective-permute-start.34 = (bf16[160,768]{1,0:T(8,128)(2,1)S(1)}, bf16[160,768]{1,0:T(8,128)(2,1)S(1)}, u32[]{:S(2)}, u32[]{:S(2)}) collective-permute-start(bf16[160,768]{1,0:T(8,128)(2,1)S(1)} %get-tuple-element.149), channel_id=1, source_target_pairs={{0,8},{8,0},{16,24},{24,16},{1,9},{9,1},{17,25},{25,17},{2,10},{10... | collective-permute-start | bytes 737288 | tf_op jit(solution)/shard_map/ppermute | solution.py:435
  98.6 13.3 %collective-permute-start.35 = (bf16[160,768]{1,0:T(8,128)(2,1)S(1)}, bf16[160,768]{1,0:T(8,128)(2,1)S(1)}, u32[]{:S(2)}, u32[]{:S(2)}) collective-permute-start(bf16[160,768]{1,0:T(8,128)(2,1)S(1)} %get-tuple-element.150), channel_id=1, source_target_pairs={{0,16},{8,24},{16,0},{24,8},{1,17},{9,25},{17,1},{25,9},{2,18},{10... | collective-permute-start | bytes 737288 | tf_op jit(solution)/shard_map/ppermute | solution.py:435
  99.8 12.2 %collective-permute-start.36 = (bf16[160,768]{1,0:T(8,128)(2,1)S(1)}, bf16[160,768]{1,0:T(8,128)(2,1)S(1)}, u32[]{:S(2)}, u32[]{:S(2)}) collective-permute-start(bf16[160,768]{1,0:T(8,128)(2,1)S(1)} %get-tuple-element.151), channel_id=1, source_target_pairs={{0,24},{8,16},{16,8},{24,0},{1,25},{9,17},{17,9},{25,1},{2,26},{10... | collective-permute-start | bytes 737288 | tf_op jit(solution)/shard_map/ppermute | solution.py:435
  106.6 10.1 %collective-permute-start.37 = (bf16[128,768]{1,0:T(8,128)(2,1)S(1)}, bf16[128,768]{1,0:T(8,128)(2,1)S(1)}, u32[]{:S(2)}, u32[]{:S(2)}) collective-permute-start(bf16[128,768]{1,0:T(8,128)(2,1)S(1)} %get-tuple-element.152), channel_id=1, source_target_pairs={{0,2},{1,3},{2,0},{3,1},{4,6},{5,7},{6,4},{7,5},{8,10},{9,11},{10,... | collective-permute-start | bytes 589832 | tf_op jit(solution)/shard_map/ppermute | solution.py:435
  107.3 17.2 %collective-permute-start.38 = (bf16[128,768]{1,0:T(8,128)(2,1)S(1)}, bf16[128,768]{1,0:T(8,128)(2,1)S(1)}, u32[]{:S(2)}, u32[]{:S(2)}) collective-permute-start(bf16[128,768]{1,0:T(8,128)(2,1)S(1)} %get-tuple-element.161), channel_id=1, source_target_pairs={{0,4},{1,5},{2,6},{3,7},{4,0},{5,1},{6,2},{7,3},{8,12},{9,13},{10,... | collective-permute-start | bytes 589832 | tf_op jit(solution)/shard_map/ppermute | solution.py:435
  109.3 15.2 %collective-permute-start.39 = (bf16[128,768]{1,0:T(8,128)(2,1)S(1)}, bf16[128,768]{1,0:T(8,128)(2,1)S(1)}, u32[]{:S(2)}, u32[]{:S(2)}) collective-permute-start(bf16[128,768]{1,0:T(8,128)(2,1)S(1)} %get-tuple-element.162), channel_id=1, source_target_pairs={{0,6},{1,7},{2,4},{3,5},{4,2},{5,3},{6,0},{7,1},{8,14},{9,15},{10,... | collective-permute-start | bytes 589832 | tf_op jit(solution)/shard_map/ppermute | solution.py:435
  129.7 6.2 %collective-permute-start.41 = (bf16[208,384]{1,0:T(8,128)(2,1)S(1)}, bf16[208,384]{1,0:T(8,128)(2,1)S(1)}, u32[]{:S(2)}, u32[]{:S(2)}) collective-permute-start(bf16[208,384]{1,0:T(8,128)(2,1)S(1)} %get-tuple-element.166), channel_id=1, source_target_pairs={{0,16},{8,24},{16,0},{24,8},{1,17},{9,25},{17,1},{25,9},{2,18},{10... | collective-permute-start | bytes 479240 | tf_op jit(solution)/shard_map/ppermute | solution.py:435
  130.8 10.3 %collective-permute-start.46 = (bf16[208,384]{1,0:T(8,128)(2,1)S(1)}, bf16[208,384]{1,0:T(8,128)(2,1)S(1)}, u32[]{:S(2)}, u32[]{:S(2)}) collective-permute-start(bf16[208,384]{1,0:T(8,128)(2,1)S(1)} %get-tuple-element.172), channel_id=1, source_target_pairs={{0,8},{8,0},{16,24},{24,16},{1,9},{9,1},{17,25},{25,17},{2,10},{10... | collective-permute-start | bytes 479240 | tf_op jit(solution)/shard_map/ppermute | solution.py:435
  131.9 9.3 %collective-permute-start.47 = (bf16[208,384]{1,0:T(8,128)(2,1)S(1)}, bf16[208,384]{1,0:T(8,128)(2,1)S(1)}, u32[]{:S(2)}, u32[]{:S(2)}) collective-permute-start(bf16[208,384]{1,0:T(8,128)(2,1)S(1)} %get-tuple-element.173), channel_id=1, source_target_pairs={{0,24},{8,16},{16,8},{24,0},{1,25},{9,17},{17,9},{25,1},{2,26},{10... | collective-permute-start | bytes 479240 | tf_op jit(solution)/shard_map/ppermute | solution.py:435
  136.0 10.1 %collective-permute-start.44 = (bf16[40,768]{1,0:T(8,128)(2,1)S(1)}, bf16[40,768]{1,0:T(8,128)(2,1)S(1)}, u32[]{:S(2)}, u32[]{:S(2)}) collective-permute-start(bf16[40,768]{1,0:T(8,128)(2,1)S(1)} %get-tuple-element.191), channel_id=1, source_target_pairs={{0,6},{1,7},{2,4},{3,5},{4,2},{5,3},{6,0},{7,1},{8,14},{9,15},{10,... | collective-permute-start | bytes 184328 | tf_op jit(solution)/shard_map/ppermute | solution.py:435
  138.4 8.2 %collective-permute-start.43 = (bf16[40,768]{1,0:T(8,128)(2,1)S(1)}, bf16[40,768]{1,0:T(8,128)(2,1)S(1)}, u32[]{:S(2)}, u32[]{:S(2)}) collective-permute-start(bf16[40,768]{1,0:T(8,128)(2,1)S(1)} %get-tuple-element.192), channel_id=1, source_target_pairs={{0,4},{1,5},{2,6},{3,7},{4,0},{5,1},{6,2},{7,3},{8,12},{9,13},{10,... | collective-permute-start | bytes 184328 | tf_op jit(solution)/shard_map/ppermute | solution.py:435
  140.7 5.9 %collective-permute-start.42 = (bf16[40,768]{1,0:T(8,128)(2,1)S(1)}, bf16[40,768]{1,0:T(8,128)(2,1)S(1)}, u32[]{:S(2)}, u32[]{:S(2)}) collective-permute-start(bf16[40,768]{1,0:T(8,128)(2,1)S(1)} %get-tuple-element.193), channel_id=1, source_target_pairs={{0,2},{1,3},{2,0},{3,1},{4,6},{5,7},{6,4},{7,5},{8,10},{9,11},{10,... | collective-permute-start | bytes 184328 | tf_op jit(solution)/shard_map/ppermute | solution.py:435
  141.8 11.8 %collective-permute-start.50 = (bf16[208,384]{1,0:T(8,128)(2,1)S(1)}, bf16[208,384]{1,0:T(8,128)(2,1)S(1)}, u32[]{:S(2)}, u32[]{:S(2)}) collective-permute-start(bf16[208,384]{1,0:T(8,128)(2,1)S(1)} %sum_share.1.a0), channel_id=1, source_target_pairs={{0,6},{1,7},{2,4},{3,5},{4,2},{5,3},{6,0},{7,1},{8,14},{9,15},{10,... | collective-permute-start | bytes 479240 | tf_op jit(solution)/shard_map/ppermute | solution.py:435
  144.2 15.1 %collective-permute-start.49 = (bf16[208,384]{1,0:T(8,128)(2,1)S(1)}, bf16[208,384]{1,0:T(8,128)(2,1)S(1)}, u32[]{:S(2)}, u32[]{:S(2)}) collective-permute-start(bf16[208,384]{1,0:T(8,128)(2,1)S(1)} %sum_share.1.a0), channel_id=1, source_target_pairs={{0,4},{1,5},{2,6},{3,7},{4,0},{5,1},{6,2},{7,3},{8,12},{9,13},{10,... | collective-permute-start | bytes 479240 | tf_op jit(solution)/shard_map/ppermute | solution.py:435
  146.1 13.2 %collective-permute-start.48 = (bf16[208,384]{1,0:T(8,128)(2,1)S(1)}, bf16[208,384]{1,0:T(8,128)(2,1)S(1)}, u32[]{:S(2)}, u32[]{:S(2)}) collective-permute-start(bf16[208,384]{1,0:T(8,128)(2,1)S(1)} %sum_share.1.a0), channel_id=1, source_target_pairs={{0,2},{1,3},{2,0},{3,1},{4,6},{5,7},{6,4},{7,5},{8,10},{9,11},{10,... | collective-permute-start | bytes 479240 | tf_op jit(solution)/shard_map/ppermute | solution.py:435
  147.5 12.4 %collective-permute-start.45 = (bf16[128,768]{1,0:T(8,128)(2,1)S(1)}, bf16[128,768]{1,0:T(8,128)(2,1)S(1)}, u32[]{:S(2)}, u32[]{:S(2)}) collective-permute-start(bf16[128,768]{1,0:T(8,128)(2,1)S(1)} %get-tuple-element.169), channel_id=1, source_target_pairs={{0,1},{1,0},{2,3},{3,2},{4,5},{5,4},{6,7},{7,6},{8,9},{9,8},{10,11... | collective-permute-start | bytes 589832 | tf_op jit(solution)/shard_map/ppermute | solution.py:435
  153.1 7.5 %collective-permute-start.51 = (bf16[208,384]{1,0:T(8,128)(2,1)S(1)}, bf16[208,384]{1,0:T(8,128)(2,1)S(1)}, u32[]{:S(2)}, u32[]{:S(2)}) collective-permute-start(bf16[208,384]{1,0:T(8,128)(2,1)S(1)} %sum_share.1.a0), channel_id=1, source_target_pairs={{0,1},{1,0},{2,3},{3,2},{4,5},{5,4},{6,7},{7,6},{8,9},{9,8},{10,11... | collective-permute-start | bytes 479240 | tf_op jit(solution)/shard_map/ppermute | solution.py:435
  153.6 7.0 %collective-permute-start.54 = (bf16[208,384]{1,0:T(8,128)(2,1)S(1)}, bf16[208,384]{1,0:T(8,128)(2,1)S(1)}, u32[]{:S(2)}, u32[]{:S(2)}) collective-permute-start(bf16[208,384]{1,0:T(8,128)(2,1)S(1)} %collective-permute-done.50.a3), channel_id=1, source_target_pairs={{0,1},{1,0},{2,3},{3,2},{4,5},{5,4},{6,7},{7,6},{8,9},{9,8},{10,11... | collective-permute-start | bytes 479240 | tf_op jit(solution)/shard_map/ppermute | solution.py:435
  (25 other events, 167.0 us)
